TPU v7x, 32 devices: a whole 2x2x4 slice. The times are simulated.
32 devices in a mesh: trip: 8 (over z, y), row: 4 (over x, core).
Axes of the slice: x: 2, y: 2, z: 4, core: 2. Of those that a mesh axis runs over, the one named last changes fastest.
Arguments:
- eigvecs: bfloat16 [2048, 64, 128], P(('trip', 'row')), may hold values from -0.5 to 0.5
- cubic: bfloat16 [768, 64, 4096], P(('trip', 'row')), may hold values from -0.09375 to 0.09375
- triplets: int32 [768, 3], P(('trip', 'row')), may hold values from 0 to 2047, as said below
- weights: int32 [768], P(('trip', 'row')), may hold values from 1 to 6
- deviation: float32 [2048, 768], P(('trip', 'row')), may hold values from -6 to 6
- source: float32 [2048, 768], P(('trip', 'row')), may hold values from -6 to 6
- base_rate: float32 [2048, 64], P(('trip', 'row')), may hold values from 0.5 to 2
Outputs:
- relaxed: float32 [2048, 768], P(('trip', 'row'))
Inputs may be any that keep to these rules, and one draw needn't show every extreme that they name: Column 0 of a device's triplets names wavevectors homed on devices of its own trip group; at most 12 of them on any one device, and in every trip group one device is named exactly 12 times by each device of the group. Columns 1 and 2 of one device's triplets together name at most 2 wavevectors homed on any one device, and one device is named exactly 2 times by every device. Wavevectors may repeat.
All inputs are finite; a program needn't handle non-finite values.
Results may differ from a plain program's by a relative error of at most 0.0003.
Values may be sent and summed in bfloat16 or wider, within the bound.
No kernel may reach another device: no remote copies, remote signals or barrier semaphores. Data moves between devices by JAX's collectives and lax.ppermute only.
A program may use at most 128 MiB of HBM per device.

v0:
```python
import jax
import jax.numpy as jnp
from jax import lax
from jax.sharding import PartitionSpec as P

ITERS = 2


damping = 0.7


def for_sending(value):

    def short(part):
        return part.astype(jnp.bfloat16) if part.dtype == jnp.float32 else part

    return jax.tree.map(short, value)


def ranks_of(target):
    chain_length = target.shape[0]
    matches = target[:, None] == target[None, :]
    earlier = lax.broadcasted_iota(
        jnp.int32, (chain_length, chain_length), 1
    ) < lax.broadcasted_iota(jnp.int32, (chain_length, chain_length), 0)
    return jnp.sum((matches & earlier).astype(jnp.int32), axis=1)


def slot_onehot(places, extent):
    return lax.broadcasted_iota(jnp.int32, (extent, places.shape[0]), 0) == places[None, :]


def pack_ints(places, values, extent):
    return jnp.sum(jnp.where(slot_onehot(places, extent), values[None, :], 0), axis=1)


def pack_rows(places, values, extent):
    onehot = slot_onehot(places, extent).astype(values.dtype)
    packed = jnp.dot(
        onehot, values, preferred_element_type=jnp.float32, precision=lax.Precision.HIGHEST
    )
    return packed.astype(values.dtype)


def complex_block(vectors):
    branches = vectors.shape[1]
    real_half = vectors[:, :, :branches]
    imag_half = vectors[:, :, branches:]
    upper = jnp.concatenate([real_half, imag_half], -1)
    lower = jnp.concatenate([-imag_half, real_half], -1)
    return jnp.stack([upper, lower], 2)


def contract_batch(tensor, vec_one, vec_two, vec_three, weight):
    batch = tensor.shape[0]
    branches = vec_one.shape[1]
    flat = tensor.reshape(batch, branches * branches, branches)
    section_one = jnp.einsum(
        "tmk,tky->tmy", flat, vec_three, preferred_element_type=jnp.float32
    ).astype(jnp.bfloat16)
    section_one = section_one.reshape(batch, branches, branches, 2, branches)
    mixer_two = complex_block(vec_two)
    mixed = jnp.einsum(
        "tijpc,tjpw->ticw", section_one, mixer_two, preferred_element_type=jnp.float32
    ).astype(jnp.bfloat16)
    mixed = mixed.reshape(batch, branches, branches, 2, branches)
    mixer_one = complex_block(vec_one)
    section_three = jnp.einsum(
        "tiqz,ticqb->tzcb", mixer_one, mixed, preferred_element_type=jnp.float32
    )
    vreal = section_three[:, :branches]
    vimag = section_three[:, branches:]
    power = (vreal * vreal + vimag * vimag) * weight.astype(jnp.float32)[:, None, None, None]
    return (jnp.sum(power, 2).astype(jnp.bfloat16), jnp.sum(power, 3).astype(jnp.bfloat16))


def look_up(table_rows, queries):
    looked_values = jnp.take(table_rows, queries.reshape(-1), axis=0)
    return looked_values.reshape(queries.shape + table_rows.shape[1:])


def fetch_state(phonon_state, queries):
    return lax.all_to_all(
        look_up(phonon_state, queries).astype(jnp.bfloat16),
        ("trip", "row"),
        split_axis=0,
        concat_axis=0,
        tiled=True,
    ).astype(jnp.float32)


def body(eigvecs, cubic, triplets, weights, deviation, source, base_rate):
    trip_count = lax.axis_size("trip")
    row_count = lax.axis_size("row")
    devices = trip_count * row_count
    home_rows = eigvecs.shape[0]
    branches = eigvecs.shape[1]
    trip_local = cubic.shape[0]
    columns = deviation.shape[1] // branches
    far_cap = (2 * trip_local + devices - 1) // devices
    row_cap = trip_local // 2
    row_slots = row_count * row_cap
    home_dev = triplets[:, 0] // home_rows
    row_target = home_dev % row_count
    row_place = row_target * row_cap + ranks_of(row_target)
    row_local = triplets[:, 0] - home_dev * home_rows
    row_queries = pack_ints(row_place, row_local, row_slots).reshape(row_count, row_cap)
    row_found = lax.all_to_all(
        look_up(
            eigvecs, lax.all_to_all(row_queries, "row", split_axis=0, concat_axis=0, tiled=True)
        ),
        "row",
        split_axis=0,
        concat_axis=0,
        tiled=True,
    )
    first_vecs = jnp.take(row_found.reshape((row_slots,) + eigvecs.shape[1:]), row_place, axis=0)
    far_index = triplets[:, 1:].reshape(-1)
    far_owner = far_index // home_rows
    far_place = far_owner * far_cap + ranks_of(far_owner)
    far_queries = pack_ints(
        far_place, far_index - far_owner * home_rows, devices * far_cap
    ).reshape(devices, far_cap)
    queries_here = lax.all_to_all(
        far_queries, ("trip", "row"), split_axis=0, concat_axis=0, tiled=True
    )
    far_found = lax.all_to_all(
        look_up(eigvecs, queries_here), ("trip", "row"), split_axis=0, concat_axis=0, tiled=True
    )
    far_table = far_found.reshape((devices * far_cap,) + eigvecs.shape[1:])
    place_pairs = far_place.reshape(trip_local, 2)
    second_vecs = jnp.take(far_table, place_pairs[:, 0], axis=0)
    third_vecs = jnp.take(far_table, place_pairs[:, 1], axis=0)
    count_per_round = 4
    turns = trip_local // count_per_round

    def one_turn(bundle):
        return contract_batch(*bundle)

    first_pairing, second_pairing = lax.map(
        one_turn,
        (
            cubic.reshape(turns, count_per_round, branches, branches * branches),
            first_vecs.reshape(turns, count_per_round, branches, 2 * branches),
            second_vecs.reshape(turns, count_per_round, branches, 2 * branches),
            third_vecs.reshape(turns, count_per_round, branches, 2 * branches),
            weights.reshape(turns, count_per_round),
        ),
    )
    first_pairing = first_pairing.reshape(trip_local, branches, branches)
    second_pairing = second_pairing.reshape(trip_local, branches, branches)
    row_code = pack_ints(row_place, row_local + 1, row_slots).reshape(row_count, row_cap)
    phonon_state = deviation.reshape(home_rows, branches, columns)
    driven = source.reshape(home_rows, branches, columns)
    highest = lax.Precision.HIGHEST
    rate_terms = jnp.sum(first_pairing.astype(jnp.float32), 2) + jnp.sum(
        second_pairing.astype(jnp.float32), 2
    )
    outgoing = pack_rows(row_place, rate_terms, row_slots).reshape(row_count, row_cap, branches)
    arrived_rates, arrived_codes = (
        lax.all_to_all(outgoing, "row", split_axis=0, concat_axis=0, tiled=True),
        lax.all_to_all(row_code, "row", split_axis=0, concat_axis=0, tiled=True),
    )
    onehot = (
        lax.broadcasted_iota(jnp.int32, (home_rows, row_slots), 0)
        == arrived_codes.reshape(-1)[None, :] - 1
    ).astype(jnp.float32)
    total_rate = base_rate + jnp.dot(
        onehot,
        arrived_rates.reshape(row_slots, branches),
        preferred_element_type=jnp.float32,
        precision=highest,
    )
    for update in range(ITERS):
        far_phonon_state = phonon_state.reshape(home_rows, branches * columns)
        arrived_state = fetch_state(
            far_phonon_state,
            lax.all_to_all(far_queries, ("trip", "row"), split_axis=0, concat_axis=0, tiled=True),
        )
        picked = jnp.take(
            arrived_state.reshape(devices * far_cap, far_phonon_state.shape[1]), far_place, axis=0
        )
        remote = picked.reshape(trip_local, 2, branches, columns)
        terms = jnp.einsum(
            "hzy,hye->hze", first_pairing.astype(jnp.float32), remote[:, 0], precision=highest
        )
        terms = terms + jnp.einsum(
            "hzy,hye->hze", second_pairing.astype(jnp.float32), remote[:, 1], precision=highest
        )
        packed = pack_rows(row_place, terms.reshape(trip_local, branches * columns), row_slots)
        arrived_terms = lax.all_to_all(
            for_sending(packed.reshape(row_count, row_cap, branches * columns)),
            "row",
            split_axis=0,
            concat_axis=0,
            tiled=True,
        )
        coupled = jnp.dot(
            onehot,
            arrived_terms.reshape(row_slots, branches * columns),
            preferred_element_type=jnp.float32,
            precision=highest,
        )
        phonon_state = (1.0 - damping) * phonon_state + damping * (
            driven + coupled.reshape(home_rows, branches, columns)
        ) / total_rate[:, :, None]
    return phonon_state.reshape(home_rows, branches * columns)


def solution(mesh):
    in_specs = (
        P(("trip", "row"), None, None),
        P(("trip", "row"), None, None),
        P(("trip", "row"), None),
        P(("trip", "row")),
        P(("trip", "row"), None),
        P(("trip", "row"), None),
        P(("trip", "row"), None),
    )
    out_specs = P(("trip", "row"), None)
    return jax.shard_map(body, mesh=mesh, in_specs=in_specs, out_specs=out_specs, check_vma=False)
```

profile of v0, /device:TPU:0, one launch (start us, length us, event | category | flops | bytes accessed | tf_op | source)
XLA Modules:
  0.0 479.1 jit_solution(7397142703072189855)
XLA Ops:
  3.7 4.2 all-to-all-start.1
  16.9 6.8 %all-to-all-start.3 = ((s32[32,1,2]{2,1,0:T(1,128)}), s32[32,1,2]{2,1,0:T(1,128)S(1)}, u32[]{:S(2)}, u32[]{:S(2)}) async-start(s32[32,1,2]{2,1,0:T(1,128)} %bitcast.33), calls=%async_computation.3 | async-start | bytes 32768 | tf_op jit(solution)/shard_map/all_to_all | solution.py:124
  26.8 4.0 all-to-all-done.3
  40.3 7.8 %all-to-all-done.5 = bf16[32,2,768]{2,1,0:T(2,128)(2,1)S(1)} async-done(((bf16[32,2,768]{2,1,0:T(2,128)(2,1)}), bf16[32,2,768]{2,1,0:T(2,128)(2,1)S(1)}, u32[]{:S(2)}, u32[]{:S(2)}) %all-to-all-start.5) | async-done | bytes 98336 | tf_op jit(solution)/shard_map/all_to_all | solution.py:83
  48.1 3.5 all-to-all-start.2
  53.8 9.5 %all-to-all-done.2 = bf16[4,12,64,128]{3,2,1,0:T(8,128)(2,1)S(1)} async-done(((bf16[4,12,64,128]{3,2,1,0:T(8,128)(2,1)}), bf16[4,12,64,128]{3,2,1,0:T(8,128)(2,1)S(1)}, u32[]{:S(2)}, u32[]{:S(2)}) %all-to-all-start.2) | async-done | bytes 786464 | tf_op jit(solution)/shard_map/all_to_all | solution.py:108
  71.5 20.7 %all-to-all-done.4 = bf16[32,2,64,128]{3,2,1,0:T(8,128)(2,1)S(1)} async-done(((bf16[32,2,64,128]{3,2,1,0:T(8,128)(2,1)}), bf16[32,2,64,128]{3,2,1,0:T(8,128)(2,1)S(1)}, u32[]{:S(2)}, u32[]{:S(2)}) %all-to-all-start.4) | async-done | bytes 1048608 | tf_op jit(solution)/shard_map/all_to_all | solution.py:127
  94.4 335.0 %while.12 = (s32[]{:T(128)}, bf16[6,4,64,64]{2,3,1,0:T(8,128)(2,1)S(1)}, bf16[6,4,64,64]{2,3,1,0:T(8,128)(2,1)}, bf16[6,4,64,128]{3,2,1,0:T(8,128)(2,1)}, bf16[6...) while((s32[]{:T(128)}, ...), condition=%wide.region_8.10_spmd, body=%wide.region_5.9_spmd.sunk | while | flops 1353252864 | bytes 64488604 | solution.py:140
  96.5 5.5 %reshape.644 = bf16[4,4096,64]{2,1,0:T(8,128)(2,1)} reshape(bf16[1,4,64,4096]{3,2,1,0:T(8,128)(2,1)S(1)} %constant_dynamic-slice_fusion.3) | data formatting | bytes 4194304 | tf_op jit(solution)/shard_map/while/body/eval_jaxpr/reshape | solution.py:57
  102.1 5.4 %convolution_convert_fusion.4 = bf16[4,4096,128]{2,1,0:T(8,128)(2,1)} fusion(bf16[4,4096,64]{2,1,0:T(8,128)(2,1)} %reshape.644, bf16[6,4,64,128]{3,2,1,0:T(8,128)(2,1)} %get-tuple-element.196, s32[]{:T(128)} %get-tuple-element.182), kind=kOutput, calls=%fused_computation.16.clone.1 | convolution fusion | flops 270532608 | bytes 8454656 | tf_op jit(solution)/shard_map/while/body/eval_jaxpr/tmk,tky->tmy/dot_general | solution.py:58
  107.5 14.7 %reshape.645 = bf16[4,64,64,2,64]{4,3,2,1,0:T(2,128)(2,1)} reshape(bf16[4,4096,128]{2,1,0:T(8,128)(2,1)} %convolution_convert_fusion.4) | data formatting | bytes 8388608 | tf_op jit(solution)/shard_map/while/body/eval_jaxpr/reshape | solution.py:61
  122.2 7.7 %bitcast_convert_fusion.2 = bf16[4,64,64,128]{3,2,1,0:T(8,128)(2,1)} fusion(bf16[4,64,64,2,64]{4,3,2,1,0:T(2,128)(2,1)} %reshape.645, bf16[4,64,1,128]{3,1,2,0:T(8,128)(2,1)S(1)} %maximum_bitcast_fusion.12, bf16[4,64,1,128]{3,1,2,0:T(8,128)(2,1)S(1)} %get-tuple-element.164), kind=kOutput, calls=%fused_computation.13.clone.1 | convolution fusion | flops 539033600 | bytes 8519680 | tf_op jit(solution)/shard_map/while/body/eval_jaxpr/tijpc,tjpw->ticw/dot_general | solution.py:63
  129.9 9.4 %copy.128 = bf16[4,64,64,128]{1,3,2,0:T(8,128)(2,1)} copy(bf16[4,64,64,128]{3,2,1,0:T(8,128)(2,1)} %bitcast_convert_fusion.2) | data formatting | bytes 8388608 | tf_op jit(solution)/shard_map/while/body/eval_jaxpr/reshape | solution.py:66
  140.3 5.3 %convolution_bitcast_fusion.2 = f32[4,128,64,64]{1,3,2,0:T(8,128)S(1)} fusion(bf16[4,64,64,2,64]{1,4,3,2,0:T(8,128)(2,1)} %bitcast.152, bf16[4,64,1,128]{3,1,2,0:T(8,128)(2,1)S(1)} %maximum_bitcast_fusion.13, bf16[4,64,1,128]{3,1,2,0:T(8,128)(2,1)S(1)} %get-tuple-element.168), kind=kOutput, calls=%fused_computation.17.clone.1 | convolution fusion | flops 537133056 | bytes 12713984 | tf_op jit(solution)/shard_map/while/body/eval_jaxpr/tiqz,ticqb->tzcb/dot_general | solution.py:68
  152.4 5.5 %reshape.644 = bf16[4,4096,64]{2,1,0:T(8,128)(2,1)} reshape(bf16[1,4,64,4096]{3,2,1,0:T(8,128)(2,1)S(1)} %constant_dynamic-slice_fusion.3) | data formatting | bytes 4194304 | tf_op jit(solution)/shard_map/while/body/eval_jaxpr/reshape | solution.py:57
  157.9 5.4 %convolution_convert_fusion.4 = bf16[4,4096,128]{2,1,0:T(8,128)(2,1)} fusion(bf16[4,4096,64]{2,1,0:T(8,128)(2,1)} %reshape.644, bf16[6,4,64,128]{3,2,1,0:T(8,128)(2,1)} %get-tuple-element.196, s32[]{:T(128)} %get-tuple-element.182), kind=kOutput, calls=%fused_computation.16.clone.1 | convolution fusion | flops 270532608 | bytes 8454656 | tf_op jit(solution)/shard_map/while/body/eval_jaxpr/tmk,tky->tmy/dot_general | solution.py:58
  163.3 14.7 %reshape.645 = bf16[4,64,64,2,64]{4,3,2,1,0:T(2,128)(2,1)} reshape(bf16[4,4096,128]{2,1,0:T(8,128)(2,1)} %convolution_convert_fusion.4) | data formatting | bytes 8388608 | tf_op jit(solution)/shard_map/while/body/eval_jaxpr/reshape | solution.py:61
  178.0 7.7 %bitcast_convert_fusion.2 = bf16[4,64,64,128]{3,2,1,0:T(8,128)(2,1)} fusion(bf16[4,64,64,2,64]{4,3,2,1,0:T(2,128)(2,1)} %reshape.645, bf16[4,64,1,128]{3,1,2,0:T(8,128)(2,1)S(1)} %maximum_bitcast_fusion.12, bf16[4,64,1,128]{3,1,2,0:T(8,128)(2,1)S(1)} %get-tuple-element.164), kind=kOutput, calls=%fused_computation.13.clone.1 | convolution fusion | flops 539033600 | bytes 8519680 | tf_op jit(solution)/shard_map/while/body/eval_jaxpr/tijpc,tjpw->ticw/dot_general | solution.py:63
  185.7 9.4 %copy.128 = bf16[4,64,64,128]{1,3,2,0:T(8,128)(2,1)} copy(bf16[4,64,64,128]{3,2,1,0:T(8,128)(2,1)} %bitcast_convert_fusion.2) | data formatting | bytes 8388608 | tf_op jit(solution)/shard_map/while/body/eval_jaxpr/reshape | solution.py:66
  196.1 5.3 %convolution_bitcast_fusion.2 = f32[4,128,64,64]{1,3,2,0:T(8,128)S(1)} fusion(bf16[4,64,64,2,64]{1,4,3,2,0:T(8,128)(2,1)} %bitcast.152, bf16[4,64,1,128]{3,1,2,0:T(8,128)(2,1)S(1)} %maximum_bitcast_fusion.13, bf16[4,64,1,128]{3,1,2,0:T(8,128)(2,1)S(1)} %get-tuple-element.168), kind=kOutput, calls=%fused_computation.17.clone.1 | convolution fusion | flops 537133056 | bytes 12713984 | tf_op jit(solution)/shard_map/while/body/eval_jaxpr/tiqz,ticqb->tzcb/dot_general | solution.py:68
  202.2 3.4 fusion.77
  208.2 5.5 %reshape.644 = bf16[4,4096,64]{2,1,0:T(8,128)(2,1)} reshape(bf16[1,4,64,4096]{3,2,1,0:T(8,128)(2,1)S(1)} %constant_dynamic-slice_fusion.3) | data formatting | bytes 4194304 | tf_op jit(solution)/shard_map/while/body/eval_jaxpr/reshape | solution.py:57
  213.7 5.4 %convolution_convert_fusion.4 = bf16[4,4096,128]{2,1,0:T(8,128)(2,1)} fusion(bf16[4,4096,64]{2,1,0:T(8,128)(2,1)} %reshape.644, bf16[6,4,64,128]{3,2,1,0:T(8,128)(2,1)} %get-tuple-element.196, s32[]{:T(128)} %get-tuple-element.182), kind=kOutput, calls=%fused_computation.16.clone.1 | convolution fusion | flops 270532608 | bytes 8454656 | tf_op jit(solution)/shard_map/while/body/eval_jaxpr/tmk,tky->tmy/dot_general | solution.py:58
  219.1 14.7 %reshape.645 = bf16[4,64,64,2,64]{4,3,2,1,0:T(2,128)(2,1)} reshape(bf16[4,4096,128]{2,1,0:T(8,128)(2,1)} %convolution_convert_fusion.4) | data formatting | bytes 8388608 | tf_op jit(solution)/shard_map/while/body/eval_jaxpr/reshape | solution.py:61
  233.8 7.7 %bitcast_convert_fusion.2 = bf16[4,64,64,128]{3,2,1,0:T(8,128)(2,1)} fusion(bf16[4,64,64,2,64]{4,3,2,1,0:T(2,128)(2,1)} %reshape.645, bf16[4,64,1,128]{3,1,2,0:T(8,128)(2,1)S(1)} %maximum_bitcast_fusion.12, bf16[4,64,1,128]{3,1,2,0:T(8,128)(2,1)S(1)} %get-tuple-element.164), kind=kOutput, calls=%fused_computation.13.clone.1 | convolution fusion | flops 539033600 | bytes 8519680 | tf_op jit(solution)/shard_map/while/body/eval_jaxpr/tijpc,tjpw->ticw/dot_general | solution.py:63
  241.5 9.4 %copy.128 = bf16[4,64,64,128]{1,3,2,0:T(8,128)(2,1)} copy(bf16[4,64,64,128]{3,2,1,0:T(8,128)(2,1)} %bitcast_convert_fusion.2) | data formatting | bytes 8388608 | tf_op jit(solution)/shard_map/while/body/eval_jaxpr/reshape | solution.py:66
  252.0 5.3 %convolution_bitcast_fusion.2 = f32[4,128,64,64]{1,3,2,0:T(8,128)S(1)} fusion(bf16[4,64,64,2,64]{1,4,3,2,0:T(8,128)(2,1)} %bitcast.152, bf16[4,64,1,128]{3,1,2,0:T(8,128)(2,1)S(1)} %maximum_bitcast_fusion.13, bf16[4,64,1,128]{3,1,2,0:T(8,128)(2,1)S(1)} %get-tuple-element.168), kind=kOutput, calls=%fused_computation.17.clone.1 | convolution fusion | flops 537133056 | bytes 12713984 | tf_op jit(solution)/shard_map/while/body/eval_jaxpr/tiqz,ticqb->tzcb/dot_general | solution.py:68
  264.0 5.5 %reshape.644 = bf16[4,4096,64]{2,1,0:T(8,128)(2,1)} reshape(bf16[1,4,64,4096]{3,2,1,0:T(8,128)(2,1)S(1)} %constant_dynamic-slice_fusion.3) | data formatting | bytes 4194304 | tf_op jit(solution)/shard_map/while/body/eval_jaxpr/reshape | solution.py:57
  269.5 5.4 %convolution_convert_fusion.4 = bf16[4,4096,128]{2,1,0:T(8,128)(2,1)} fusion(bf16[4,4096,64]{2,1,0:T(8,128)(2,1)} %reshape.644, bf16[6,4,64,128]{3,2,1,0:T(8,128)(2,1)} %get-tuple-element.196, s32[]{:T(128)} %get-tuple-element.182), kind=kOutput, calls=%fused_computation.16.clone.1 | convolution fusion | flops 270532608 | bytes 8454656 | tf_op jit(solution)/shard_map/while/body/eval_jaxpr/tmk,tky->tmy/dot_general | solution.py:58
  274.9 14.7 %reshape.645 = bf16[4,64,64,2,64]{4,3,2,1,0:T(2,128)(2,1)} reshape(bf16[4,4096,128]{2,1,0:T(8,128)(2,1)} %convolution_convert_fusion.4) | data formatting | bytes 8388608 | tf_op jit(solution)/shard_map/while/body/eval_jaxpr/reshape | solution.py:61
  289.6 7.7 %bitcast_convert_fusion.2 = bf16[4,64,64,128]{3,2,1,0:T(8,128)(2,1)} fusion(bf16[4,64,64,2,64]{4,3,2,1,0:T(2,128)(2,1)} %reshape.645, bf16[4,64,1,128]{3,1,2,0:T(8,128)(2,1)S(1)} %maximum_bitcast_fusion.12, bf16[4,64,1,128]{3,1,2,0:T(8,128)(2,1)S(1)} %get-tuple-element.164), kind=kOutput, calls=%fused_computation.13.clone.1 | convolution fusion | flops 539033600 | bytes 8519680 | tf_op jit(solution)/shard_map/while/body/eval_jaxpr/tijpc,tjpw->ticw/dot_general | solution.py:63
  297.3 9.4 %copy.128 = bf16[4,64,64,128]{1,3,2,0:T(8,128)(2,1)} copy(bf16[4,64,64,128]{3,2,1,0:T(8,128)(2,1)} %bitcast_convert_fusion.2) | data formatting | bytes 8388608 | tf_op jit(solution)/shard_map/while/body/eval_jaxpr/reshape | solution.py:66
  307.8 5.3 %convolution_bitcast_fusion.2 = f32[4,128,64,64]{1,3,2,0:T(8,128)S(1)} fusion(bf16[4,64,64,2,64]{1,4,3,2,0:T(8,128)(2,1)} %bitcast.152, bf16[4,64,1,128]{3,1,2,0:T(8,128)(2,1)S(1)} %maximum_bitcast_fusion.13, bf16[4,64,1,128]{3,1,2,0:T(8,128)(2,1)S(1)} %get-tuple-element.168), kind=kOutput, calls=%fused_computation.17.clone.1 | convolution fusion | flops 537133056 | bytes 12713984 | tf_op jit(solution)/shard_map/while/body/eval_jaxpr/tiqz,ticqb->tzcb/dot_general | solution.py:68
  319.8 5.5 %reshape.644 = bf16[4,4096,64]{2,1,0:T(8,128)(2,1)} reshape(bf16[1,4,64,4096]{3,2,1,0:T(8,128)(2,1)S(1)} %constant_dynamic-slice_fusion.3) | data formatting | bytes 4194304 | tf_op jit(solution)/shard_map/while/body/eval_jaxpr/reshape | solution.py:57
  325.3 5.4 %convolution_convert_fusion.4 = bf16[4,4096,128]{2,1,0:T(8,128)(2,1)} fusion(bf16[4,4096,64]{2,1,0:T(8,128)(2,1)} %reshape.644, bf16[6,4,64,128]{3,2,1,0:T(8,128)(2,1)} %get-tuple-element.196, s32[]{:T(128)} %get-tuple-element.182), kind=kOutput, calls=%fused_computation.16.clone.1 | convolution fusion | flops 270532608 | bytes 8454656 | tf_op jit(solution)/shard_map/while/body/eval_jaxpr/tmk,tky->tmy/dot_general | solution.py:58
  330.7 14.7 %reshape.645 = bf16[4,64,64,2,64]{4,3,2,1,0:T(2,128)(2,1)} reshape(bf16[4,4096,128]{2,1,0:T(8,128)(2,1)} %convolution_convert_fusion.4) | data formatting | bytes 8388608 | tf_op jit(solution)/shard_map/while/body/eval_jaxpr/reshape | solution.py:61
  345.4 7.7 %bitcast_convert_fusion.2 = bf16[4,64,64,128]{3,2,1,0:T(8,128)(2,1)} fusion(bf16[4,64,64,2,64]{4,3,2,1,0:T(2,128)(2,1)} %reshape.645, bf16[4,64,1,128]{3,1,2,0:T(8,128)(2,1)S(1)} %maximum_bitcast_fusion.12, bf16[4,64,1,128]{3,1,2,0:T(8,128)(2,1)S(1)} %get-tuple-element.164), kind=kOutput, calls=%fused_computation.13.clone.1 | convolution fusion | flops 539033600 | bytes 8519680 | tf_op jit(solution)/shard_map/while/body/eval_jaxpr/tijpc,tjpw->ticw/dot_general | solution.py:63
  353.1 9.4 %copy.128 = bf16[4,64,64,128]{1,3,2,0:T(8,128)(2,1)} copy(bf16[4,64,64,128]{3,2,1,0:T(8,128)(2,1)} %bitcast_convert_fusion.2) | data formatting | bytes 8388608 | tf_op jit(solution)/shard_map/while/body/eval_jaxpr/reshape | solution.py:66
  363.6 5.3 %convolution_bitcast_fusion.2 = f32[4,128,64,64]{1,3,2,0:T(8,128)S(1)} fusion(bf16[4,64,64,2,64]{1,4,3,2,0:T(8,128)(2,1)} %bitcast.152, bf16[4,64,1,128]{3,1,2,0:T(8,128)(2,1)S(1)} %maximum_bitcast_fusion.13, bf16[4,64,1,128]{3,1,2,0:T(8,128)(2,1)S(1)} %get-tuple-element.168), kind=kOutput, calls=%fused_computation.17.clone.1 | convolution fusion | flops 537133056 | bytes 12713984 | tf_op jit(solution)/shard_map/while/body/eval_jaxpr/tiqz,ticqb->tzcb/dot_general | solution.py:68
  375.6 5.5 %reshape.644 = bf16[4,4096,64]{2,1,0:T(8,128)(2,1)} reshape(bf16[1,4,64,4096]{3,2,1,0:T(8,128)(2,1)S(1)} %constant_dynamic-slice_fusion.3) | data formatting | bytes 4194304 | tf_op jit(solution)/shard_map/while/body/eval_jaxpr/reshape | solution.py:57
  381.1 5.4 %convolution_convert_fusion.4 = bf16[4,4096,128]{2,1,0:T(8,128)(2,1)} fusion(bf16[4,4096,64]{2,1,0:T(8,128)(2,1)} %reshape.644, bf16[6,4,64,128]{3,2,1,0:T(8,128)(2,1)} %get-tuple-element.196, s32[]{:T(128)} %get-tuple-element.182), kind=kOutput, calls=%fused_computation.16.clone.1 | convolution fusion | flops 270532608 | bytes 8454656 | tf_op jit(solution)/shard_map/while/body/eval_jaxpr/tmk,tky->tmy/dot_general | solution.py:58
  386.5 14.7 %reshape.645 = bf16[4,64,64,2,64]{4,3,2,1,0:T(2,128)(2,1)} reshape(bf16[4,4096,128]{2,1,0:T(8,128)(2,1)} %convolution_convert_fusion.4) | data formatting | bytes 8388608 | tf_op jit(solution)/shard_map/while/body/eval_jaxpr/reshape | solution.py:61
  401.2 7.7 %bitcast_convert_fusion.2 = bf16[4,64,64,128]{3,2,1,0:T(8,128)(2,1)} fusion(bf16[4,64,64,2,64]{4,3,2,1,0:T(2,128)(2,1)} %reshape.645, bf16[4,64,1,128]{3,1,2,0:T(8,128)(2,1)S(1)} %maximum_bitcast_fusion.12, bf16[4,64,1,128]{3,1,2,0:T(8,128)(2,1)S(1)} %get-tuple-element.164), kind=kOutput, calls=%fused_computation.13.clone.1 | convolution fusion | flops 539033600 | bytes 8519680 | tf_op jit(solution)/shard_map/while/body/eval_jaxpr/tijpc,tjpw->ticw/dot_general | solution.py:63
  408.9 9.4 %copy.128 = bf16[4,64,64,128]{1,3,2,0:T(8,128)(2,1)} copy(bf16[4,64,64,128]{3,2,1,0:T(8,128)(2,1)} %bitcast_convert_fusion.2) | data formatting | bytes 8388608 | tf_op jit(solution)/shard_map/while/body/eval_jaxpr/reshape | solution.py:66
  419.4 5.3 %convolution_bitcast_fusion.2 = f32[4,128,64,64]{1,3,2,0:T(8,128)S(1)} fusion(bf16[4,64,64,2,64]{1,4,3,2,0:T(8,128)(2,1)} %bitcast.152, bf16[4,64,1,128]{3,1,2,0:T(8,128)(2,1)S(1)} %maximum_bitcast_fusion.13, bf16[4,64,1,128]{3,1,2,0:T(8,128)(2,1)S(1)} %get-tuple-element.168), kind=kOutput, calls=%fused_computation.17.clone.1 | convolution fusion | flops 537133056 | bytes 12713984 | tf_op jit(solution)/shard_map/while/body/eval_jaxpr/tiqz,ticqb->tzcb/dot_general | solution.py:68
  431.6 3.5 all-to-all-start.7
  452.5 10.3 %all_to_all.64 = bf16[32,2,768]{2,1,0:T(2,128)(2,1)S(1)} all-to-all(bf16[32,2,768]{2,1,0:T(2,128)(2,1)S(1)} %convert_element_type.92), channel_id=1, replica_groups=mesh['trip'=8,'row'=4] {'trip','row'}, dimensions={0} | all-to-all | bytes 196608 | tf_op jit(solution)/shard_map/all_to_all | solution.py:83
  469.4 6.7 %all_to_all.65 = bf16[4,12,768]{2,1,0:T(8,128)(2,1)S(1)} all-to-all(bf16[4,12,768]{2,1,0:T(8,128)(2,1)S(1)} %convolution_convert_fusion.1), channel_id=1, replica_groups=mesh['trip'=8,'row'=4] {'row'}, dimensions={0} | all-to-all | bytes 147456 | tf_op jit(solution)/shard_map/all_to_all | solution.py:191
  (208 shorter events, 109.5 us)
Async XLA Ops:
  0.0 25.0 %copy-start = (bf16[64,64,128]{2,1,0:T(8,128)(2,1)S(1)}, bf16[64,64,128]{2,1,0:T(8,128)(2,1)}, u32[]{:S(2)}) copy-start(bf16[64,64,128]{2,1,0:T(8,128)(2,1)} %param.15) | copy-start | bytes 3145732
  0.0 34.2 %copy-start.2 = (f32[64,768]{1,0:T(8,128)S(1)}, f32[64,768]{1,0:T(8,128)}, u32[]{:S(2)}) copy-start(f32[64,768]{1,0:T(8,128)} %param.19) | copy-start | bytes 589828
  2.4 0.6 copy-start.7
  3.7 13.3 %all-to-all-start.1 = ((s32[4,1,12]{2,1,0:T(1,128)}), s32[4,1,12]{2,1,0:T(1,128)S(1)}, u32[]{:S(2)}, u32[]{:S(2)}) async-start(s32[4,1,12]{2,1,0:T(1,128)} %bitcast.25), calls=%async_computation.1 | async-start | bytes 4096 | tf_op jit(solution)/shard_map/all_to_all | solution.py:110
  16.9 13.8 %all-to-all-start.3 = ((s32[32,1,2]{2,1,0:T(1,128)}), s32[32,1,2]{2,1,0:T(1,128)S(1)}, u32[]{:S(2)}, u32[]{:S(2)}) async-start(s32[32,1,2]{2,1,0:T(1,128)} %bitcast.33), calls=%async_computation.3 | async-start | bytes 32768 | tf_op jit(solution)/shard_map/all_to_all | solution.py:124
  30.8 7.0 %all-to-all-start = ((s32[4,1,12]{2,1,0:T(1,128)}), s32[4,1,12]{2,1,0:T(1,128)S(1)}, u32[]{:S(2)}, u32[]{:S(2)}) async-start(s32[4,1,12]{2,1,0:T(1,128)} %bitcast.22), calls=%async_computation | async-start | bytes 4096 | tf_op jit(solution)/shard_map/all_to_all | solution.py:162
  34.2 29.1 %copy-start.10 = (pred[64]{0:T(512)(128)(4,1)}, pred[64]{0:T(512)(128)(4,1)S(1)}, u32[]{:S(2)}) copy-start(pred[64]{0:T(512)(128)(4,1)S(1)} %compare_and_fusion.1) | copy-start | bytes 196
  34.2 0.7 copy-start.9
  37.8 10.4 %all-to-all-start.5 = ((bf16[32,2,768]{2,1,0:T(2,128)(2,1)}), bf16[32,2,768]{2,1,0:T(2,128)(2,1)S(1)}, u32[]{:S(2)}, u32[]{:S(2)}) async-start(bf16[32,2,768]{2,1,0:T(2,128)(2,1)} %convert_element_type.87), calls=%async_computation.5 | async-start | bytes 196608 | tf_op jit(solution)/shard_map/all_to_all | solution.py:83
  48.1 15.1 %all-to-all-start.2 = ((bf16[4,12,64,128]{3,2,1,0:T(8,128)(2,1)}), bf16[4,12,64,128]{3,2,1,0:T(8,128)(2,1)S(1)}, u32[]{:S(2)}, u32[]{:S(2)}) async-start(bf16[4,12,64,128]{3,2,1,0:T(8,128)(2,1)} %broadcast_select_fusion.1), calls=%async_computation.2 | async-start | bytes 1572864 | tf_op jit(solution)/shard_map/all_to_all | solution.py:108
  63.3 28.9 %all-to-all-start.4 = ((bf16[32,2,64,128]{3,2,1,0:T(8,128)(2,1)}), bf16[32,2,64,128]{3,2,1,0:T(8,128)(2,1)S(1)}, u32[]{:S(2)}, u32[]{:S(2)}) async-start(bf16[32,2,64,128]{3,2,1,0:T(8,128)(2,1)} %broadcast_select_fusion), calls=%async_computation.4 | async-start | bytes 2097152 | tf_op jit(solution)/shard_map/all_to_all | solution.py:127
  66.3 378.9 %copy-start.12 = (s32[48]{0:T(128)}, s32[48]{0:T(128)S(1)}, u32[]{:S(2)}) copy-start(s32[48]{0:T(128)S(1)} %sub.41) | copy-start | bytes 580
  94.4 336.4 %copy-start.8 = (s32[24]{0:T(128)S(1)}, s32[24]{0:T(128)}, u32[]{:S(2)}) copy-start(s32[24]{0:T(128)} %copy-done.7) | copy-start | bytes 292
  94.4 350.9 %copy-start.5 = (f32[64,64]{1,0:T(8,128)S(1)}, f32[64,64]{1,0:T(8,128)}, u32[]{:S(2)}) copy-start(f32[64,64]{1,0:T(8,128)} %param.21) | copy-start | bytes 49156
  429.4 22.9 %copy-start.11 = (pred[64]{0:T(512)(128)(4,1)S(1)}, pred[64]{0:T(512)(128)(4,1)}, u32[]{:S(2)}) copy-start(pred[64]{0:T(512)(128)(4,1)} %copy-done.10) | copy-start | bytes 196
  429.4 38.2 %copy-start.3 = (bf16[6,4,64,64]{2,3,1,0:T(8,128)(2,1)S(1)}, bf16[6,4,64,64]{2,3,1,0:T(8,128)(2,1)}, u32[]{:S(2)}) copy-start(bf16[6,4,64,64]{2,3,1,0:T(8,128)(2,1)} %get-tuple-element.52) | copy-start | bytes 589828
  431.6 9.1 %all-to-all-start.7 = ((f32[4,1,768]{2,1,0:T(1,128)}), f32[4,1,768]{2,1,0:T(1,128)S(1)}, u32[]{:S(2)}, u32[]{:S(2)}) async-start(f32[4,1,768]{2,1,0:T(1,128)} %reshape.640), calls=%async_computation.7 | async-start | bytes 24576 | tf_op jit(solution)/shard_map/all_to_all | solution.py:161
  440.7 7.6 %all-to-all-start.6 = ((bf16[4,12,768]{2,1,0:T(8,128)(2,1)}), bf16[4,12,768]{2,1,0:T(8,128)(2,1)S(1)}, u32[]{:S(2)}, u32[]{:S(2)}) async-start(bf16[4,12,768]{2,1,0:T(8,128)(2,1)} %convolution_convert_fusion.2), calls=%async_computation.6 | async-start | bytes 196608 | tf_op jit(solution)/shard_map/all_to_all | solution.py:191
  445.6 21.3 %copy-start.6 = (f32[64,64]{1,0:T(8,128)}, f32[64,64]{1,0:T(8,128)S(1)}, u32[]{:S(2)}) copy-start(f32[64,64]{1,0:T(8,128)S(1)} %convolution_add_fusion.4) | copy-start | bytes 49156
  448.6 30.5 %copy-start.1 = (bf16[64,64,128]{2,1,0:T(8,128)(2,1)S(1)}, bf16[64,64,128]{2,1,0:T(8,128)(2,1)}, u32[]{:S(2)}) copy-start(bf16[64,64,128]{2,1,0:T(8,128)(2,1)} %param.15) | copy-start | bytes 3145732
  450.2 0.8 copy-start.4
where the time goes:
time: 484 us; the launch traced here: 479 us
  local copies, waits for them, and re-layouts  225 us (46%)
  matrix products  121 us (25%)
  waiting for transfers between devices  46 us (10%)
  other arithmetic  39.6 us (8%)
  starting transfers between devices  29.7 us (6%)
  blocking collectives  17 us (4%)
    reshape x6, local copies, waits for them, and re-layouts, contract_batch(): section_one = section_one.reshape(batch, branches, branches, 2, branches)  88.2 us
    reshape x6, local copies, waits for them, and re-layouts, contract_batch(): mixed = mixed.reshape(batch, branches, branches, 2, branches)  56.4 us
    dot_general x6, matrix products, contract_batch(): jnp.einsum('tijpc,tjpw->ticw', section_one, mixer_two, preferred_element_...  46.3 us
    reshape x6, local copies, waits for them, and re-layouts, contract_batch(): flat = tensor.reshape(batch, branches * branches, branches)  33.2 us
    dot_general x6, matrix products, contract_batch(): jnp.einsum('tmk,tky->tmy', flat, vec_three, preferred_element_type=jnp.fl...  32.4 us
    dot_general x6, matrix products, contract_batch(): jnp.einsum('tiqz,ticqb->tzcb', mixer_one, mixed, preferred_element_type=j...  31.8 us
    all_to_all x1, waiting for transfers between devices, body(): lax.all_to_all(look_up(eigvecs, queries_here), ('trip', 'row'), split_axi...  20.7 us
    reduce_sum x6, other arithmetic, contract_batch(): jnp.sum(power, 3).astype(jnp.bfloat16)  20.5 us
  transfers between devices with their start and end apart: 8, of which 6 were waited for; matrix products, arithmetic and copies ran while one was open for 6% of the time, Pallas kernels for 0%

commit v1 on v0

v1 whole, which is shorter than its diff:
```python
import functools

import jax
import jax.numpy as jnp
from jax import lax
from jax.experimental import pallas as pl
from jax.experimental.pallas import tpu as pltpu
from jax.sharding import PartitionSpec as P

ITERS = 2
DAMPING = 0.7
AXES = ("trip", "row")
F32 = jnp.float32
BF16 = jnp.bfloat16
CONTRACT_LANES = (((1,), (1,)), ((), ()))
MIB = 2**20


def ranks_of(target):
    extent = target.shape[0]
    matches = target[:, None] == target[None, :]
    earlier = lax.broadcasted_iota(jnp.int32, (extent, extent), 1) < lax.broadcasted_iota(
        jnp.int32, (extent, extent), 0
    )
    return jnp.sum((matches & earlier).astype(jnp.int32), axis=1)


def pack_ints(places, values, extent):
    onehot = lax.broadcasted_iota(jnp.int32, (extent, places.shape[0]), 0) == places[None, :]
    return jnp.sum(jnp.where(onehot, values[None, :], 0), axis=1)


def from_peers(blocks):
    count = len(blocks)
    return [blocks[0]] + [
        lax.ppermute(blocks[d], "row", [(i, (i + d) % count) for i in range(count)])
        for d in range(1, count)
    ]


def first_kernel(places, vec_ref, cubic_ref, out_ref):
    mixer = vec_ref[0].astype(F32).T.astype(BF16)
    extent = cubic_ref.shape[2]
    chunk = min(512, extent)
    for start in range(0, extent, chunk):
        part = cubic_ref[0, :, start : start + chunk]
        out_ref[0, :, start : start + chunk] = jnp.dot(
            mixer, part, preferred_element_type=F32
        ).astype(BF16)


def contract_first(places, table, cubic):
    count, branches, pairs = cubic.shape
    both = 2 * branches
    return pl.pallas_call(
        first_kernel,
        grid_spec=pltpu.PrefetchScalarGridSpec(
            num_scalar_prefetch=1,
            grid=(count,),
            in_specs=[
                pl.BlockSpec((1, branches, both), lambda t, places: (places[t], 0, 0)),
                pl.BlockSpec((1, branches, pairs), lambda t, places: (t, 0, 0)),
            ],
            out_specs=pl.BlockSpec((1, both, pairs), lambda t, places: (t, 0, 0)),
        ),
        out_shape=jax.ShapeDtypeStruct((count, both, pairs), BF16),
        compiler_params=pltpu.CompilerParams(vmem_limit_bytes=32 * MIB),
        cost_estimate=pl.CostEstimate(
            flops=2 * count * both * branches * pairs,
            bytes_accessed=2 * count * (both + branches) * pairs,
            transcendentals=0,
        ),
        name="contract_first",
    )(places, table, cubic)


def second_kernel(
    stride, second_place, third_place, weights, second_ref, third_ref, first_ref, pair_ref, turned
):
    branches = second_ref.shape[1]
    both = 2 * branches
    third = third_ref[0].astype(F32).T
    third_real, third_imag = third[:branches], third[branches:]
    none = jnp.zeros_like(third_real)
    third_mixer = jnp.concatenate(
        [
            jnp.concatenate([third_real, none, -third_imag, none], 1),
            jnp.concatenate([none, third_real, none, -third_imag], 1),
        ],
        0,
    ).astype(BF16)
    second = second_ref[0].astype(F32).T
    second_mixer = jnp.concatenate([second[:branches], second[branches:]], 1).astype(BF16)
    for group in range(branches // 4):
        rows = []
        for half in range(2):
            start = (2 * group + half) * both
            real = first_ref[0, :branches, start : start + both]
            imag = first_ref[0, branches:, start : start + both]
            rows += [jnp.concatenate([real, imag], 1), jnp.concatenate([imag, -real], 1)]
        mixed = lax.dot_general(
            third_mixer, jnp.concatenate(rows, 0), CONTRACT_LANES, preferred_element_type=F32
        )
        for half in range(2):
            for parity in range(2):
                turned[pl.ds(4 * group + 2 * half + parity, branches, stride=stride), :] = mixed[
                    parity * branches : (parity + 1) * branches, half * both : (half + 1) * both
                ]
    total = jnp.zeros((branches, both), F32)
    for group in range(branches // 2):
        columns = []
        for half in range(2):
            start = (2 * group + half) * stride
            block = turned[start : start + branches, :].astype(BF16)
            rotated = jnp.concatenate([-block[:, branches:], block[:, :branches]], 1)
            columns.append(jnp.concatenate([block, rotated], 0))
        values = jnp.dot(second_mixer, jnp.concatenate(columns, 1), preferred_element_type=F32)
        power = values * values
        total = total + power[:, :both] + power[:, both:]
        over_b = jnp.sum(power, 0, keepdims=True)
        turned[pl.ds(2 * group, 1), :] = over_b[:, :both]
        turned[pl.ds(2 * group + 1, 1), :] = over_b[:, both:]
    weight = weights[pl.program_id(0)].astype(F32)
    left = lax.broadcasted_iota(jnp.int32, (branches, both), 1) < branches
    for part, parted in enumerate((total, turned[:branches, :])):
        pairing = (parted + pltpu.roll(parted, branches, 1)) * weight
        pair_ref[0, part * both : part * both + branches, :] = jnp.where(
            left, pairing, 0.0
        ).astype(BF16)
        pair_ref[0, part * both + branches : (part + 1) * both, :] = jnp.where(
            left, 0.0, pairing
        ).astype(BF16)


def contract_rest(second_place, third_place, weights, table, first):
    count, both, pairs = first.shape
    branches = both // 2
    stride = branches + 8
    return pl.pallas_call(
        functools.partial(second_kernel, stride),
        grid_spec=pltpu.PrefetchScalarGridSpec(
            num_scalar_prefetch=3,
            grid=(count,),
            in_specs=[
                pl.BlockSpec((1, branches, both), lambda t, two, three, w: (two[t], 0, 0)),
                pl.BlockSpec((1, branches, both), lambda t, two, three, w: (three[t], 0, 0)),
                pl.BlockSpec((1, both, pairs), lambda t, two, three, w: (t, 0, 0)),
            ],
            out_specs=pl.BlockSpec((1, 2 * both, both), lambda t, two, three, w: (t, 0, 0)),
            scratch_shapes=[pltpu.VMEM((branches * stride, both), F32)],
        ),
        out_shape=jax.ShapeDtypeStruct((count, 2 * both, both), BF16),
        compiler_params=pltpu.CompilerParams(vmem_limit_bytes=32 * MIB),
        cost_estimate=pl.CostEstimate(
            flops=8 * count * both * branches * pairs,
            bytes_accessed=2 * count * both * pairs,
            transcendentals=0,
        ),
        name="contract_rest",
    )(second_place, third_place, weights, table, table, first)


def terms_kernel(
    columns, second_place, third_place, row_place, table_ref, pair_ref, *rest
):
    out_refs, packed = rest[:-1], rest[-1]
    rows, lanes = table_ref.shape[1:]
    packed[...] = jnp.zeros_like(packed)
    row = lax.broadcasted_iota(jnp.int32, (rows, lanes), 0)
    lane = lax.broadcasted_iota(jnp.int32, (rows, lanes), 1)
    is_rest = (row == columns - rows + 1) & (lane >= lanes // 2)
    for t in range(pair_ref.shape[0]):
        states = jnp.concatenate([table_ref[second_place[t]], table_ref[third_place[t]]], 1)
        terms = jnp.dot(states, pair_ref[t], preferred_element_type=F32)
        short = terms.astype(BF16).astype(F32)
        terms = jnp.where(is_rest, pltpu.roll(terms - short, 1, 0), terms)
        packed[row_place[t]] = terms.astype(BF16)
    cap = out_refs[0].shape[0]
    for d, out_ref in enumerate(out_refs):
        out_ref[...] = packed[d * cap : (d + 1) * cap]


def coupling_terms(second_place, third_place, row_place, table, pairs, columns, row_count, row_cap):
    rows, lanes = table.shape[1:]
    return pl.pallas_call(
        functools.partial(terms_kernel, columns),
        in_specs=[pl.BlockSpec(memory_space=pltpu.SMEM)] * 3
        + [pl.BlockSpec(memory_space=pltpu.VMEM)] * 2,
        out_specs=[pl.BlockSpec(memory_space=pltpu.VMEM)] * row_count,
        out_shape=[jax.ShapeDtypeStruct((row_cap, rows, lanes), BF16)] * row_count,
        scratch_shapes=[pltpu.VMEM((row_count * row_cap, rows, lanes), BF16)],
        compiler_params=pltpu.CompilerParams(vmem_limit_bytes=16 * MIB),
        name="coupling_terms",
    )(second_place, third_place, row_place, table, pairs)


def update_kernel(columns, first, last, codes, queries, *rest):
    row_count = codes.shape[0]
    arrived, rest = rest[:row_count], rest[row_count:]
    state_ref, source_ref, rate_ref = rest[:3]
    new_ref, next_ref, total = rest[3:]
    homes, rows, lanes = state_ref.shape
    total[...] = jnp.zeros_like(total)
    for d in range(row_count):
        for slot in range(codes.shape[1]):
            code = codes[d, slot]
            total[code] += arrived[d][slot].astype(F32)
    coupled = total[1:]
    if first:
        at = columns - rows
        rate = coupled[:, at : at + 1, :] + coupled[:, at + 1 : at + 2, :]
        lane = lax.broadcasted_iota(jnp.int32, rate.shape, 2)
        rate = jnp.where(lane < lanes // 2, pltpu.roll(rate, lanes // 2, 2), rate)
        rate = jnp.broadcast_to(rate + rate_ref[...], (homes, rows, lanes))
    else:
        rate = rate_ref[...]
    new = (1.0 - DAMPING) * state_ref[...] + DAMPING * (source_ref[...] + coupled) / rate
    new_ref[...] = new
    if first:
        next_ref[0][...] = rate
    if not last:
        send_ref = next_ref[-1]
        for slot in range(queries.shape[0]):
            send_ref[slot] = new_ref[queries[slot]].astype(BF16)


def update(codes, queries, arrived, state, source, rate, columns, first, last):
    homes, rows, lanes = state.shape
    outs = [jax.ShapeDtypeStruct(state.shape, F32)]
    if first:
        outs.append(jax.ShapeDtypeStruct(state.shape, F32))
    if not last:
        outs.append(jax.ShapeDtypeStruct((queries.shape[0], rows, lanes), BF16))
    row_count = len(arrived)

    def kernel(codes, queries, *refs):
        ins = refs[: row_count + 3]
        new_ref = refs[row_count + 3]
        more = refs[row_count + 4 : row_count + 3 + len(outs)]
        update_kernel(columns, first, last, codes, queries, *ins, new_ref, more, refs[-1])

    return pl.pallas_call(
        kernel,
        in_specs=[pl.BlockSpec(memory_space=pltpu.SMEM)] * 2
        + [pl.BlockSpec(memory_space=pltpu.VMEM)] * (row_count + 3),
        out_specs=[pl.BlockSpec(memory_space=pltpu.VMEM)] * len(outs),
        out_shape=outs,
        scratch_shapes=[pltpu.VMEM((homes + 1, rows, lanes), F32)],
        compiler_params=pltpu.CompilerParams(vmem_limit_bytes=16 * MIB),
        name="update",
    )(codes, queries, *arrived, state, source, rate)


def body(eigvecs, cubic, triplets, weights, deviation, source, base_rate):
    row_count = lax.axis_size("row")
    devices = lax.axis_size("trip") * row_count
    home_rows, branches = eigvecs.shape[:2]
    trip_local = cubic.shape[0]
    columns = deviation.shape[1] // branches
    far_cap = (2 * trip_local + devices - 1) // devices
    row_cap = trip_local // 2
    row_slots = row_count * row_cap
    rows = 8 * ((columns + 2 + 15) // 16)

    def packed(values):
        values = jnp.swapaxes(values.reshape(home_rows, branches, columns), 1, 2)
        values = jnp.pad(values, ((0, 0), (0, 2 * rows - columns), (0, 0)))
        values = values.reshape(home_rows, 2, rows, branches)
        return jnp.swapaxes(values, 1, 2).reshape(home_rows, rows, 2 * branches)

    def unpacked(values):
        values = jnp.swapaxes(values.reshape(home_rows, rows, 2, branches), 1, 2)
        values = values.reshape(home_rows, 2 * rows, branches)[:, :columns]
        return jnp.swapaxes(values, 1, 2).reshape(home_rows, branches * columns)

    first_dev = triplets[:, 0] // home_rows
    first_local = triplets[:, 0] - first_dev * home_rows
    ahead = (first_dev - lax.axis_index("row")) % row_count
    row_place = ahead * row_cap + ranks_of(ahead)
    row_codes = pack_ints(row_place, first_local + 1, row_slots).reshape(row_count, row_cap)
    codes = jnp.stack(from_peers([row_codes[d] for d in range(row_count)]))
    row_queries = jnp.maximum(codes - 1, 0)

    far_index = triplets[:, 1:].reshape(-1)
    far_owner = far_index // home_rows
    far_place = far_owner * far_cap + ranks_of(far_owner)
    far_queries = pack_ints(
        far_place, far_index - far_owner * home_rows, devices * far_cap
    ).reshape(devices, far_cap)

    def far(values):
        return lax.all_to_all(values, AXES, split_axis=0, concat_axis=0, tiled=True)

    queries = far(far_queries).reshape(-1)
    second_place, third_place = far_place.reshape(trip_local, 2).T

    far_table = far(jnp.take(eigvecs, queries, axis=0, mode="clip"))
    first_table = jnp.concatenate(
        [jnp.take(eigvecs, row_queries[0], axis=0, mode="clip")]
        + [
            lax.ppermute(
                jnp.take(eigvecs, row_queries[d], axis=0, mode="clip"),
                "row",
                [(i, (i - d) % row_count) for i in range(row_count)],
            )
            for d in range(1, row_count)
        ],
        0,
    )
    first_part = contract_first(row_place, first_table, cubic)

    state = packed(deviation)
    driven = packed(source)
    one = lax.broadcasted_iota(jnp.int32, state.shape[1:], 0) + rows * (
        lax.broadcasted_iota(jnp.int32, state.shape[1:], 1) // branches
    )
    sent = jnp.where(one == columns, 1.0, state).astype(BF16)
    arrived_state = far(jnp.take(sent, queries, axis=0, mode="clip"))
    rate = jnp.concatenate([base_rate, base_rate], 1)[:, None, :]

    pairs = contract_rest(second_place, third_place, weights, far_table, first_part)

    for step in range(ITERS):
        terms = coupling_terms(
            second_place, third_place, row_place, arrived_state, pairs, columns, row_count, row_cap
        )
        arrived = from_peers(terms)
        first, last = step == 0, step == ITERS - 1
        results = update(codes, queries, arrived, state, driven, rate, columns, first, last)
        state = results[0]
        if first:
            rate = results[1]
        if not last:
            arrived_state = far(results[-1])
    return unpacked(state)


def solution(mesh):
    whole = P(AXES, None, None)
    flat = P(AXES, None)
    in_specs = (whole, whole, flat, P(AXES), flat, flat, flat)
    return jax.shard_map(body, mesh=mesh, in_specs=in_specs, out_specs=flat, check_vma=False)
```

time: 484 us -> 151 us (0.31)
  local copies, waits for them, and re-layouts: 225 us -> 27.5 us
  matrix products: 121 us -> 0 us
  Pallas kernels: 0 us -> 63.3 us
  other arithmetic: 39.6 us -> 3.72 us
  waiting for transfers between devices: 46 us -> 18.5 us
  starting transfers between devices: 29.7 us -> 24.2 us
    reshape x37 -> x9, local copies, waits for them, and re-layouts: 188 us -> 4.07 us  [the longest x2 2.67 us: packed(): return jnp.swapaxes(values, 1, 2).reshape(home_rows, rows, 2 * branches)]
    dot_general x28 -> x0, matrix products: 121 us -> none  [the longest x6 46.3 us: contract_batch(): jnp.einsum('tijpc,tjpw->ticw', section_one, mixer_two, preferred_element_...]
    pallas_call x0 -> x6, Pallas kernels: none -> 63.3 us  [the longest x1 40.8 us: contract_rest(): pl.pallas_call(functools.partial(second_kernel, stride), grid_spec=pltpu....]
    all_to_all x8 -> x3, waiting for transfers between devices: 46 us -> 5.88 us  [far(): return lax.all_to_all(values, AXES, split_axis=0, concat_axis=0, tiled=True)]
    reduce_sum x10 -> x2, other arithmetic: 21.9 us -> 0.19 us  [pack_ints(): return jnp.sum(jnp.where(onehot, values[None, :], 0), axis=1)]
    all_to_all x8 -> x3, starting transfers between devices: 29.7 us -> 12.9 us  [far(): return lax.all_to_all(values, AXES, split_axis=0, concat_axis=0, tiled=True)]
    ppermute x0 -> x12, waiting for transfers between devices: none -> 12.6 us  [the longest x3 9.38 us: body(): lax.ppermute(jnp.take(eigvecs, row_queries[d], axis=0, mode='clip'), 'row...]
    ppermute x0 -> x12, starting transfers between devices: none -> 11.2 us  [the longest x9 9.34 us: from_peers(): lax.ppermute(blocks[d], 'row', [(i, (i + d) % count) for i in range(count)])]
  transfers between devices with their start and end apart: 8 -> 15, of which waited for: 6 -> 6; matrix products, arithmetic and copies ran while one was open for 6% -> 13% of each run, Pallas kernels for 0% -> 40%
where the time goes in v1:
time: 151 us; the launch traced here: 150 us
  Pallas kernels  63.3 us (42%)
  local copies, waits for them, and re-layouts  27.5 us (18%)
  starting transfers between devices  24.2 us (16%)
  waiting for transfers between devices  18.5 us (12%)
  blocking collectives  12.7 us (8%)
  other arithmetic  3.72 us (2%)
    pallas_call x1, Pallas kernels, contract_rest(): pl.pallas_call(functools.partial(second_kernel, stride), grid_spec=pltpu....  40.8 us
    pallas_call x1, Pallas kernels, contract_first(): pl.pallas_call(first_kernel, grid_spec=pltpu.PrefetchScalarGridSpec(num_s...  18.8 us
    all_to_all x3, starting transfers between devices, far(): return lax.all_to_all(values, AXES, split_axis=0, concat_axis=0, tiled=True)  12.9 us
    all_to_all x1, blocking collectives, far(): return lax.all_to_all(values, AXES, split_axis=0, concat_axis=0, tiled=True)  12.7 us
    ppermute x3, waiting for transfers between devices, body(): lax.ppermute(jnp.take(eigvecs, row_queries[d], axis=0, mode='clip'), 'row...  9.38 us
    ppermute x9, starting transfers between devices, from_peers(): lax.ppermute(blocks[d], 'row', [(i, (i + d) % count) for i in range(count)])  9.34 us
    unnamed x15, local copies, waits for them, and re-layouts  9.14 us
    all_to_all x3, waiting for transfers between devices, far(): return lax.all_to_all(values, AXES, split_axis=0, concat_axis=0, tiled=True)  5.88 us
  transfers between devices with their start and end apart: 15, of which 6 were waited for; matrix products, arithmetic and copies ran while one was open for 13% of the time, Pallas kernels for 40%

profile of v1, /device:TPU:0, one launch (start us, length us, event | category | flops | bytes accessed | tf_op | source)
XLA Modules:
  0.0 150.2 jit_solution(10283068218567184024)
XLA Ops:
  0.0 0.8 and_select_fusion.3
  0.8 0.7 fusion.7
  1.7 0.7 fusion.10
  2.5 0.5 collective-permute-start
  3.0 2.5 %collective-permute-start.1 = (s32[12]{0:T(128)S(1)}, s32[12]{0:T(128)S(1)}, u32[]{:S(2)}, u32[]{:S(2)}) collective-permute-start(s32[12]{0:T(128)S(1)} %get-tuple-element.41), channel_id=1, source_target_pairs={{0,2},{1,3},{2,0},{3,1},{4,6},{5,7},{6,4},{7,5},{8,10},{9,11},{10,... | collective-permute-start | bytes 152 | tf_op jit(solution)/shard_map/ppermute | solution.py:36
  5.5 1.4 collective-permute-start.2
  6.9 0.7 slice.46
  8.1 0.7 all_to_all.15
  8.8 4.9 %all-to-all-start = ((s32[32,1,2]{2,1,0:T(1,128)}), s32[32,1,2]{2,1,0:T(1,128)S(1)}, u32[]{:S(2)}, u32[]{:S(2)}) async-start(s32[32,1,2]{2,1,0:T(1,128)} %bitcast.6), calls=%async_computation | async-start | bytes 32768 | tf_op jit(solution)/shard_map/all_to_all | solution.py:292
  13.8 1.1 copy.32
  15.0 5.9 %all-to-all-done = s32[32,1,2]{2,1,0:T(1,128)S(1)} async-done(((s32[32,1,2]{2,1,0:T(1,128)}), s32[32,1,2]{2,1,0:T(1,128)S(1)}, u32[]{:S(2)}, u32[]{:S(2)}) %all-to-all-start) | async-done | bytes 288 | tf_op jit(solution)/shard_map/all_to_all | solution.py:292
  20.8 0.5 broadcast.355
  21.4 0.7 reduce.7
  22.2 1.8 %gather_fusion.1 = bf16[64,64,128]{2,1,0:T(8,128)(2,1)} fusion(bf16[64,64,128]{2,1,0:T(8,128)(2,1)S(1)} %copy-done, s32[1024]{0:T(1024)S(1)} %pad_clamp_fusion.4), kind=kCustom, calls=%fused_computation.1 | custom fusion | bytes 2097408 | tf_op jit(solution)/shard_map/jit(_take)/gather | solution.py:297
  23.9 2.6 %all-to-all-start.2 = ((bf16[64,64,128]{2,1,0:T(8,128)(2,1)}), bf16[64,64,128]{2,1,0:T(8,128)(2,1)S(1)}, u32[]{:S(2)}, u32[]{:S(2)}) async-start(bf16[64,64,128]{2,1,0:T(8,128)(2,1)} %gather_fusion.1), calls=%async_computation.2 | async-start | bytes 2097152 | tf_op jit(solution)/shard_map/all_to_all | solution.py:292
  26.7 1.1 copy.34
  27.8 1.3 reshape.209.refs_4_
  29.2 1.1 copy.35
  30.3 0.8 pad_bitcast_fusion
  31.3 1.3 gather_fusion.3
  32.6 1.4 collective-permute-start.3
  33.9 1.3 gather_fusion.4
  35.6 1.3 gather_fusion.5
  37.1 0.6 gather_fusion.2
  37.7 1.3 gather_fusion
  39.0 1.2 collective-permute-done.3
  40.2 7.7 %collective-permute-done.4 = bf16[12,64,128]{2,1,0:T(8,128)(2,1)S(1)} collective-permute-done((bf16[12,64,128]{2,1,0:T(8,128)(2,1)}, bf16[12,64,128]{2,1,0:T(8,128)(2,1)S(1)}, u32[]{:S(2)}, u32[]{:S(2)}) %collective-permute-start.4) | collective-permute-done | bytes 196640 | tf_op jit(solution)/shard_map/ppermute | solution.py:301
  47.9 0.5 collective-permute-done.5
  48.5 4.6 %copy-done.1 = bf16[24,64,4096]{2,1,0:T(8,128)(2,1)S(1)} copy-done((bf16[24,64,4096]{2,1,0:T(8,128)(2,1)S(1)}, bf16[24,64,4096]{2,1,0:T(8,128)(2,1)}, u32[]{:S(2)}) %copy-start.1) | copy-done | bytes 12582936
  53.1 18.8 %contract_first.1.first_ref = bf16[24,128,4096]{2,1,0:T(8,128)(2,1)} custom-call(s32[24]{0:T(128)S(1)} %multiply_add_fusion.1.places.row_place, bf16[48,64,128]{2,1,0:T(8,128)(2,1)S(1)} %pad_maximum_fusion.vec_ref, bf16[24,64,4096]{2,1,0:T(8,128)(2,1)S(1)} %copy-done.1), custom_call_target="tpu_custom_call" | custom-call | flops 1610612736 | bytes 37748736 | tf_op jit(solution)/shard_map/contract_first/pallas_call | solution.py:55
  71.9 1.1 copy-done.2
  73.0 5.4 %all-to-all-start.1 = ((bf16[64,8,128]{2,1,0:T(8,128)(2,1)}), bf16[64,8,128]{2,1,0:T(8,128)(2,1)S(1)}, u32[]{:S(2)}, u32[]{:S(2)}) async-start(bf16[64,8,128]{2,1,0:T(8,128)(2,1)} %gather_fusion), calls=%async_computation.1 | async-start | bytes 262144 | tf_op jit(solution)/shard_map/all_to_all | solution.py:292
  78.4 1.2 copy-done.3
  79.6 40.8 %contract_rest.1.pair_ref = bf16[24,256,128]{2,1,0:T(8,128)(2,1)S(1)} custom-call(s32[24]{0:T(128)S(1)} %get-tuple-element.28.second_place, s32[24]{0:T(128)S(1)} %get-tuple-element.27.third_place, s32[24]{0:T(128)S(1)} %copy-done.4, bf16[64,64,128]{2,1,0:T(8,128)(2,1)S(1)} %copy-done.3, bf16[64,64,128]{2,1,0:T(8,128)(2,1)S(1)} %copy-done.3, ...), custom_call_target="tpu_custom_call" | custom-call | flops 6442450944 | bytes 25165824 | tf_op jit(solution)/shard_map/contract_rest/pallas_call | solution.py:139
  120.4 0.9 coupling_terms.2
  121.6 1.7 %collective-permute-start.7 = (bf16[12,8,128]{2,1,0:T(8,128)(2,1)S(1)}, bf16[12,8,128]{2,1,0:T(8,128)(2,1)S(1)}, u32[]{:S(2)}, u32[]{:S(2)}) collective-permute-start(bf16[12,8,128]{2,1,0:T(8,128)(2,1)S(1)} %get-tuple-element.18), channel_id=1, source_target_pairs={{0,2},{1,3},{2,0},{3,1},{4,6},{5,7},{6,4},{7,5},{8,10},{9,11},{10,... | collective-permute-start | bytes 73736 | tf_op jit(solution)/shard_map/ppermute | solution.py:36
  123.3 1.3 collective-permute-start.8
  124.7 2.2 %copy.37 = f32[64,8,2,64]{3,2,1,0:T(2,128)} copy(f32[64,8,2,64]{0,1,2,3:T(8,128)} %pad_bitcast_fusion) | data formatting | bytes 524288 | tf_op jit(solution)/shard_map/transpose | solution.py:269
  126.8 1.3 reshape.212.refs_5_
  128.2 1.0 update.2
  129.2 12.7 %all_to_all.24.table_ref = bf16[64,8,128]{2,1,0:T(8,128)(2,1)S(1)} all-to-all(bf16[64,8,128]{2,1,0:T(8,128)(2,1)S(1)} %get-tuple-element.20), channel_id=1, replica_groups=mesh['trip'=8,'row'=4] {'trip','row'}, dimensions={0} | all-to-all | bytes 262144 | tf_op jit(solution)/shard_map/all_to_all | solution.py:292
  141.9 0.9 coupling_terms.3
  142.8 0.5 collective-permute-start.10
  143.3 1.1 collective-permute-start.11
  144.4 2.3 %collective-permute-done.10.refs_2_ = bf16[12,8,128]{2,1,0:T(8,128)(2,1)S(1)} collective-permute-done((bf16[12,8,128]{2,1,0:T(8,128)(2,1)S(1)}, bf16[12,8,128]{2,1,0:T(8,128)(2,1)S(1)}, u32[]{:S(2)}, u32[]{:S(2)}) %collective-permute-start.10) | collective-permute-done | bytes 24608 | tf_op jit(solution)/shard_map/ppermute | solution.py:36
  146.7 1.0 collective-permute-done.9.refs_1_
  147.7 0.9 update.3
  149.4 0.8 copy.40
  (57 shorter events, 3.2 us)
Async XLA Ops:
  0.0 22.2 %copy-start = (bf16[64,64,128]{2,1,0:T(8,128)(2,1)S(1)}, bf16[64,64,128]{2,1,0:T(8,128)(2,1)}, u32[]{:S(2)}) copy-start(bf16[64,64,128]{2,1,0:T(8,128)(2,1)} %param.7) | copy-start | bytes 3145732
  2.5 28.7 %collective-permute-start = (s32[12]{0:T(128)S(1)}, s32[12]{0:T(128)S(1)}, u32[]{:S(2)}, u32[]{:S(2)}) collective-permute-start(s32[12]{0:T(128)S(1)} %get-tuple-element.42), channel_id=1, source_target_pairs={{0,1},{1,2},{2,3},{3,0},{4,5},{5,6},{6,7},{7,4},{8,9},{9,10},{10,1... | collective-permute-start | bytes 152 | tf_op jit(solution)/shard_map/ppermute | solution.py:36
  3.0 28.2 %collective-permute-start.1 = (s32[12]{0:T(128)S(1)}, s32[12]{0:T(128)S(1)}, u32[]{:S(2)}, u32[]{:S(2)}) collective-permute-start(s32[12]{0:T(128)S(1)} %get-tuple-element.41), channel_id=1, source_target_pairs={{0,2},{1,3},{2,0},{3,1},{4,6},{5,7},{6,4},{7,5},{8,10},{9,11},{10,... | collective-permute-start | bytes 152 | tf_op jit(solution)/shard_map/ppermute | solution.py:36
  5.5 25.7 %collective-permute-start.2 = (s32[12]{0:T(128)S(1)}, s32[12]{0:T(128)S(1)}, u32[]{:S(2)}, u32[]{:S(2)}) collective-permute-start(s32[12]{0:T(128)S(1)} %get-tuple-element.40), channel_id=1, source_target_pairs={{0,3},{1,0},{2,1},{3,2},{4,7},{5,4},{6,5},{7,6},{8,11},{9,8},{10,9... | collective-permute-start | bytes 152 | tf_op jit(solution)/shard_map/ppermute | solution.py:36
  8.8 12.0 %all-to-all-start = ((s32[32,1,2]{2,1,0:T(1,128)}), s32[32,1,2]{2,1,0:T(1,128)S(1)}, u32[]{:S(2)}, u32[]{:S(2)}) async-start(s32[32,1,2]{2,1,0:T(1,128)} %bitcast.6), calls=%async_computation | async-start | bytes 32768 | tf_op jit(solution)/shard_map/all_to_all | solution.py:292
  23.9 48.0 %all-to-all-start.2 = ((bf16[64,64,128]{2,1,0:T(8,128)(2,1)}), bf16[64,64,128]{2,1,0:T(8,128)(2,1)S(1)}, u32[]{:S(2)}, u32[]{:S(2)}) async-start(bf16[64,64,128]{2,1,0:T(8,128)(2,1)} %gather_fusion.1), calls=%async_computation.2 | async-start | bytes 2097152 | tf_op jit(solution)/shard_map/all_to_all | solution.py:292
  32.6 7.7 %collective-permute-start.3 = (bf16[12,64,128]{2,1,0:T(8,128)(2,1)}, bf16[12,64,128]{2,1,0:T(8,128)(2,1)S(1)}, u32[]{:S(2)}, u32[]{:S(2)}) collective-permute-start(bf16[12,64,128]{2,1,0:T(8,128)(2,1)} %gather_fusion.3), channel_id=1, source_target_pairs={{0,3},{1,0},{2,1},{3,2},{4,7},{5,4},{6,5},{7,6},{8,11},{9,8},{10,9... | collective-permute-start | bytes 589832 | tf_op jit(solution)/shard_map/ppermute | solution.py:301
  35.2 12.7 %collective-permute-start.4 = (bf16[12,64,128]{2,1,0:T(8,128)(2,1)}, bf16[12,64,128]{2,1,0:T(8,128)(2,1)S(1)}, u32[]{:S(2)}, u32[]{:S(2)}) collective-permute-start(bf16[12,64,128]{2,1,0:T(8,128)(2,1)} %gather_fusion.4), channel_id=1, source_target_pairs={{0,2},{1,3},{2,0},{3,1},{4,6},{5,7},{6,4},{7,5},{8,10},{9,11},{10,... | collective-permute-start | bytes 589832 | tf_op jit(solution)/shard_map/ppermute | solution.py:301
  36.8 11.6 %collective-permute-start.5 = (bf16[12,64,128]{2,1,0:T(8,128)(2,1)}, bf16[12,64,128]{2,1,0:T(8,128)(2,1)S(1)}, u32[]{:S(2)}, u32[]{:S(2)}) collective-permute-start(bf16[12,64,128]{2,1,0:T(8,128)(2,1)} %gather_fusion.5), channel_id=1, source_target_pairs={{0,1},{1,2},{2,3},{3,0},{4,5},{5,6},{6,7},{7,4},{8,9},{9,10},{10,1... | collective-permute-start | bytes 589832 | tf_op jit(solution)/shard_map/ppermute | solution.py:301
  48.5 4.6 %copy-start.1 = (bf16[24,64,4096]{2,1,0:T(8,128)(2,1)S(1)}, bf16[24,64,4096]{2,1,0:T(8,128)(2,1)}, u32[]{:S(2)}) copy-start(bf16[24,64,4096]{2,1,0:T(8,128)(2,1)} %cubic_ref.1) | copy-start | bytes 37748740
  53.1 25.3 %copy-start.4 = (s32[24]{0:T(128)S(1)}, s32[24]{0:T(128)}, u32[]{:S(2)}) copy-start(s32[24]{0:T(128)} %weights.1) | copy-start | bytes 292
  71.9 1.1 copy-start.2
  73.0 47.4 %all-to-all-start.1 = ((bf16[64,8,128]{2,1,0:T(8,128)(2,1)}), bf16[64,8,128]{2,1,0:T(8,128)(2,1)S(1)}, u32[]{:S(2)}, u32[]{:S(2)}) async-start(bf16[64,8,128]{2,1,0:T(8,128)(2,1)} %gather_fusion), calls=%async_computation.1 | async-start | bytes 262144 | tf_op jit(solution)/shard_map/all_to_all | solution.py:292
  78.4 1.2 copy-start.3
  79.6 45.0 %copy-start.5 = (f32[64,64]{1,0:T(8,128)S(1)}, f32[64,64]{1,0:T(8,128)}, u32[]{:S(2)}) copy-start(f32[64,64]{1,0:T(8,128)} %param.13) | copy-start | bytes 49156
  121.3 6.9 %collective-permute-start.6 = (bf16[12,8,128]{2,1,0:T(8,128)(2,1)S(1)}, bf16[12,8,128]{2,1,0:T(8,128)(2,1)S(1)}, u32[]{:S(2)}, u32[]{:S(2)}) collective-permute-start(bf16[12,8,128]{2,1,0:T(8,128)(2,1)S(1)} %get-tuple-element.17), channel_id=1, source_target_pairs={{0,1},{1,2},{2,3},{3,0},{4,5},{5,6},{6,7},{7,4},{8,9},{9,10},{10,1... | collective-permute-start | bytes 73736 | tf_op jit(solution)/shard_map/ppermute | solution.py:36
  121.6 6.6 %collective-permute-start.7 = (bf16[12,8,128]{2,1,0:T(8,128)(2,1)S(1)}, bf16[12,8,128]{2,1,0:T(8,128)(2,1)S(1)}, u32[]{:S(2)}, u32[]{:S(2)}) collective-permute-start(bf16[12,8,128]{2,1,0:T(8,128)(2,1)S(1)} %get-tuple-element.18), channel_id=1, source_target_pairs={{0,2},{1,3},{2,0},{3,1},{4,6},{5,7},{6,4},{7,5},{8,10},{9,11},{10,... | collective-permute-start | bytes 73736 | tf_op jit(solution)/shard_map/ppermute | solution.py:36
  123.3 4.9 %collective-permute-start.8 = (bf16[12,8,128]{2,1,0:T(8,128)(2,1)S(1)}, bf16[12,8,128]{2,1,0:T(8,128)(2,1)S(1)}, u32[]{:S(2)}, u32[]{:S(2)}) collective-permute-start(bf16[12,8,128]{2,1,0:T(8,128)(2,1)S(1)} %get-tuple-element.19), channel_id=1, source_target_pairs={{0,3},{1,0},{2,1},{3,2},{4,7},{5,4},{6,5},{7,6},{8,11},{9,8},{10,9... | collective-permute-start | bytes 73736 | tf_op jit(solution)/shard_map/ppermute | solution.py:36
  142.8 3.9 %collective-permute-start.10 = (bf16[12,8,128]{2,1,0:T(8,128)(2,1)S(1)}, bf16[12,8,128]{2,1,0:T(8,128)(2,1)S(1)}, u32[]{:S(2)}, u32[]{:S(2)}) collective-permute-start(bf16[12,8,128]{2,1,0:T(8,128)(2,1)S(1)} %get-tuple-element.23), channel_id=1, source_target_pairs={{0,2},{1,3},{2,0},{3,1},{4,6},{5,7},{6,4},{7,5},{8,10},{9,11},{10,... | collective-permute-start | bytes 73736 | tf_op jit(solution)/shard_map/ppermute | solution.py:36
  143.3 3.4 %collective-permute-start.11 = (bf16[12,8,128]{2,1,0:T(8,128)(2,1)S(1)}, bf16[12,8,128]{2,1,0:T(8,128)(2,1)S(1)}, u32[]{:S(2)}, u32[]{:S(2)}) collective-permute-start(bf16[12,8,128]{2,1,0:T(8,128)(2,1)S(1)} %get-tuple-element.24), channel_id=1, source_target_pairs={{0,3},{1,0},{2,1},{3,2},{4,7},{5,4},{6,5},{7,6},{8,11},{9,8},{10,9... | collective-permute-start | bytes 73736 | tf_op jit(solution)/shard_map/ppermute | solution.py:36
  144.4 3.3 %collective-permute-start.9 = (bf16[12,8,128]{2,1,0:T(8,128)(2,1)S(1)}, bf16[12,8,128]{2,1,0:T(8,128)(2,1)S(1)}, u32[]{:S(2)}, u32[]{:S(2)}) collective-permute-start(bf16[12,8,128]{2,1,0:T(8,128)(2,1)S(1)} %get-tuple-element.22), channel_id=1, source_target_pairs={{0,1},{1,2},{2,3},{3,0},{4,5},{5,6},{6,7},{7,4},{8,9},{9,10},{10,1... | collective-permute-start | bytes 73736 | tf_op jit(solution)/shard_map/ppermute | solution.py:36

commit v2 on v1

--- a/solution.py
+++ b/solution.py
@@ -12,7 +12,7 @@
 AXES = ("trip", "row")
 F32 = jnp.float32
 BF16 = jnp.bfloat16
-CONTRACT_LANES = (((1,), (1,)), ((), ()))
+LANES = 128
 MIB = 2**20
 
 
@@ -38,15 +38,56 @@
     ]
 
 
-def first_kernel(places, vec_ref, cubic_ref, out_ref):
-    mixer = vec_ref[0].astype(F32).T.astype(BF16)
-    extent = cubic_ref.shape[2]
-    chunk = min(512, extent)
-    for start in range(0, extent, chunk):
-        part = cubic_ref[0, :, start : start + chunk]
-        out_ref[0, :, start : start + chunk] = jnp.dot(
-            mixer, part, preferred_element_type=F32
-        ).astype(BF16)
+def lookup_kernel(far_queries, row_queries, vec_ref, state_ref, far_ref, far_state_ref, *row_refs):
+    for slot in range(far_queries.shape[0]):
+        far_ref[slot] = vec_ref[far_queries[slot]]
+        far_state_ref[slot] = state_ref[far_queries[slot]]
+    for d, row_ref in enumerate(row_refs):
+        for slot in range(row_ref.shape[0]):
+            row_ref[slot] = vec_ref[row_queries[d, slot]]
+
+
+def look_up(far_queries, row_queries, eigvecs, state):
+    row_count, row_cap = row_queries.shape
+    far_slots = far_queries.shape[0]
+    outs = [
+        jax.ShapeDtypeStruct((far_slots,) + eigvecs.shape[1:], eigvecs.dtype),
+        jax.ShapeDtypeStruct((far_slots,) + state.shape[1:], state.dtype),
+    ] + [jax.ShapeDtypeStruct((row_cap,) + eigvecs.shape[1:], eigvecs.dtype)] * row_count
+    found = pl.pallas_call(
+        lookup_kernel,
+        in_specs=[pl.BlockSpec(memory_space=pltpu.SMEM)] * 2
+        + [pl.BlockSpec(memory_space=pltpu.VMEM)] * 2,
+        out_specs=[pl.BlockSpec(memory_space=pltpu.VMEM)] * len(outs),
+        out_shape=outs,
+        compiler_params=pltpu.CompilerParams(vmem_limit_bytes=16 * MIB),
+        name="look_up",
+    )(far_queries, row_queries, eigvecs, state)
+    return found[0], found[1], found[2:]
+
+
+def first_kernel(places, one_ref, two_ref, cubic_ref, out_ref):
+    branches = cubic_ref.shape[1]
+    both = 2 * branches
+    one, two = one_ref[0], two_ref[0]
+    none = jnp.zeros((branches, branches), one.dtype)
+    mixer = jnp.concatenate(
+        [
+            jnp.concatenate([one[:, :branches], none, one[:, branches:], none], 1),
+            jnp.concatenate([none, two[:, :branches], none, two[:, branches:]], 1),
+        ],
+        0,
+    )
+    step = 4
+    for start in range(0, branches, step):
+        lanes = slice(start * branches, (start + step) * branches)
+        turned = jnp.concatenate([cubic_ref[0, :, lanes], cubic_ref[1, :, lanes]], 0).T
+        mixed = jnp.dot(turned, mixer, preferred_element_type=F32).astype(BF16)
+        for j in range(step):
+            for part in range(2):
+                out_ref[0, start + j, part * branches : (part + 1) * branches] = mixed[
+                    j * branches : (j + 1) * branches, part * both : (part + 1) * both
+                ]
 
 
 def contract_first(places, table, cubic):
@@ -56,108 +97,115 @@
         first_kernel,
         grid_spec=pltpu.PrefetchScalarGridSpec(
             num_scalar_prefetch=1,
-            grid=(count,),
+            grid=(count // 2,),
             in_specs=[
-                pl.BlockSpec((1, branches, both), lambda t, places: (places[t], 0, 0)),
-                pl.BlockSpec((1, branches, pairs), lambda t, places: (t, 0, 0)),
+                pl.BlockSpec((1, branches, both), lambda t, places: (places[2 * t], 0, 0)),
+                pl.BlockSpec((1, branches, both), lambda t, places: (places[2 * t + 1], 0, 0)),
+                pl.BlockSpec((2, branches, pairs), lambda t, places: (t, 0, 0)),
             ],
-            out_specs=pl.BlockSpec((1, both, pairs), lambda t, places: (t, 0, 0)),
+            out_specs=pl.BlockSpec((1, branches, both, both), lambda t, places: (t, 0, 0, 0)),
         ),
-        out_shape=jax.ShapeDtypeStruct((count, both, pairs), BF16),
-        compiler_params=pltpu.CompilerParams(vmem_limit_bytes=32 * MIB),
+        out_shape=jax.ShapeDtypeStruct((count // 2, branches, both, both), BF16),
+        compiler_params=pltpu.CompilerParams(vmem_limit_bytes=60 * MIB),
         cost_estimate=pl.CostEstimate(
             flops=2 * count * both * branches * pairs,
             bytes_accessed=2 * count * (both + branches) * pairs,
             transcendentals=0,
         ),
         name="contract_first",
-    )(places, table, cubic)
+    )(places, table, table, cubic)
 
 
 def second_kernel(
-    stride, second_place, third_place, weights, second_ref, third_ref, first_ref, pair_ref, turned
+    stride, second_place, third_place, weights, *refs
 ):
-    branches = second_ref.shape[1]
+    second_refs, third_refs = refs[:2], refs[2:4]
+    first_ref, pair_ref, turned = refs[4:]
+    branches = second_refs[0].shape[1]
     both = 2 * branches
-    third = third_ref[0].astype(F32).T
-    third_real, third_imag = third[:branches], third[branches:]
-    none = jnp.zeros_like(third_real)
-    third_mixer = jnp.concatenate(
-        [
-            jnp.concatenate([third_real, none, -third_imag, none], 1),
-            jnp.concatenate([none, third_real, none, -third_imag], 1),
-        ],
-        0,
-    ).astype(BF16)
-    second = second_ref[0].astype(F32).T
-    second_mixer = jnp.concatenate([second[:branches], second[branches:]], 1).astype(BF16)
-    for group in range(branches // 4):
-        rows = []
-        for half in range(2):
-            start = (2 * group + half) * both
-            real = first_ref[0, :branches, start : start + both]
-            imag = first_ref[0, branches:, start : start + both]
-            rows += [jnp.concatenate([real, imag], 1), jnp.concatenate([imag, -real], 1)]
-        mixed = lax.dot_general(
-            third_mixer, jnp.concatenate(rows, 0), CONTRACT_LANES, preferred_element_type=F32
+
+    def mixer(vec_refs):
+        columns = []
+        for vec_ref in vec_refs:
+            vectors = vec_ref[0].astype(F32).T
+            real, imag = vectors[:branches], vectors[branches:]
+            columns += [jnp.concatenate([real, imag], 0), jnp.concatenate([-imag, real], 0)]
+        return jnp.concatenate(columns, 1).astype(BF16)
+
+    left = lax.broadcasted_iota(jnp.int32, (both, both), 1) < branches
+    none = jnp.zeros((both, both), BF16)
+
+    def apart(block):
+        return jnp.concatenate([jnp.where(left, block, none), jnp.where(left, none, block)], 0)
+
+    second_mixer, third_mixer = mixer(second_refs), mixer(third_refs)
+    for j in range(0, branches, 2):
+        mixed = jnp.dot(
+            third_mixer,
+            jnp.concatenate([apart(first_ref[0, j]), apart(first_ref[0, j + 1])], 1),
+            preferred_element_type=F32,
         )
         for half in range(2):
-            for parity in range(2):
-                turned[pl.ds(4 * group + 2 * half + parity, branches, stride=stride), :] = mixed[
-                    parity * branches : (parity + 1) * branches, half * both : (half + 1) * both
+            for part in range(2):
+                turned[pl.ds(part * branches + j + half, branches, stride=stride), :] = mixed[
+                    part * branches : (part + 1) * branches, half * both : (half + 1) * both
                 ]
     total = jnp.zeros((branches, both), F32)
-    for group in range(branches // 2):
-        columns = []
+    for c in range(0, branches, 2):
+        columns = [
+            apart(turned[(c + half) * stride : (c + half) * stride + both, :].astype(BF16))
+            for half in range(2)
+        ]
+        values = jnp.dot(second_mixer, jnp.concatenate(columns, 1), preferred_element_type=F32)
+        real, imag = values[:branches], values[branches:]
+        power = real * real + imag * imag
+        over_b = jnp.sum(power, 0, keepdims=True)
         for half in range(2):
-            start = (2 * group + half) * stride
-            block = turned[start : start + branches, :].astype(BF16)
-            rotated = jnp.concatenate([-block[:, branches:], block[:, :branches]], 1)
-            columns.append(jnp.concatenate([block, rotated], 0))
-        values = jnp.dot(second_mixer, jnp.concatenate(columns, 1), preferred_element_type=F32)
-        power = values * values
-        total = total + power[:, :both] + power[:, both:]
-        over_b = jnp.sum(power, 0, keepdims=True)
-        turned[pl.ds(2 * group, 1), :] = over_b[:, :both]
-        turned[pl.ds(2 * group + 1, 1), :] = over_b[:, both:]
-    weight = weights[pl.program_id(0)].astype(F32)
-    left = lax.broadcasted_iota(jnp.int32, (branches, both), 1) < branches
+            lanes = slice(half * both, (half + 1) * both)
+            total = total + power[:, lanes]
+            turned[pl.ds(c + half, 1), :] = over_b[:, lanes]
+    step = pl.program_id(0)
+    left = left[:branches]
+    weight = jnp.where(left, weights[2 * step].astype(F32), weights[2 * step + 1].astype(F32))
     for part, parted in enumerate((total, turned[:branches, :])):
-        pairing = (parted + pltpu.roll(parted, branches, 1)) * weight
-        pair_ref[0, part * both : part * both + branches, :] = jnp.where(
-            left, pairing, 0.0
-        ).astype(BF16)
-        pair_ref[0, part * both + branches : (part + 1) * both, :] = jnp.where(
-            left, 0.0, pairing
-        ).astype(BF16)
+        own = parted * weight
+        other = pltpu.roll(own, branches, 1)
+        for t, (upper, lower) in enumerate(((own, other), (other, own))):
+            start = part * both
+            pair_ref[t, start : start + branches, :] = jnp.where(left, upper, 0.0).astype(BF16)
+            pair_ref[t, start + branches : start + both, :] = jnp.where(left, 0.0, lower).astype(
+                BF16
+            )
 
 
 def contract_rest(second_place, third_place, weights, table, first):
-    count, both, pairs = first.shape
-    branches = both // 2
-    stride = branches + 8
+    steps, branches, both = first.shape[:3]
+    stride = both + 8
+
+    def vectors(which, t):
+        return pl.BlockSpec(
+            (1, branches, both), lambda s, *places: (places[which][2 * s + t], 0, 0)
+        )
+
     return pl.pallas_call(
         functools.partial(second_kernel, stride),
         grid_spec=pltpu.PrefetchScalarGridSpec(
             num_scalar_prefetch=3,
-            grid=(count,),
-            in_specs=[
-                pl.BlockSpec((1, branches, both), lambda t, two, three, w: (two[t], 0, 0)),
-                pl.BlockSpec((1, branches, both), lambda t, two, three, w: (three[t], 0, 0)),
-                pl.BlockSpec((1, both, pairs), lambda t, two, three, w: (t, 0, 0)),
-            ],
-            out_specs=pl.BlockSpec((1, 2 * both, both), lambda t, two, three, w: (t, 0, 0)),
+            grid=(steps,),
+            in_specs=[vectors(0, 0), vectors(0, 1), vectors(1, 0), vectors(1, 1)]
+            + [pl.BlockSpec((1, branches, both, both), lambda s, *places: (s, 0, 0, 0))],
+            out_specs=pl.BlockSpec((2, 2 * both, both), lambda s, *places: (s, 0, 0)),
             scratch_shapes=[pltpu.VMEM((branches * stride, both), F32)],
         ),
-        out_shape=jax.ShapeDtypeStruct((count, 2 * both, both), BF16),
-        compiler_params=pltpu.CompilerParams(vmem_limit_bytes=32 * MIB),
+        out_shape=jax.ShapeDtypeStruct((2 * steps, 2 * both, both), BF16),
+        compiler_params=pltpu.CompilerParams(vmem_limit_bytes=60 * MIB),
         cost_estimate=pl.CostEstimate(
-            flops=8 * count * both * branches * pairs,
-            bytes_accessed=2 * count * both * pairs,
+            flops=16 * steps * both * both * branches * branches,
+            bytes_accessed=2 * steps * both * both * branches,
             transcendentals=0,
         ),
         name="contract_rest",
-    )(second_place, third_place, weights, table, table, first)
+    )(second_place, third_place, weights, table, table, table, table, first)
 
 
 def terms_kernel(
@@ -273,51 +321,54 @@
         values = values.reshape(home_rows, 2 * rows, branches)[:, :columns]
         return jnp.swapaxes(values, 1, 2).reshape(home_rows, branches * columns)
 
-    first_dev = triplets[:, 0] // home_rows
-    first_local = triplets[:, 0] - first_dev * home_rows
-    ahead = (first_dev - lax.axis_index("row")) % row_count
-    row_place = ahead * row_cap + ranks_of(ahead)
-    row_codes = pack_ints(row_place, first_local + 1, row_slots).reshape(row_count, row_cap)
-    codes = jnp.stack(from_peers([row_codes[d] for d in range(row_count)]))
-    row_queries = jnp.maximum(codes - 1, 0)
-
-    far_index = triplets[:, 1:].reshape(-1)
-    far_owner = far_index // home_rows
-    far_place = far_owner * far_cap + ranks_of(far_owner)
-    far_queries = pack_ints(
-        far_place, far_index - far_owner * home_rows, devices * far_cap
-    ).reshape(devices, far_cap)
+    me = lax.axis_index("trip") * row_count + lax.axis_index("row")
+    owner = triplets // home_rows
+    local = triplets - owner * home_rows
+    first_dev, far_owner = owner[:, 0], owner[:, 1:].reshape(-1)
+    ahead = (first_dev - me) % row_count
+    row_rank = ranks_of(first_dev)
+    far_rank = ranks_of(far_owner)
+    row_place = ahead * row_cap + row_rank
+    far_place = far_owner * far_cap + far_rank
+    message = pack_ints(
+        jnp.concatenate([far_owner * LANES + far_rank, first_dev * LANES + far_cap + row_rank]),
+        jnp.concatenate([local[:, 1:].reshape(-1), local[:, 0] + 1]),
+        devices * LANES,
+    ).reshape(devices, 1, LANES)
 
     def far(values):
         return lax.all_to_all(values, AXES, split_axis=0, concat_axis=0, tiled=True)
 
-    queries = far(far_queries).reshape(-1)
+    heard = far(message)[:, 0]
+    queries = heard[:, :far_cap].reshape(-1)
     second_place, third_place = far_place.reshape(trip_local, 2).T
-
-    far_table = far(jnp.take(eigvecs, queries, axis=0, mode="clip"))
+    group = lax.dynamic_slice(
+        heard, (lax.axis_index("trip") * row_count, far_cap), (row_count, row_cap)
+    )
+    codes = jnp.take(
+        group, (lax.axis_index("row") - jnp.arange(row_count)) % row_count, axis=0, mode="clip"
+    )
+
+    state = packed(deviation)
+    one = lax.broadcasted_iota(jnp.int32, state.shape[1:], 0) + rows * (
+        lax.broadcasted_iota(jnp.int32, state.shape[1:], 1) // branches
+    )
+    sent_state = jnp.where(one == columns, 1.0, state).astype(BF16)
+    far_vecs, far_state, row_vecs = look_up(queries, jnp.maximum(codes - 1, 0), eigvecs, sent_state)
+    far_table = far(far_vecs)
     first_table = jnp.concatenate(
-        [jnp.take(eigvecs, row_queries[0], axis=0, mode="clip")]
+        [row_vecs[0]]
         + [
-            lax.ppermute(
-                jnp.take(eigvecs, row_queries[d], axis=0, mode="clip"),
-                "row",
-                [(i, (i - d) % row_count) for i in range(row_count)],
-            )
+            lax.ppermute(row_vecs[d], "row", [(i, (i - d) % row_count) for i in range(row_count)])
             for d in range(1, row_count)
         ],
         0,
     )
+    driven = packed(source)
+    rate = jnp.concatenate([base_rate, base_rate], 1)[:, None, :]
+    first_table, driven, rate = lax.optimization_barrier((first_table, driven, rate))
     first_part = contract_first(row_place, first_table, cubic)
-
-    state = packed(deviation)
-    driven = packed(source)
-    one = lax.broadcasted_iota(jnp.int32, state.shape[1:], 0) + rows * (
-        lax.broadcasted_iota(jnp.int32, state.shape[1:], 1) // branches
-    )
-    sent = jnp.where(one == columns, 1.0, state).astype(BF16)
-    arrived_state = far(jnp.take(sent, queries, axis=0, mode="clip"))
-    rate = jnp.concatenate([base_rate, base_rate], 1)[:, None, :]
-
+    arrived_state = far(far_state)
     pairs = contract_rest(second_place, third_place, weights, far_table, first_part)
 
     for step in range(ITERS):

time: 151 us -> 132 us (0.87)
  local copies, waits for them, and re-layouts: 27.5 us -> 8.77 us
  Pallas kernels: 63.3 us -> 55.3 us
  waiting for transfers between devices: 18.5 us -> 25.5 us
    pallas_call x1, Pallas kernels: 40.8 us -> 30 us  [contract_rest(): pl.pallas_call(functools.partial(second_kernel, stride), grid_spec=pltpu....]
    ppermute x3, waiting for transfers between devices: 9.38 us -> 16.9 us  [body(): lax.ppermute(row_vecs[d], 'row', [(i, (i - d) % row_count) for i in range...]
    gather x6 -> x1, local copies, waits for them, and re-layouts: 7.36 us -> 0.56 us  [body(): jnp.take(group, (lax.axis_index('row') - jnp.arange(row_count)) % row_cou...]
    unnamed x15 -> x19, local copies, waits for them, and re-layouts: 9.14 us -> 3.45 us
    ppermute x9 -> x6, starting transfers between devices: 9.34 us -> 5.26 us  [from_peers(): lax.ppermute(blocks[d], 'row', [(i, (i + d) % count) for i in range(count)])]
    all_to_all x3, starting transfers between devices: 12.9 us -> 16.6 us  [far(): return lax.all_to_all(values, AXES, split_axis=0, concat_axis=0, tiled=True)]
    transpose x4, local copies, waits for them, and re-layouts: 4.18 us -> 1.11 us  [packed(): return jnp.swapaxes(values, 1, 2).reshape(home_rows, rows, 2 * branches)]
    reshape x2, local copies, waits for them, and re-layouts: 2.67 us -> 0.59 us  [packed(): return jnp.swapaxes(values, 1, 2).reshape(home_rows, rows, 2 * branches)]
  transfers between devices with their start and end apart: 15 -> 12, of which waited for: 6 -> 7; matrix products, arithmetic and copies ran while one was open for 13% -> 4% of each run, Pallas kernels for 40% -> 38%
where the time goes in v2:
time: 132 us; the launch traced here: 130 us
  Pallas kernels  55.3 us (42%)
  waiting for transfers between devices  25.5 us (19%)
  starting transfers between devices  23.6 us (18%)
  blocking collectives  13.7 us (10%)
  local copies, waits for them, and re-layouts  8.77 us (7%)
  other arithmetic  3.21 us (2%)
    pallas_call x1, Pallas kernels, contract_rest(): pl.pallas_call(functools.partial(second_kernel, stride), grid_spec=pltpu....  30 us
    pallas_call x1, Pallas kernels, contract_first(): pl.pallas_call(first_kernel, grid_spec=pltpu.PrefetchScalarGridSpec(num_s...  19.8 us
    ppermute x3, waiting for transfers between devices, body(): lax.ppermute(row_vecs[d], 'row', [(i, (i - d) % row_count) for i in range...  16.9 us
    all_to_all x3, starting transfers between devices, far(): return lax.all_to_all(values, AXES, split_axis=0, concat_axis=0, tiled=True)  16.6 us
    all_to_all x1, blocking collectives, far(): return lax.all_to_all(values, AXES, split_axis=0, concat_axis=0, tiled=True)  13.7 us
    ppermute x6, starting transfers between devices, from_peers(): lax.ppermute(blocks[d], 'row', [(i, (i + d) % count) for i in range(count)])  5.26 us
    all_to_all x3, waiting for transfers between devices, far(): return lax.all_to_all(values, AXES, split_axis=0, concat_axis=0, tiled=True)  4.95 us
    ppermute x6, waiting for transfers between devices, from_peers(): lax.ppermute(blocks[d], 'row', [(i, (i + d) % count) for i in range(count)])  3.65 us
  transfers between devices with their start and end apart: 12, of which 7 were waited for; matrix products, arithmetic and copies ran while one was open for 4% of the time, Pallas kernels for 38%

profile of v2, /device:TPU:0, one launch (start us, length us, event | category | flops | bytes accessed | tf_op | source)
XLA Modules:
  0.0 130.5 jit_solution(3265408327452830666)
XLA Ops:
  0.0 0.8 copy.41
  0.9 0.1 fusion.2
  1.0 0.1 reshape.90
  1.1 0.2 convert_reduce_fusion.1
  1.4 0.2 convert_reduce_fusion
  1.7 0.5 fusion.7
  2.3 0.8 select_reduce_fusion
  3.1 7.3 %all-to-all-start = ((s32[32,1,128]{2,1,0:T(1,128)}), s32[32,1,128]{2,1,0:T(1,128)S(1)}, u32[]{:S(2)}, u32[]{:S(2)}) async-start(s32[32,1,128]{2,1,0:T(1,128)} %bitcast), calls=%async_computation | async-start | bytes 32768 | tf_op jit(solution)/shard_map/all_to_all | solution.py:340
  10.5 1.1 copy.46
  11.7 0.5 copy.48
  12.2 0.3 reshape.95.refs_4_
  12.6 4.9 %all-to-all-done = s32[32,1,128]{2,1,0:T(1,128)S(1)} async-done(((s32[32,1,128]{2,1,0:T(1,128)}), s32[32,1,128]{2,1,0:T(1,128)S(1)}, u32[]{:S(2)}, u32[]{:S(2)}) %all-to-all-start) | async-done | bytes 16416 | tf_op jit(solution)/shard_map/all_to_all | solution.py:340
  17.5 0.1 reshape.92.far_queries.queries
  17.7 0.6 gather_fusion
  18.3 1.8 %look_up.1 = (bf16[64,64,128]{2,1,0:T(8,128)(2,1)}, bf16[64,8,128]{2,1,0:T(8,128)(2,1)}, bf16[12,64,128]{2,1,0:T(8,128)(2,1)S(1)}, bf16[12,64,128]{2,1,0:T(8,128...) custom-call(s32[64]{0:T(128)S(1)} %reshape.92.far_queries.queries, ...), custom_call_target="tpu_custom_call" | custom-call | tf_op jit(solution)/shard_map/look_up/pallas_call | solution.py:57
  20.1 3.5 %all-to-all-start.2 = ((bf16[64,64,128]{2,1,0:T(8,128)(2,1)}), bf16[64,64,128]{2,1,0:T(8,128)(2,1)}, u32[]{:S(2)}, u32[]{:S(2)}) async-start(bf16[64,64,128]{2,1,0:T(8,128)(2,1)} %get-tuple-element.26), calls=%async_computation.2 | async-start | bytes 2097152 | tf_op jit(solution)/shard_map/all_to_all | solution.py:340
  23.7 0.2 copy.49
  24.0 0.5 copy.51
  24.5 0.3 reshape.98.refs_5_
  24.9 1.3 %collective-permute-start = (bf16[12,64,128]{2,1,0:T(8,128)(2,1)S(1)}, bf16[12,64,128]{2,1,0:T(8,128)(2,1)S(1)}, u32[]{:S(2)}, u32[]{:S(2)}) collective-permute-start(bf16[12,64,128]{2,1,0:T(8,128)(2,1)S(1)} %get-tuple-element.28), channel_id=1, source_target_pairs={{0,3},{1,0},{2,1},{3,2},{4,7},{5,4},{6,5},{7,6},{8,11},{9,8},{10,9... | collective-permute-start | bytes 589832 | tf_op jit(solution)/shard_map/ppermute | solution.py:362
  26.2 0.4 collective-permute-start.1
  26.5 0.1 collective-permute-start.2
  26.7 0.8 slice_reduce_fusion
  27.5 9.4 %collective-permute-done = bf16[12,64,128]{2,1,0:T(8,128)(2,1)S(1)} collective-permute-done((bf16[12,64,128]{2,1,0:T(8,128)(2,1)S(1)}, bf16[12,64,128]{2,1,0:T(8,128)(2,1)S(1)}, u32[]{:S(2)}, u32[]{:S(2)}) %collective-permute-start) | collective-permute-done | bytes 196640 | tf_op jit(solution)/shard_map/ppermute | solution.py:362
  37.0 7.5 %collective-permute-done.1 = bf16[12,64,128]{2,1,0:T(8,128)(2,1)S(1)} collective-permute-done((bf16[12,64,128]{2,1,0:T(8,128)(2,1)S(1)}, bf16[12,64,128]{2,1,0:T(8,128)(2,1)S(1)}, u32[]{:S(2)}, u32[]{:S(2)}) %collective-permute-start.1) | collective-permute-done | bytes 196640 | tf_op jit(solution)/shard_map/ppermute | solution.py:362
  44.4 1.0 pad_maximum_fusion.one_ref.two_ref
  45.4 19.8 %contract_first.1.refs_4_ = bf16[12,64,128,128]{3,2,1,0:T(8,128)(2,1)} custom-call(s32[24]{0:T(128)} %get-tuple-element.49.places.row_place, bf16[48,64,128]{2,1,0:T(8,128)(2,1)} %pad_maximum_fusion.one_ref.two_ref, bf16[48,64,128]{2,1,0:T(8,128)(2,1)} %pad_maximum_fusion.one_ref.two_ref, bf16[24,64,4096]{2,1,0:T(8,128)(2,1)} %cubic_ref.1), custom_call_target="tpu_custom_call" | custom-call | flops 1610612736 | bytes 37748736 | tf_op jit(solution)/shard_map/contract_first/pallas_call | solution.py:96
  65.3 5.8 %all-to-all-start.1 = ((bf16[64,8,128]{2,1,0:T(8,128)(2,1)}), bf16[64,8,128]{2,1,0:T(8,128)(2,1)S(1)}, u32[]{:S(2)}, u32[]{:S(2)}) async-start(bf16[64,8,128]{2,1,0:T(8,128)(2,1)} %get-tuple-element.25), calls=%async_computation.1 | async-start | bytes 262144 | tf_op jit(solution)/shard_map/all_to_all | solution.py:340
  71.0 30.0 %contract_rest.1.pair_ref = bf16[24,256,128]{2,1,0:T(8,128)(2,1)} custom-call(s32[24]{0:T(128)} %get-tuple-element.46.second_place, s32[24]{0:T(128)} %get-tuple-element.45.third_place, s32[24]{0:T(128)} %weights.1, bf16[64,64,128]{2,1,0:T(8,128)(2,1)} %all-to-all-done.2.refs_0_.refs_1_.refs_2_.refs_3_, ...), custom_call_target="tpu_custom_call" | custom-call | flops 12884901888 | bytes 25165824 | tf_op jit(solution)/shard_map/contract_rest/pallas_call | solution.py:190
  101.0 1.4 %copy-done = bf16[24,256,128]{2,1,0:T(8,128)(2,1)S(1)} copy-done((bf16[24,256,128]{2,1,0:T(8,128)(2,1)S(1)}, bf16[24,256,128]{2,1,0:T(8,128)(2,1)}, u32[]{:S(2)}) %copy-start) | copy-done | bytes 1572888
  102.4 0.9 coupling_terms.2
  103.3 0.3 collective-permute-start.3
  103.6 1.7 %collective-permute-start.4 = (bf16[12,8,128]{2,1,0:T(8,128)(2,1)S(1)}, bf16[12,8,128]{2,1,0:T(8,128)(2,1)S(1)}, u32[]{:S(2)}, u32[]{:S(2)}) collective-permute-start(bf16[12,8,128]{2,1,0:T(8,128)(2,1)S(1)} %get-tuple-element.34), channel_id=1, source_target_pairs={{0,2},{1,3},{2,0},{3,1},{4,6},{5,7},{6,4},{7,5},{8,10},{9,11},{10,... | collective-permute-start | bytes 73736 | tf_op jit(solution)/shard_map/ppermute | solution.py:36
  105.3 1.3 %collective-permute-start.5 = (bf16[12,8,128]{2,1,0:T(8,128)(2,1)S(1)}, bf16[12,8,128]{2,1,0:T(8,128)(2,1)S(1)}, u32[]{:S(2)}, u32[]{:S(2)}) collective-permute-start(bf16[12,8,128]{2,1,0:T(8,128)(2,1)S(1)} %get-tuple-element.35), channel_id=1, source_target_pairs={{0,3},{1,0},{2,1},{3,2},{4,7},{5,4},{6,5},{7,6},{8,11},{9,8},{10,9... | collective-permute-start | bytes 73736 | tf_op jit(solution)/shard_map/ppermute | solution.py:36
  106.6 0.8 collective-permute-done.4.refs_2_
  107.4 0.7 collective-permute-done.5.refs_3_
  108.2 1.0 update.2
  109.2 13.7 %all_to_all.20.table_ref = bf16[64,8,128]{2,1,0:T(8,128)(2,1)S(1)} all-to-all(bf16[64,8,128]{2,1,0:T(8,128)(2,1)S(1)} %get-tuple-element.38), channel_id=1, replica_groups=mesh['trip'=8,'row'=4] {'trip','row'}, dimensions={0} | all-to-all | bytes 262144 | tf_op jit(solution)/shard_map/all_to_all | solution.py:340
  122.9 0.9 coupling_terms.3
  123.8 0.3 collective-permute-start.6
  124.1 0.3 collective-permute-start.7
  124.4 1.3 %collective-permute-start.8 = (bf16[12,8,128]{2,1,0:T(8,128)(2,1)S(1)}, bf16[12,8,128]{2,1,0:T(8,128)(2,1)S(1)}, u32[]{:S(2)}, u32[]{:S(2)}) collective-permute-start(bf16[12,8,128]{2,1,0:T(8,128)(2,1)S(1)} %get-tuple-element.42), channel_id=1, source_target_pairs={{0,3},{1,0},{2,1},{3,2},{4,7},{5,4},{6,5},{7,6},{8,11},{9,8},{10,9... | collective-permute-start | bytes 73736 | tf_op jit(solution)/shard_map/ppermute | solution.py:36
  125.8 1.3 %collective-permute-done.6.refs_1_ = bf16[12,8,128]{2,1,0:T(8,128)(2,1)S(1)} collective-permute-done((bf16[12,8,128]{2,1,0:T(8,128)(2,1)S(1)}, bf16[12,8,128]{2,1,0:T(8,128)(2,1)S(1)}, u32[]{:S(2)}, u32[]{:S(2)}) %collective-permute-start.6) | collective-permute-done | bytes 24608 | tf_op jit(solution)/shard_map/ppermute | solution.py:36
  127.1 0.8 collective-permute-done.7.refs_2_
  127.9 0.9 update.3
  128.8 0.3 reshape.99
  129.2 0.4 copy.53
  129.7 0.8 copy.54
  (45 shorter events, 1.1 us)
Async XLA Ops:
  3.1 14.4 %all-to-all-start = ((s32[32,1,128]{2,1,0:T(1,128)}), s32[32,1,128]{2,1,0:T(1,128)S(1)}, u32[]{:S(2)}, u32[]{:S(2)}) async-start(s32[32,1,128]{2,1,0:T(1,128)} %bitcast), calls=%async_computation | async-start | bytes 32768 | tf_op jit(solution)/shard_map/all_to_all | solution.py:340
  11.7 6.6 %copy-start.2 = (bf16[64,64,128]{2,1,0:T(8,128)(2,1)S(1)}, bf16[64,64,128]{2,1,0:T(8,128)(2,1)}, u32[]{:S(2)}) copy-start(bf16[64,64,128]{2,1,0:T(8,128)(2,1)} %vec_ref.1) | copy-start | bytes 3145732
  20.1 3.6 %copy-start.6 = (f32[64,768]{1,0:T(8,128)S(1)}, f32[64,768]{1,0:T(8,128)}, u32[]{:S(2)}) copy-start(f32[64,768]{1,0:T(8,128)} %param.12) | copy-start | bytes 589828
  20.1 45.2 %all-to-all-start.2 = ((bf16[64,64,128]{2,1,0:T(8,128)(2,1)}), bf16[64,64,128]{2,1,0:T(8,128)(2,1)}, u32[]{:S(2)}, u32[]{:S(2)}) async-start(bf16[64,64,128]{2,1,0:T(8,128)(2,1)} %get-tuple-element.26), calls=%async_computation.2 | async-start | bytes 2097152 | tf_op jit(solution)/shard_map/all_to_all | solution.py:340
  23.9 3.5 %copy-start.7 = (f32[64,64]{1,0:T(8,128)S(1)}, f32[64,64]{1,0:T(8,128)}, u32[]{:S(2)}) copy-start(f32[64,64]{1,0:T(8,128)} %param.13) | copy-start | bytes 49156
  24.9 12.1 %collective-permute-start = (bf16[12,64,128]{2,1,0:T(8,128)(2,1)S(1)}, bf16[12,64,128]{2,1,0:T(8,128)(2,1)S(1)}, u32[]{:S(2)}, u32[]{:S(2)}) collective-permute-start(bf16[12,64,128]{2,1,0:T(8,128)(2,1)S(1)} %get-tuple-element.28), channel_id=1, source_target_pairs={{0,3},{1,0},{2,1},{3,2},{4,7},{5,4},{6,5},{7,6},{8,11},{9,8},{10,9... | collective-permute-start | bytes 589832 | tf_op jit(solution)/shard_map/ppermute | solution.py:362
  26.2 18.3 %collective-permute-start.1 = (bf16[12,64,128]{2,1,0:T(8,128)(2,1)S(1)}, bf16[12,64,128]{2,1,0:T(8,128)(2,1)S(1)}, u32[]{:S(2)}, u32[]{:S(2)}) collective-permute-start(bf16[12,64,128]{2,1,0:T(8,128)(2,1)S(1)} %get-tuple-element.29), channel_id=1, source_target_pairs={{0,2},{1,3},{2,0},{3,1},{4,6},{5,7},{6,4},{7,5},{8,10},{9,11},{10,... | collective-permute-start | bytes 589832 | tf_op jit(solution)/shard_map/ppermute | solution.py:362
  26.5 17.9 %collective-permute-start.2 = (bf16[12,64,128]{2,1,0:T(8,128)(2,1)S(1)}, bf16[12,64,128]{2,1,0:T(8,128)(2,1)S(1)}, u32[]{:S(2)}, u32[]{:S(2)}) collective-permute-start(bf16[12,64,128]{2,1,0:T(8,128)(2,1)S(1)} %get-tuple-element.30), channel_id=1, source_target_pairs={{0,1},{1,2},{2,3},{3,0},{4,5},{5,6},{6,7},{7,4},{8,9},{9,10},{10,1... | collective-permute-start | bytes 589832 | tf_op jit(solution)/shard_map/ppermute | solution.py:362
  65.3 35.7 %all-to-all-start.1 = ((bf16[64,8,128]{2,1,0:T(8,128)(2,1)}), bf16[64,8,128]{2,1,0:T(8,128)(2,1)S(1)}, u32[]{:S(2)}, u32[]{:S(2)}) async-start(bf16[64,8,128]{2,1,0:T(8,128)(2,1)} %get-tuple-element.25), calls=%async_computation.1 | async-start | bytes 262144 | tf_op jit(solution)/shard_map/all_to_all | solution.py:340
  71.0 30.0 %copy-start.3 = (s32[24]{0:T(128)S(1)}, s32[24]{0:T(128)}, u32[]{:S(2)}) copy-start(s32[24]{0:T(128)} %get-tuple-element.49.places.row_place) | copy-start | bytes 292
  71.0 30.0 %copy-start.4 = (s32[24]{0:T(128)S(1)}, s32[24]{0:T(128)}, u32[]{:S(2)}) copy-start(s32[24]{0:T(128)} %get-tuple-element.45.third_place) | copy-start | bytes 292
  71.0 30.0 %copy-start.5 = (s32[24]{0:T(128)S(1)}, s32[24]{0:T(128)}, u32[]{:S(2)}) copy-start(s32[24]{0:T(128)} %get-tuple-element.46.second_place) | copy-start | bytes 292
  101.0 1.4 %copy-start = (bf16[24,256,128]{2,1,0:T(8,128)(2,1)S(1)}, bf16[24,256,128]{2,1,0:T(8,128)(2,1)}, u32[]{:S(2)}) copy-start(bf16[24,256,128]{2,1,0:T(8,128)(2,1)} %contract_rest.1.pair_ref) | copy-start | bytes 4718596
  102.4 20.5 %copy-start.1 = (bf16[24,256,128]{2,1,0:T(8,128)(2,1)S(1)}, bf16[24,256,128]{2,1,0:T(8,128)(2,1)}, u32[]{:S(2)}) copy-start(bf16[24,256,128]{2,1,0:T(8,128)(2,1)} %contract_rest.1.pair_ref) | copy-start | bytes 4718596
  103.3 3.3 %collective-permute-start.3 = (bf16[12,8,128]{2,1,0:T(8,128)(2,1)S(1)}, bf16[12,8,128]{2,1,0:T(8,128)(2,1)S(1)}, u32[]{:S(2)}, u32[]{:S(2)}) collective-permute-start(bf16[12,8,128]{2,1,0:T(8,128)(2,1)S(1)} %get-tuple-element.33), channel_id=1, source_target_pairs={{0,1},{1,2},{2,3},{3,0},{4,5},{5,6},{6,7},{7,4},{8,9},{9,10},{10,1... | collective-permute-start | bytes 73736 | tf_op jit(solution)/shard_map/ppermute | solution.py:36
  103.6 3.8 %collective-permute-start.4 = (bf16[12,8,128]{2,1,0:T(8,128)(2,1)S(1)}, bf16[12,8,128]{2,1,0:T(8,128)(2,1)S(1)}, u32[]{:S(2)}, u32[]{:S(2)}) collective-permute-start(bf16[12,8,128]{2,1,0:T(8,128)(2,1)S(1)} %get-tuple-element.34), channel_id=1, source_target_pairs={{0,2},{1,3},{2,0},{3,1},{4,6},{5,7},{6,4},{7,5},{8,10},{9,11},{10,... | collective-permute-start | bytes 73736 | tf_op jit(solution)/shard_map/ppermute | solution.py:36
  105.3 2.9 %collective-permute-start.5 = (bf16[12,8,128]{2,1,0:T(8,128)(2,1)S(1)}, bf16[12,8,128]{2,1,0:T(8,128)(2,1)S(1)}, u32[]{:S(2)}, u32[]{:S(2)}) collective-permute-start(bf16[12,8,128]{2,1,0:T(8,128)(2,1)S(1)} %get-tuple-element.35), channel_id=1, source_target_pairs={{0,3},{1,0},{2,1},{3,2},{4,7},{5,4},{6,5},{7,6},{8,11},{9,8},{10,9... | collective-permute-start | bytes 73736 | tf_op jit(solution)/shard_map/ppermute | solution.py:36
  123.8 3.3 %collective-permute-start.6 = (bf16[12,8,128]{2,1,0:T(8,128)(2,1)S(1)}, bf16[12,8,128]{2,1,0:T(8,128)(2,1)S(1)}, u32[]{:S(2)}, u32[]{:S(2)}) collective-permute-start(bf16[12,8,128]{2,1,0:T(8,128)(2,1)S(1)} %get-tuple-element.40), channel_id=1, source_target_pairs={{0,1},{1,2},{2,3},{3,0},{4,5},{5,6},{6,7},{7,4},{8,9},{9,10},{10,1... | collective-permute-start | bytes 73736 | tf_op jit(solution)/shard_map/ppermute | solution.py:36
  124.1 3.8 %collective-permute-start.7 = (bf16[12,8,128]{2,1,0:T(8,128)(2,1)S(1)}, bf16[12,8,128]{2,1,0:T(8,128)(2,1)S(1)}, u32[]{:S(2)}, u32[]{:S(2)}) collective-permute-start(bf16[12,8,128]{2,1,0:T(8,128)(2,1)S(1)} %get-tuple-element.41), channel_id=1, source_target_pairs={{0,2},{1,3},{2,0},{3,1},{4,6},{5,7},{6,4},{7,5},{8,10},{9,11},{10,... | collective-permute-start | bytes 73736 | tf_op jit(solution)/shard_map/ppermute | solution.py:36
  124.4 3.5 %collective-permute-start.8 = (bf16[12,8,128]{2,1,0:T(8,128)(2,1)S(1)}, bf16[12,8,128]{2,1,0:T(8,128)(2,1)S(1)}, u32[]{:S(2)}, u32[]{:S(2)}) collective-permute-start(bf16[12,8,128]{2,1,0:T(8,128)(2,1)S(1)} %get-tuple-element.42), channel_id=1, source_target_pairs={{0,3},{1,0},{2,1},{3,2},{4,7},{5,4},{6,5},{7,6},{8,11},{9,8},{10,9... | collective-permute-start | bytes 73736 | tf_op jit(solution)/shard_map/ppermute | solution.py:36

commit v3 on v2

--- a/solution.py
+++ b/solution.py
@@ -38,32 +38,26 @@
     ]
 
 
-def lookup_kernel(far_queries, row_queries, vec_ref, state_ref, far_ref, far_state_ref, *row_refs):
-    for slot in range(far_queries.shape[0]):
-        far_ref[slot] = vec_ref[far_queries[slot]]
-        far_state_ref[slot] = state_ref[far_queries[slot]]
-    for d, row_ref in enumerate(row_refs):
-        for slot in range(row_ref.shape[0]):
-            row_ref[slot] = vec_ref[row_queries[d, slot]]
-
-
-def look_up(far_queries, row_queries, eigvecs, state):
-    row_count, row_cap = row_queries.shape
-    far_slots = far_queries.shape[0]
-    outs = [
-        jax.ShapeDtypeStruct((far_slots,) + eigvecs.shape[1:], eigvecs.dtype),
-        jax.ShapeDtypeStruct((far_slots,) + state.shape[1:], state.dtype),
-    ] + [jax.ShapeDtypeStruct((row_cap,) + eigvecs.shape[1:], eigvecs.dtype)] * row_count
-    found = pl.pallas_call(
+def lookup_kernel(queries, table_ref, *found_refs):
+    cap = found_refs[0].shape[0]
+    for d, found_ref in enumerate(found_refs):
+        for slot in range(cap):
+            found_ref[slot] = table_ref[queries[d * cap + slot]]
+
+
+def look_up(queries, table, parts):
+    cap = queries.shape[0] // parts
+    return pl.pallas_call(
         lookup_kernel,
-        in_specs=[pl.BlockSpec(memory_space=pltpu.SMEM)] * 2
-        + [pl.BlockSpec(memory_space=pltpu.VMEM)] * 2,
-        out_specs=[pl.BlockSpec(memory_space=pltpu.VMEM)] * len(outs),
-        out_shape=outs,
+        in_specs=[
+            pl.BlockSpec(memory_space=pltpu.SMEM),
+            pl.BlockSpec(memory_space=pltpu.VMEM),
+        ],
+        out_specs=[pl.BlockSpec(memory_space=pltpu.VMEM)] * parts,
+        out_shape=[jax.ShapeDtypeStruct((cap,) + table.shape[1:], table.dtype)] * parts,
         compiler_params=pltpu.CompilerParams(vmem_limit_bytes=16 * MIB),
         name="look_up",
-    )(far_queries, row_queries, eigvecs, state)
-    return found[0], found[1], found[2:]
+    )(queries, table)
 
 
 def first_kernel(places, one_ref, two_ref, cubic_ref, out_ref):
@@ -116,12 +110,10 @@
     )(places, table, table, cubic)
 
 
-def second_kernel(
-    stride, second_place, third_place, weights, *refs
-):
-    second_refs, third_refs = refs[:2], refs[2:4]
-    first_ref, pair_ref, turned = refs[4:]
-    branches = second_refs[0].shape[1]
+def second_kernel(stride, group, second_place, third_place, weights, *refs):
+    second_refs, third_refs = refs[: 2 * group], refs[2 * group : 4 * group]
+    first_ref, pair_ref, *scratch = refs[4 * group :]
+    branches = first_ref.shape[1]
     both = 2 * branches
 
     def mixer(vec_refs):
@@ -138,11 +130,11 @@
     def apart(block):
         return jnp.concatenate([jnp.where(left, block, none), jnp.where(left, none, block)], 0)
 
-    second_mixer, third_mixer = mixer(second_refs), mixer(third_refs)
-    for j in range(0, branches, 2):
+    def over_k(pair, third_mixer, j):
+        turned = scratch[pair % 2]
         mixed = jnp.dot(
             third_mixer,
-            jnp.concatenate([apart(first_ref[0, j]), apart(first_ref[0, j + 1])], 1),
+            jnp.concatenate([apart(first_ref[pair, j]), apart(first_ref[pair, j + 1])], 1),
             preferred_element_type=F32,
         )
         for half in range(2):
@@ -150,8 +142,9 @@
                 turned[pl.ds(part * branches + j + half, branches, stride=stride), :] = mixed[
                     part * branches : (part + 1) * branches, half * both : (half + 1) * both
                 ]
-    total = jnp.zeros((branches, both), F32)
-    for c in range(0, branches, 2):
+
+    def over_j(pair, second_mixer, c, total):
+        turned = scratch[pair % 2]
         columns = [
             apart(turned[(c + half) * stride : (c + half) * stride + both, :].astype(BF16))
             for half in range(2)
@@ -164,48 +157,69 @@
             lanes = slice(half * both, (half + 1) * both)
             total = total + power[:, lanes]
             turned[pl.ds(c + half, 1), :] = over_b[:, lanes]
-    step = pl.program_id(0)
-    left = left[:branches]
-    weight = jnp.where(left, weights[2 * step].astype(F32), weights[2 * step + 1].astype(F32))
-    for part, parted in enumerate((total, turned[:branches, :])):
-        own = parted * weight
-        other = pltpu.roll(own, branches, 1)
-        for t, (upper, lower) in enumerate(((own, other), (other, own))):
+        return total
+
+    def finish(pair, total):
+        first = 2 * (group * pl.program_id(0) + pair)
+        near = left[:branches]
+        weight = jnp.where(near, weights[first].astype(F32), weights[first + 1].astype(F32))
+        for part, parted in enumerate((total, scratch[pair % 2][:branches, :])):
+            own = parted * weight
+            other = pltpu.roll(own, branches, 1)
             start = part * both
-            pair_ref[t, start : start + branches, :] = jnp.where(left, upper, 0.0).astype(BF16)
-            pair_ref[t, start + branches : start + both, :] = jnp.where(left, 0.0, lower).astype(
-                BF16
-            )
+            for t, (upper, lower) in enumerate(((own, other), (other, own))):
+                pair_ref[2 * pair + t, start : start + branches, :] = jnp.where(
+                    near, upper, 0.0
+                ).astype(BF16)
+                pair_ref[2 * pair + t, start + branches : start + both, :] = jnp.where(
+                    near, 0.0, lower
+                ).astype(BF16)
+
+    for phase in range(group + 1):
+        before = phase - 1
+        if phase < group:
+            third_mixer = mixer(third_refs[2 * phase : 2 * phase + 2])
+        if phase > 0:
+            second_mixer = mixer(second_refs[2 * before : 2 * before + 2])
+            total = jnp.zeros((branches, both), F32)
+        for at in range(0, branches, 2):
+            if phase > 0:
+                total = over_j(before, second_mixer, at, total)
+            if phase < group:
+                over_k(phase, third_mixer, at)
+        if phase > 0:
+            finish(before, total)
 
 
 def contract_rest(second_place, third_place, weights, table, first):
-    steps, branches, both = first.shape[:3]
-    stride = both + 8
+    pairs, branches, both = first.shape[:3]
+    group = 2 if pairs % 2 == 0 else 1
+    stride = both + 9
 
     def vectors(which, t):
         return pl.BlockSpec(
-            (1, branches, both), lambda s, *places: (places[which][2 * s + t], 0, 0)
+            (1, branches, both), lambda s, *places: (places[which][2 * group * s + t], 0, 0)
         )
 
     return pl.pallas_call(
-        functools.partial(second_kernel, stride),
+        functools.partial(second_kernel, stride, group),
         grid_spec=pltpu.PrefetchScalarGridSpec(
             num_scalar_prefetch=3,
-            grid=(steps,),
-            in_specs=[vectors(0, 0), vectors(0, 1), vectors(1, 0), vectors(1, 1)]
-            + [pl.BlockSpec((1, branches, both, both), lambda s, *places: (s, 0, 0, 0))],
-            out_specs=pl.BlockSpec((2, 2 * both, both), lambda s, *places: (s, 0, 0)),
-            scratch_shapes=[pltpu.VMEM((branches * stride, both), F32)],
+            grid=(pairs // group,),
+            in_specs=[vectors(which, t) for which in range(2) for t in range(2 * group)]
+            + [pl.BlockSpec((group, branches, both, both), lambda s, *places: (s, 0, 0, 0))],
+            out_specs=pl.BlockSpec((2 * group, 2 * both, both), lambda s, *places: (s, 0, 0)),
+            scratch_shapes=[pltpu.VMEM((branches * stride, both), F32)] * 2,
         ),
-        out_shape=jax.ShapeDtypeStruct((2 * steps, 2 * both, both), BF16),
-        compiler_params=pltpu.CompilerParams(vmem_limit_bytes=60 * MIB),
+        out_shape=jax.ShapeDtypeStruct((2 * pairs, 2 * both, both), BF16),
+        compiler_params=pltpu.CompilerParams(vmem_limit_bytes=32 * MIB),
         cost_estimate=pl.CostEstimate(
-            flops=16 * steps * both * both * branches * branches,
-            bytes_accessed=2 * steps * both * both * branches,
+            flops=16 * pairs * both * both * branches * branches,
+            bytes_accessed=2 * pairs * both * both * branches,
             transcendentals=0,
         ),
         name="contract_rest",
-    )(second_place, third_place, weights, table, table, table, table, first)
+    )(second_place, third_place, weights, *[table] * (4 * group), first)
 
 
 def terms_kernel(
@@ -321,41 +335,27 @@
         values = values.reshape(home_rows, 2 * rows, branches)[:, :columns]
         return jnp.swapaxes(values, 1, 2).reshape(home_rows, branches * columns)
 
-    me = lax.axis_index("trip") * row_count + lax.axis_index("row")
-    owner = triplets // home_rows
-    local = triplets - owner * home_rows
-    first_dev, far_owner = owner[:, 0], owner[:, 1:].reshape(-1)
-    ahead = (first_dev - me) % row_count
-    row_rank = ranks_of(first_dev)
+    first_dev = triplets[:, 0] // home_rows
+    first_local = triplets[:, 0] - first_dev * home_rows
+    ahead = (first_dev - lax.axis_index("row")) % row_count
+    row_place = ahead * row_cap + ranks_of(ahead)
+    row_codes = pack_ints(row_place, first_local + 1, row_slots).reshape(row_count, row_cap)
+
+    far_index = triplets[:, 1:].reshape(-1)
+    far_owner = far_index // home_rows
     far_rank = ranks_of(far_owner)
-    row_place = ahead * row_cap + row_rank
     far_place = far_owner * far_cap + far_rank
     message = pack_ints(
-        jnp.concatenate([far_owner * LANES + far_rank, first_dev * LANES + far_cap + row_rank]),
-        jnp.concatenate([local[:, 1:].reshape(-1), local[:, 0] + 1]),
-        devices * LANES,
+        far_owner * LANES + far_rank, far_index - far_owner * home_rows, devices * LANES
     ).reshape(devices, 1, LANES)
 
     def far(values):
         return lax.all_to_all(values, AXES, split_axis=0, concat_axis=0, tiled=True)
 
-    heard = far(message)[:, 0]
-    queries = heard[:, :far_cap].reshape(-1)
+    queries = far(message)[:, 0, :far_cap].reshape(-1)
     second_place, third_place = far_place.reshape(trip_local, 2).T
-    group = lax.dynamic_slice(
-        heard, (lax.axis_index("trip") * row_count, far_cap), (row_count, row_cap)
-    )
-    codes = jnp.take(
-        group, (lax.axis_index("row") - jnp.arange(row_count)) % row_count, axis=0, mode="clip"
-    )
-
-    state = packed(deviation)
-    one = lax.broadcasted_iota(jnp.int32, state.shape[1:], 0) + rows * (
-        lax.broadcasted_iota(jnp.int32, state.shape[1:], 1) // branches
-    )
-    sent_state = jnp.where(one == columns, 1.0, state).astype(BF16)
-    far_vecs, far_state, row_vecs = look_up(queries, jnp.maximum(codes - 1, 0), eigvecs, sent_state)
-    far_table = far(far_vecs)
+    codes = jnp.stack(from_peers([row_codes[d] for d in range(row_count)]))
+    row_vecs = look_up(jnp.maximum(codes - 1, 0).reshape(-1), eigvecs, row_count)
     first_table = jnp.concatenate(
         [row_vecs[0]]
         + [
@@ -364,11 +364,20 @@
         ],
         0,
     )
+
+    state = packed(deviation)
+    one = lax.broadcasted_iota(jnp.int32, state.shape[1:], 0) + rows * (
+        lax.broadcasted_iota(jnp.int32, state.shape[1:], 1) // branches
+    )
+    sent_state = jnp.where(one == columns, 1.0, state).astype(BF16)
+    records = jnp.concatenate([eigvecs, sent_state], 1)
+    queries, row_vecs = lax.optimization_barrier((queries, row_vecs))
+    far_table = far(look_up(queries, records, 1)[0])
     driven = packed(source)
     rate = jnp.concatenate([base_rate, base_rate], 1)[:, None, :]
     first_table, driven, rate = lax.optimization_barrier((first_table, driven, rate))
     first_part = contract_first(row_place, first_table, cubic)
-    arrived_state = far(far_state)
+    arrived_state = far_table[:, branches:]
     pairs = contract_rest(second_place, third_place, weights, far_table, first_part)
 
     for step in range(ITERS):

time: 132 us -> 120 us (0.909)
  Pallas kernels: 55.3 us -> 46.1 us
  starting transfers between devices: 23.6 us -> 18.3 us
  other arithmetic: 3.21 us -> 6.8 us
    pallas_call x1, Pallas kernels: 30 us -> 20.3 us  [contract_rest(): pl.pallas_call(functools.partial(second_kernel, stride, group), grid_spec...]
    all_to_all x3 -> x2, starting transfers between devices: 16.6 us -> 8.05 us  [far(): return lax.all_to_all(values, AXES, split_axis=0, concat_axis=0, tiled=True)]
    ppermute x6 -> x9, starting transfers between devices: 5.26 us -> 8.19 us  [from_peers(): lax.ppermute(blocks[d], 'row', [(i, (i + d) % count) for i in range(count)])]
    all_to_all x3 -> x2, waiting for transfers between devices: 4.95 us -> 2.77 us  [far(): return lax.all_to_all(values, AXES, split_axis=0, concat_axis=0, tiled=True)]
    slice x2 -> x4, local copies, waits for them, and re-layouts: 0.15 us -> 2.12 us  [the longest x1 0.76 us: body(): queries = far(message)[:, 0, :far_cap].reshape(-1)]
    ppermute x6 -> x9, waiting for transfers between devices: 3.65 us -> 5.06 us  [from_peers(): lax.ppermute(blocks[d], 'row', [(i, (i + d) % count) for i in range(count)])]
    unnamed x19 -> x21, local copies, waits for them, and re-layouts: 3.45 us -> 2.38 us
  transfers between devices with their start and end apart: 12 -> 14, of which waited for: 7 -> 7; matrix products, arithmetic and copies ran while one was open for 4% -> 8% of each run, Pallas kernels for 38% -> 17%
where the time goes in v3:
time: 120 us; the launch traced here: 119 us
  Pallas kernels  46.1 us (38%)
  waiting for transfers between devices  24.5 us (20%)
  starting transfers between devices  18.3 us (15%)
  blocking collectives  13.5 us (11%)
  local copies, waits for them, and re-layouts  9.05 us (8%)
  other arithmetic  6.8 us (6%)
    pallas_call x1, Pallas kernels, contract_rest(): pl.pallas_call(functools.partial(second_kernel, stride, group), grid_spec...  20.3 us
    pallas_call x1, Pallas kernels, contract_first(): pl.pallas_call(first_kernel, grid_spec=pltpu.PrefetchScalarGridSpec(num_s...  20 us
    ppermute x3, waiting for transfers between devices, body(): lax.ppermute(row_vecs[d], 'row', [(i, (i - d) % row_count) for i in range...  16.6 us
    all_to_all x1, blocking collectives, far(): return lax.all_to_all(values, AXES, split_axis=0, concat_axis=0, tiled=True)  13.5 us
    ppermute x9, starting transfers between devices, from_peers(): lax.ppermute(blocks[d], 'row', [(i, (i + d) % count) for i in range(count)])  8.19 us
    all_to_all x2, starting transfers between devices, far(): return lax.all_to_all(values, AXES, split_axis=0, concat_axis=0, tiled=True)  8.05 us
    ppermute x9, waiting for transfers between devices, from_peers(): lax.ppermute(blocks[d], 'row', [(i, (i + d) % count) for i in range(count)])  5.06 us
    all_to_all x2, waiting for transfers between devices, far(): return lax.all_to_all(values, AXES, split_axis=0, concat_axis=0, tiled=True)  2.77 us
  transfers between devices with their start and end apart: 14, of which 7 were waited for; matrix products, arithmetic and copies ran while one was open for 8% of the time, Pallas kernels for 17%

profile of v3, /device:TPU:0, one launch (start us, length us, event | category | flops | bytes accessed | tf_op | source)
XLA Modules:
  0.0 118.6 jit_solution(13553095639009456498)
XLA Ops:
  0.0 0.7 and_select_fusion.3
  0.7 0.7 fusion.7
  1.6 0.7 fusion.10
  2.4 0.7 slice_bitcast_fusion.1
  3.0 0.5 collective-permute-start
  3.5 2.5 %collective-permute-start.1 = (s32[12]{0:T(128)}, s32[12]{0:T(128)}, u32[]{:S(2)}, u32[]{:S(2)}) collective-permute-start(s32[12]{0:T(128)} %get-tuple-element.53), channel_id=1, source_target_pairs={{0,2},{1,3},{2,0},{3,1},{4,6},{5,7},{6,4},{7,5},{8,10},{9,11},{10,... | collective-permute-start | bytes 152 | tf_op jit(solution)/shard_map/ppermute | solution.py:36
  6.0 1.4 %collective-permute-start.2 = (s32[12]{0:T(128)}, s32[12]{0:T(128)}, u32[]{:S(2)}, u32[]{:S(2)}) collective-permute-start(s32[12]{0:T(128)} %get-tuple-element.52), channel_id=1, source_target_pairs={{0,3},{1,0},{2,1},{3,2},{4,7},{5,4},{6,5},{7,6},{8,11},{9,8},{10,9... | collective-permute-start | bytes 152 | tf_op jit(solution)/shard_map/ppermute | solution.py:36
  7.4 0.7 slice.40
  8.5 0.5 copy-done.7
  9.1 0.8 select_reduce_fusion
  9.8 5.1 %all-to-all-start = ((s32[32,1,128]{2,1,0:T(1,128)}), s32[32,1,128]{2,1,0:T(1,128)}, u32[]{:S(2)}, u32[]{:S(2)}) async-start(s32[32,1,128]{2,1,0:T(1,128)} %bitcast.6), calls=%async_computation | async-start | bytes 32768 | tf_op jit(solution)/shard_map/all_to_all | solution.py:353
  14.9 1.1 copy.30
  16.1 0.5 copy.32
  16.7 0.3 reshape.204.refs_4_
  17.7 0.7 add_maximum_fusion
  18.4 0.6 look_up.2
  19.0 2.8 %all-to-all-done = s32[32,1,128]{2,1,0:T(1,128)} async-done(((s32[32,1,128]{2,1,0:T(1,128)}), s32[32,1,128]{2,1,0:T(1,128)}, u32[]{:S(2)}, u32[]{:S(2)}) %all-to-all-start) | async-done | bytes 16416 | tf_op jit(solution)/shard_map/all_to_all | solution.py:353
  21.8 0.8 slice_reduce_fusion
  22.7 1.7 %look_up.3 = bf16[64,72,128]{2,1,0:T(8,128)(2,1)} custom-call(s32[64]{0:T(128)S(1)} %reshape_squeeze.3.queries, bf16[64,72,128]{2,1,0:T(8,128)(2,1)S(1)} %pad_maximum_fusion.table_ref), custom_call_target="tpu_custom_call" | custom-call | tf_op jit(solution)/shard_map/look_up/pallas_call | solution.py:50
  24.4 3.0 %all-to-all-start.1 = ((bf16[64,72,128]{2,1,0:T(8,128)(2,1)}), bf16[64,72,128]{2,1,0:T(8,128)(2,1)S(1)}, u32[]{:S(2)}, u32[]{:S(2)}) async-start(bf16[64,72,128]{2,1,0:T(8,128)(2,1)} %look_up.3), calls=%async_computation.1 | async-start | bytes 2359296 | tf_op jit(solution)/shard_map/all_to_all | solution.py:353
  27.4 0.7 reduce_sum.42
  28.4 0.5 copy.35
  28.9 0.3 reshape.207.refs_5_
  29.2 0.7 fusion.4
  29.9 1.6 %collective-permute-start.3 = (bf16[12,64,128]{2,1,0:T(8,128)(2,1)S(1)}, bf16[12,64,128]{2,1,0:T(8,128)(2,1)S(1)}, u32[]{:S(2)}, u32[]{:S(2)}) collective-permute-start(bf16[12,64,128]{2,1,0:T(8,128)(2,1)S(1)} %get-tuple-element.25), channel_id=1, source_target_pairs={{0,3},{1,0},{2,1},{3,2},{4,7},{5,4},{6,5},{7,6},{8,11},{9,8},{10,9... | collective-permute-start | bytes 589832 | tf_op jit(solution)/shard_map/ppermute | solution.py:362
  31.5 0.4 collective-permute-start.4
  32.2 0.9 pad_maximum_fusion.2
  33.1 9.1 %collective-permute-done.3 = bf16[12,64,128]{2,1,0:T(8,128)(2,1)S(1)} collective-permute-done((bf16[12,64,128]{2,1,0:T(8,128)(2,1)S(1)}, bf16[12,64,128]{2,1,0:T(8,128)(2,1)S(1)}, u32[]{:S(2)}, u32[]{:S(2)}) %collective-permute-start.3) | collective-permute-done | bytes 196640 | tf_op jit(solution)/shard_map/ppermute | solution.py:362
  42.3 7.5 %collective-permute-done.4 = bf16[12,64,128]{2,1,0:T(8,128)(2,1)S(1)} collective-permute-done((bf16[12,64,128]{2,1,0:T(8,128)(2,1)S(1)}, bf16[12,64,128]{2,1,0:T(8,128)(2,1)S(1)}, u32[]{:S(2)}, u32[]{:S(2)}) %collective-permute-start.4) | collective-permute-done | bytes 196640 | tf_op jit(solution)/shard_map/ppermute | solution.py:362
  49.8 1.0 pad_maximum_fusion.1.one_ref.two_ref
  50.7 20.0 %contract_first.1.refs_8_ = bf16[12,64,128,128]{3,2,1,0:T(8,128)(2,1)} custom-call(s32[24]{0:T(128)} %copy-done.1, bf16[48,64,128]{2,1,0:T(8,128)(2,1)} %pad_maximum_fusion.1.one_ref.two_ref, bf16[48,64,128]{2,1,0:T(8,128)(2,1)} %pad_maximum_fusion.1.one_ref.two_ref, bf16[24,64,4096]{2,1,0:T(8,128)(2,1)} %cubic_ref.1), custom_call_target="tpu_custom_call" | custom-call | flops 1610612736 | bytes 37748736 | tf_op jit(solution)/shard_map/contract_first/pallas_call | solution.py:90
  70.7 20.3 %contract_rest.1.pair_ref = bf16[24,256,128]{2,1,0:T(8,128)(2,1)S(1)} custom-call(s32[24]{0:T(128)S(1)} %get-tuple-element.44.second_place, s32[24]{0:T(128)S(1)} %get-tuple-element.43.third_place, s32[24]{0:T(128)S(1)} %copy-done.3, bf16[64,72,128]{2,1,0:T(8,128)(2,1)S(1)} %all-to-all-done.1.refs_0_.refs_1_.refs_2_.refs_3_.refs_4_.refs_5_.refs_6_.refs_7_, ...), custom_call_target="tpu_custom_call" | custom-call | flops 12884901888 | bytes 25165824 | tf_op jit(solution)/shard_map/contract_rest/pallas_call | solution.py:204
  91.0 0.9 coupling_terms.2
  92.0 0.7 collective-permute-start.7
  92.7 1.4 %collective-permute-start.8 = (bf16[12,8,128]{2,1,0:T(8,128)(2,1)S(1)}, bf16[12,8,128]{2,1,0:T(8,128)(2,1)S(1)}, u32[]{:S(2)}, u32[]{:S(2)}) collective-permute-start(bf16[12,8,128]{2,1,0:T(8,128)(2,1)S(1)} %get-tuple-element.33), channel_id=1, source_target_pairs={{0,3},{1,0},{2,1},{3,2},{4,7},{5,4},{6,5},{7,6},{8,11},{9,8},{10,9... | collective-permute-start | bytes 73736 | tf_op jit(solution)/shard_map/ppermute | solution.py:36
  94.1 1.1 collective-permute-done.6.refs_1_
  95.2 0.7 collective-permute-done.7.refs_2_
  95.9 1.0 update.2
  96.8 13.5 %all_to_all.15.table_ref = bf16[64,8,128]{2,1,0:T(8,128)(2,1)S(1)} all-to-all(bf16[64,8,128]{2,1,0:T(8,128)(2,1)S(1)} %get-tuple-element.36), channel_id=1, replica_groups=mesh['trip'=8,'row'=4] {'trip','row'}, dimensions={0} | all-to-all | bytes 262144 | tf_op jit(solution)/shard_map/all_to_all | solution.py:353
  110.3 0.9 coupling_terms.3
  111.2 0.5 collective-permute-start.10
  111.7 1.1 collective-permute-start.11
  112.8 2.3 %collective-permute-done.10.refs_2_ = bf16[12,8,128]{2,1,0:T(8,128)(2,1)S(1)} collective-permute-done((bf16[12,8,128]{2,1,0:T(8,128)(2,1)S(1)}, bf16[12,8,128]{2,1,0:T(8,128)(2,1)S(1)}, u32[]{:S(2)}, u32[]{:S(2)}) %collective-permute-start.10) | collective-permute-done | bytes 24608 | tf_op jit(solution)/shard_map/ppermute | solution.py:36
  115.1 1.0 collective-permute-done.9.refs_1_
  116.1 0.8 update.3
  116.9 0.3 reshape.208
  117.3 0.4 copy.37
  117.7 0.8 copy.38
  (51 shorter events, 2.3 us)
Async XLA Ops:
  2.3 14.4 %copy-start.1 = (s32[24]{0:T(128)}, s32[24]{0:T(128)S(1)}, u32[]{:S(2)}) copy-start(s32[24]{0:T(128)S(1)} %get-tuple-element.56.places.row_place) | copy-start | bytes 292
  3.0 14.4 %collective-permute-start = (s32[12]{0:T(128)}, s32[12]{0:T(128)}, u32[]{:S(2)}, u32[]{:S(2)}) collective-permute-start(s32[12]{0:T(128)} %get-tuple-element.54), channel_id=1, source_target_pairs={{0,1},{1,2},{2,3},{3,0},{4,5},{5,6},{6,7},{7,4},{8,9},{9,10},{10,1... | collective-permute-start | bytes 152 | tf_op jit(solution)/shard_map/ppermute | solution.py:36
  3.5 13.9 %collective-permute-start.1 = (s32[12]{0:T(128)}, s32[12]{0:T(128)}, u32[]{:S(2)}, u32[]{:S(2)}) collective-permute-start(s32[12]{0:T(128)} %get-tuple-element.53), channel_id=1, source_target_pairs={{0,2},{1,3},{2,0},{3,1},{4,6},{5,7},{6,4},{7,5},{8,10},{9,11},{10,... | collective-permute-start | bytes 152 | tf_op jit(solution)/shard_map/ppermute | solution.py:36
  6.0 11.4 %collective-permute-start.2 = (s32[12]{0:T(128)}, s32[12]{0:T(128)}, u32[]{:S(2)}, u32[]{:S(2)}) collective-permute-start(s32[12]{0:T(128)} %get-tuple-element.52), channel_id=1, source_target_pairs={{0,3},{1,0},{2,1},{3,2},{4,7},{5,4},{6,5},{7,6},{8,11},{9,8},{10,9... | collective-permute-start | bytes 152 | tf_op jit(solution)/shard_map/ppermute | solution.py:36
  8.2 6.7 %copy-start.5 = (s32[24,2]{1,0:T(8,128)}, s32[24,2]{1,0:T(8,128)S(1)}, u32[]{:S(2)}) copy-start(s32[24,2]{1,0:T(8,128)S(1)} %copy.41) | copy-start | bytes 580
  8.5 0.5 copy-start.7
  9.8 12.0 %all-to-all-start = ((s32[32,1,128]{2,1,0:T(1,128)}), s32[32,1,128]{2,1,0:T(1,128)}, u32[]{:S(2)}, u32[]{:S(2)}) async-start(s32[32,1,128]{2,1,0:T(1,128)} %bitcast.6), calls=%async_computation | async-start | bytes 32768 | tf_op jit(solution)/shard_map/all_to_all | solution.py:353
  16.1 1.2 %copy-start = (bf16[64,64,128]{2,1,0:T(8,128)(2,1)S(1)}, bf16[64,64,128]{2,1,0:T(8,128)(2,1)}, u32[]{:S(2)}) copy-start(bf16[64,64,128]{2,1,0:T(8,128)(2,1)} %table_ref.1) | copy-start | bytes 3145732
  17.0 0.7 copy-start.6
  24.4 3.0 %copy-start.8 = (s32[48]{0:T(128)S(1)}, s32[48]{0:T(128)}, u32[]{:S(2)}) copy-start(s32[48]{0:T(128)} %copy-done.7) | copy-start | bytes 580
  24.4 3.7 %copy-start.4 = (f32[64,768]{1,0:T(8,128)S(1)}, f32[64,768]{1,0:T(8,128)}, u32[]{:S(2)}) copy-start(f32[64,768]{1,0:T(8,128)} %param.12) | copy-start | bytes 589828
  24.4 46.3 %all-to-all-start.1 = ((bf16[64,72,128]{2,1,0:T(8,128)(2,1)}), bf16[64,72,128]{2,1,0:T(8,128)(2,1)S(1)}, u32[]{:S(2)}, u32[]{:S(2)}) async-start(bf16[64,72,128]{2,1,0:T(8,128)(2,1)} %look_up.3), calls=%async_computation.1 | async-start | bytes 2359296 | tf_op jit(solution)/shard_map/all_to_all | solution.py:353
  29.9 12.3 %collective-permute-start.3 = (bf16[12,64,128]{2,1,0:T(8,128)(2,1)S(1)}, bf16[12,64,128]{2,1,0:T(8,128)(2,1)S(1)}, u32[]{:S(2)}, u32[]{:S(2)}) collective-permute-start(bf16[12,64,128]{2,1,0:T(8,128)(2,1)S(1)} %get-tuple-element.25), channel_id=1, source_target_pairs={{0,3},{1,0},{2,1},{3,2},{4,7},{5,4},{6,5},{7,6},{8,11},{9,8},{10,9... | collective-permute-start | bytes 589832 | tf_op jit(solution)/shard_map/ppermute | solution.py:362
  31.5 18.2 %collective-permute-start.4 = (bf16[12,64,128]{2,1,0:T(8,128)(2,1)S(1)}, bf16[12,64,128]{2,1,0:T(8,128)(2,1)S(1)}, u32[]{:S(2)}, u32[]{:S(2)}) collective-permute-start(bf16[12,64,128]{2,1,0:T(8,128)(2,1)S(1)} %get-tuple-element.26), channel_id=1, source_target_pairs={{0,2},{1,3},{2,0},{3,1},{4,6},{5,7},{6,4},{7,5},{8,10},{9,11},{10,... | collective-permute-start | bytes 589832 | tf_op jit(solution)/shard_map/ppermute | solution.py:362
  31.9 17.9 %collective-permute-start.5 = (bf16[12,64,128]{2,1,0:T(8,128)(2,1)S(1)}, bf16[12,64,128]{2,1,0:T(8,128)(2,1)S(1)}, u32[]{:S(2)}, u32[]{:S(2)}) collective-permute-start(bf16[12,64,128]{2,1,0:T(8,128)(2,1)S(1)} %get-tuple-element.27), channel_id=1, source_target_pairs={{0,1},{1,2},{2,3},{3,0},{4,5},{5,6},{6,7},{7,4},{8,9},{9,10},{10,1... | collective-permute-start | bytes 589832 | tf_op jit(solution)/shard_map/ppermute | solution.py:362
  50.7 20.0 %copy-start.3 = (s32[24]{0:T(128)S(1)}, s32[24]{0:T(128)}, u32[]{:S(2)}) copy-start(s32[24]{0:T(128)} %weights.1) | copy-start | bytes 292
  70.7 20.3 %copy-start.2 = (s32[24]{0:T(128)S(1)}, s32[24]{0:T(128)}, u32[]{:S(2)}) copy-start(s32[24]{0:T(128)} %copy-done.1) | copy-start | bytes 292
  91.9 3.3 %collective-permute-start.6 = (bf16[12,8,128]{2,1,0:T(8,128)(2,1)S(1)}, bf16[12,8,128]{2,1,0:T(8,128)(2,1)S(1)}, u32[]{:S(2)}, u32[]{:S(2)}) collective-permute-start(bf16[12,8,128]{2,1,0:T(8,128)(2,1)S(1)} %get-tuple-element.31), channel_id=1, source_target_pairs={{0,1},{1,2},{2,3},{3,0},{4,5},{5,6},{6,7},{7,4},{8,9},{9,10},{10,1... | collective-permute-start | bytes 73736 | tf_op jit(solution)/shard_map/ppermute | solution.py:36
  92.0 3.9 %collective-permute-start.7 = (bf16[12,8,128]{2,1,0:T(8,128)(2,1)S(1)}, bf16[12,8,128]{2,1,0:T(8,128)(2,1)S(1)}, u32[]{:S(2)}, u32[]{:S(2)}) collective-permute-start(bf16[12,8,128]{2,1,0:T(8,128)(2,1)S(1)} %get-tuple-element.32), channel_id=1, source_target_pairs={{0,2},{1,3},{2,0},{3,1},{4,6},{5,7},{6,4},{7,5},{8,10},{9,11},{10,... | collective-permute-start | bytes 73736 | tf_op jit(solution)/shard_map/ppermute | solution.py:36
  92.7 3.2 %collective-permute-start.8 = (bf16[12,8,128]{2,1,0:T(8,128)(2,1)S(1)}, bf16[12,8,128]{2,1,0:T(8,128)(2,1)S(1)}, u32[]{:S(2)}, u32[]{:S(2)}) collective-permute-start(bf16[12,8,128]{2,1,0:T(8,128)(2,1)S(1)} %get-tuple-element.33), channel_id=1, source_target_pairs={{0,3},{1,0},{2,1},{3,2},{4,7},{5,4},{6,5},{7,6},{8,11},{9,8},{10,9... | collective-permute-start | bytes 73736 | tf_op jit(solution)/shard_map/ppermute | solution.py:36
  111.2 3.9 %collective-permute-start.10 = (bf16[12,8,128]{2,1,0:T(8,128)(2,1)S(1)}, bf16[12,8,128]{2,1,0:T(8,128)(2,1)S(1)}, u32[]{:S(2)}, u32[]{:S(2)}) collective-permute-start(bf16[12,8,128]{2,1,0:T(8,128)(2,1)S(1)} %get-tuple-element.39), channel_id=1, source_target_pairs={{0,2},{1,3},{2,0},{3,1},{4,6},{5,7},{6,4},{7,5},{8,10},{9,11},{10,... | collective-permute-start | bytes 73736 | tf_op jit(solution)/shard_map/ppermute | solution.py:36
  111.7 3.4 %collective-permute-start.11 = (bf16[12,8,128]{2,1,0:T(8,128)(2,1)S(1)}, bf16[12,8,128]{2,1,0:T(8,128)(2,1)S(1)}, u32[]{:S(2)}, u32[]{:S(2)}) collective-permute-start(bf16[12,8,128]{2,1,0:T(8,128)(2,1)S(1)} %get-tuple-element.40), channel_id=1, source_target_pairs={{0,3},{1,0},{2,1},{3,2},{4,7},{5,4},{6,5},{7,6},{8,11},{9,8},{10,9... | collective-permute-start | bytes 73736 | tf_op jit(solution)/shard_map/ppermute | solution.py:36
  112.8 3.3 %collective-permute-start.9 = (bf16[12,8,128]{2,1,0:T(8,128)(2,1)S(1)}, bf16[12,8,128]{2,1,0:T(8,128)(2,1)S(1)}, u32[]{:S(2)}, u32[]{:S(2)}) collective-permute-start(bf16[12,8,128]{2,1,0:T(8,128)(2,1)S(1)} %get-tuple-element.38), channel_id=1, source_target_pairs={{0,1},{1,2},{2,3},{3,0},{4,5},{5,6},{6,7},{7,4},{8,9},{9,10},{10,1... | collective-permute-start | bytes 73736 | tf_op jit(solution)/shard_map/ppermute | solution.py:36

commit v4 on v3

--- a/solution.py
+++ b/solution.py
@@ -371,7 +371,7 @@
     )
     sent_state = jnp.where(one == columns, 1.0, state).astype(BF16)
     records = jnp.concatenate([eigvecs, sent_state], 1)
-    queries, row_vecs = lax.optimization_barrier((queries, row_vecs))
+    queries, first_table = lax.optimization_barrier((queries, first_table))
     far_table = far(look_up(queries, records, 1)[0])
     driven = packed(source)
     rate = jnp.concatenate([base_rate, base_rate], 1)[:, None, :]

time: 120 us -> 115 us (0.958)
  starting transfers between devices: 18.3 us -> 21.8 us
  local copies, waits for them, and re-layouts: 9.05 us -> 6.27 us
  waiting for transfers between devices: 24.5 us -> 21.8 us
  blocking collectives: 13.5 us -> 11.9 us
    ppermute x3, waiting for transfers between devices: 16.6 us -> 7.49 us  [body(): lax.ppermute(row_vecs[d], 'row', [(i, (i - d) % row_count) for i in range...]
    all_to_all x2, waiting for transfers between devices: 2.77 us -> 9.5 us  [far(): return lax.all_to_all(values, AXES, split_axis=0, concat_axis=0, tiled=True)]
    all_to_all x2, starting transfers between devices: 8.05 us -> 10.7 us  [far(): return lax.all_to_all(values, AXES, split_axis=0, concat_axis=0, tiled=True)]
    all_to_all x1, blocking collectives: 13.5 us -> 11.9 us  [far(): return lax.all_to_all(values, AXES, split_axis=0, concat_axis=0, tiled=True)]
  transfers between devices with their start and end apart: 14 -> 14, of which waited for: 7 -> 9; matrix products, arithmetic and copies ran while one was open for 8% -> 5% of each run, Pallas kernels for 17% -> 18%
where the time goes in v4:
time: 115 us; the launch traced here: 114 us
  Pallas kernels  46.3 us (40%)
  starting transfers between devices  21.8 us (19%)
  waiting for transfers between devices  21.8 us (19%)
  blocking collectives  11.9 us (10%)
  local copies, waits for them, and re-layouts  6.27 us (5%)
  other arithmetic  5.69 us (5%)
    pallas_call x1, Pallas kernels, contract_rest(): pl.pallas_call(functools.partial(second_kernel, stride, group), grid_spec...  20.3 us
    pallas_call x1, Pallas kernels, contract_first(): pl.pallas_call(first_kernel, grid_spec=pltpu.PrefetchScalarGridSpec(num_s...  20 us
    all_to_all x1, blocking collectives, far(): return lax.all_to_all(values, AXES, split_axis=0, concat_axis=0, tiled=True)  11.9 us
    all_to_all x2, starting transfers between devices, far(): return lax.all_to_all(values, AXES, split_axis=0, concat_axis=0, tiled=True)  10.7 us
    all_to_all x2, waiting for transfers between devices, far(): return lax.all_to_all(values, AXES, split_axis=0, concat_axis=0, tiled=True)  9.5 us
    ppermute x9, starting transfers between devices, from_peers(): lax.ppermute(blocks[d], 'row', [(i, (i + d) % count) for i in range(count)])  8.98 us
    ppermute x3, waiting for transfers between devices, body(): lax.ppermute(row_vecs[d], 'row', [(i, (i - d) % row_count) for i in range...  7.49 us
    ppermute x9, waiting for transfers between devices, from_peers(): lax.ppermute(blocks[d], 'row', [(i, (i + d) % count) for i in range(count)])  4.78 us
  transfers between devices with their start and end apart: 14, of which 9 were waited for; matrix products, arithmetic and copies ran while one was open for 5% of the time, Pallas kernels for 18%

profile of v4, /device:TPU:0, one launch (start us, length us, event | category | flops | bytes accessed | tf_op | source)
XLA Modules:
  0.0 114.1 jit_solution(1358292609757163720)
XLA Ops:
  0.0 0.7 and_select_fusion.3
  0.7 0.7 fusion.7
  1.4 0.2 convert_reduce_fusion.1
  1.6 0.7 fusion.10
  2.4 0.5 collective-permute-start
  2.9 2.5 %collective-permute-start.1 = (s32[12]{0:T(128)S(1)}, s32[12]{0:T(128)S(1)}, u32[]{:S(2)}, u32[]{:S(2)}) collective-permute-start(s32[12]{0:T(128)S(1)} %get-tuple-element.55), channel_id=1, source_target_pairs={{0,2},{1,3},{2,0},{3,1},{4,6},{5,7},{6,4},{7,5},{8,10},{9,11},{10,... | collective-permute-start | bytes 152 | tf_op jit(solution)/shard_map/ppermute | solution.py:36
  5.4 1.4 %collective-permute-start.2 = (s32[12]{0:T(128)S(1)}, s32[12]{0:T(128)S(1)}, u32[]{:S(2)}, u32[]{:S(2)}) collective-permute-start(s32[12]{0:T(128)S(1)} %get-tuple-element.54), channel_id=1, source_target_pairs={{0,3},{1,0},{2,1},{3,2},{4,7},{5,4},{6,5},{7,6},{8,11},{9,8},{10,9... | collective-permute-start | bytes 152 | tf_op jit(solution)/shard_map/ppermute | solution.py:36
  6.8 0.7 slice.40
  7.7 0.2 convert_reduce_fusion
  7.9 0.8 select_reduce_fusion
  8.7 4.9 %all-to-all-start = ((s32[32,1,128]{2,1,0:T(1,128)}), s32[32,1,128]{2,1,0:T(1,128)S(1)}, u32[]{:S(2)}, u32[]{:S(2)}) async-start(s32[32,1,128]{2,1,0:T(1,128)} %bitcast.6), calls=%async_computation | async-start | bytes 32768 | tf_op jit(solution)/shard_map/all_to_all | solution.py:353
  13.7 1.1 copy.30
  14.9 0.5 copy.32
  15.4 0.3 reshape.204.refs_4_
  16.0 0.6 look_up.2
  16.6 1.6 %collective-permute-start.3 = (bf16[12,64,128]{2,1,0:T(8,128)(2,1)S(1)}, bf16[12,64,128]{2,1,0:T(8,128)(2,1)}, u32[]{:S(2)}, u32[]{:S(2)}) collective-permute-start(bf16[12,64,128]{2,1,0:T(8,128)(2,1)S(1)} %get-tuple-element.26), channel_id=1, source_target_pairs={{0,3},{1,0},{2,1},{3,2},{4,7},{5,4},{6,5},{7,6},{8,11},{9,8},{10,9... | collective-permute-start | bytes 589832 | tf_op jit(solution)/shard_map/ppermute | solution.py:362
  18.2 0.4 collective-permute-start.4
  18.6 0.1 collective-permute-start.5
  18.8 1.9 %all-to-all-done = s32[32,1,128]{2,1,0:T(1,128)S(1)} async-done(((s32[32,1,128]{2,1,0:T(1,128)}), s32[32,1,128]{2,1,0:T(1,128)S(1)}, u32[]{:S(2)}, u32[]{:S(2)}) %all-to-all-start) | async-done | bytes 16416 | tf_op jit(solution)/shard_map/all_to_all | solution.py:353
  20.9 2.6 %collective-permute-done.3 = bf16[12,64,128]{2,1,0:T(8,128)(2,1)} collective-permute-done((bf16[12,64,128]{2,1,0:T(8,128)(2,1)S(1)}, bf16[12,64,128]{2,1,0:T(8,128)(2,1)}, u32[]{:S(2)}, u32[]{:S(2)}) %collective-permute-start.3) | collective-permute-done | bytes 196640 | tf_op jit(solution)/shard_map/ppermute | solution.py:362
  23.5 4.9 %collective-permute-done.4 = bf16[12,64,128]{2,1,0:T(8,128)(2,1)} collective-permute-done((bf16[12,64,128]{2,1,0:T(8,128)(2,1)S(1)}, bf16[12,64,128]{2,1,0:T(8,128)(2,1)}, u32[]{:S(2)}, u32[]{:S(2)}) %collective-permute-start.4) | collective-permute-done | bytes 196640 | tf_op jit(solution)/shard_map/ppermute | solution.py:362
  28.4 2.1 %pad_maximum_fusion.1.one_ref.two_ref = bf16[48,64,128]{2,1,0:T(8,128)(2,1)} fusion(bf16[12,64,128]{2,1,0:T(8,128)(2,1)} %collective-permute-done.5, bf16[12,64,128]{2,1,0:T(8,128)(2,1)} %collective-permute-done.4, bf16[12,64,128]{2,1,0:T(8,128)(2,1)} %collective-permute-done.3, bf16[12,64,128]{2,1,0:T(8,128)(2,1)S(1)} %get-tuple-element.25), kind=kLoop, calls=%fused_computation.1 | loop fusion | flops 1179648 | bytes 1572864 | tf_op jit(solution)/shard_map/concatenate | solution.py:359
  30.4 1.7 %look_up.3 = bf16[64,72,128]{2,1,0:T(8,128)(2,1)} custom-call(s32[64]{0:T(128)S(1)} %reshape_squeeze.3.queries, bf16[64,72,128]{2,1,0:T(8,128)(2,1)S(1)} %pad_maximum_fusion.table_ref), custom_call_target="tpu_custom_call" | custom-call | tf_op jit(solution)/shard_map/look_up/pallas_call | solution.py:50
  32.2 5.8 %all-to-all-start.1 = ((bf16[64,72,128]{2,1,0:T(8,128)(2,1)}), bf16[64,72,128]{2,1,0:T(8,128)(2,1)S(1)}, u32[]{:S(2)}, u32[]{:S(2)}) async-start(bf16[64,72,128]{2,1,0:T(8,128)(2,1)} %look_up.3), calls=%async_computation.1 | async-start | bytes 2359296 | tf_op jit(solution)/shard_map/all_to_all | solution.py:353
  38.1 0.2 copy.33
  38.4 0.5 copy.35
  38.9 0.3 reshape.207.refs_5_
  39.2 0.2 slice_reduce_fusion.1
  39.5 20.0 %contract_first.1.refs_8_ = bf16[12,64,128,128]{3,2,1,0:T(8,128)(2,1)} custom-call(s32[24]{0:T(128)} %copy-done.1, bf16[48,64,128]{2,1,0:T(8,128)(2,1)} %pad_maximum_fusion.1.one_ref.two_ref, bf16[48,64,128]{2,1,0:T(8,128)(2,1)} %pad_maximum_fusion.1.one_ref.two_ref, bf16[24,64,4096]{2,1,0:T(8,128)(2,1)} %cubic_ref.1), custom_call_target="tpu_custom_call" | custom-call | flops 1610612736 | bytes 37748736 | tf_op jit(solution)/shard_map/contract_first/pallas_call | solution.py:90
  59.5 7.6 %all-to-all-done.1.refs_0_.refs_1_.refs_2_.refs_3_.refs_4_.refs_5_.refs_6_.refs_7_ = bf16[64,72,128]{2,1,0:T(8,128)(2,1)S(1)} async-done(((bf16[64,72,128]{2,1,0:T(8,128)(2,1)}), bf16[64,72,128]{2,1,0:T(8,128)(2,1)S(1)}, u32[]{:S(2)}, u32[]{:S(2)}) %all-to-all-start.1) | async-done | bytes 1179680 | tf_op jit(solution)/shard_map/all_to_all | solution.py:353
  67.1 20.3 %contract_rest.1.pair_ref = bf16[24,256,128]{2,1,0:T(8,128)(2,1)S(1)} custom-call(s32[24]{0:T(128)S(1)} %get-tuple-element.46.second_place, s32[24]{0:T(128)S(1)} %get-tuple-element.45.third_place, s32[24]{0:T(128)S(1)} %copy-done.3, bf16[64,72,128]{2,1,0:T(8,128)(2,1)S(1)} %all-to-all-done.1.refs_0_.refs_1_.refs_2_.refs_3_.refs_4_.refs_5_.refs_6_.refs_7_, ...), custom_call_target="tpu_custom_call" | custom-call | flops 12884901888 | bytes 25165824 | tf_op jit(solution)/shard_map/contract_rest/pallas_call | solution.py:204
  87.4 0.9 coupling_terms.2
  88.4 1.5 %collective-permute-start.7 = (bf16[12,8,128]{2,1,0:T(8,128)(2,1)S(1)}, bf16[12,8,128]{2,1,0:T(8,128)(2,1)S(1)}, u32[]{:S(2)}, u32[]{:S(2)}) collective-permute-start(bf16[12,8,128]{2,1,0:T(8,128)(2,1)S(1)} %get-tuple-element.34), channel_id=1, source_target_pairs={{0,2},{1,3},{2,0},{3,1},{4,6},{5,7},{6,4},{7,5},{8,10},{9,11},{10,... | collective-permute-start | bytes 73736 | tf_op jit(solution)/shard_map/ppermute | solution.py:36
  89.9 1.4 %collective-permute-start.8 = (bf16[12,8,128]{2,1,0:T(8,128)(2,1)S(1)}, bf16[12,8,128]{2,1,0:T(8,128)(2,1)S(1)}, u32[]{:S(2)}, u32[]{:S(2)}) collective-permute-start(bf16[12,8,128]{2,1,0:T(8,128)(2,1)S(1)} %get-tuple-element.35), channel_id=1, source_target_pairs={{0,3},{1,0},{2,1},{3,2},{4,7},{5,4},{6,5},{7,6},{8,11},{9,8},{10,9... | collective-permute-start | bytes 73736 | tf_op jit(solution)/shard_map/ppermute | solution.py:36
  91.3 0.4 collective-permute-done.6.refs_1_
  91.6 0.7 collective-permute-done.7.refs_2_
  92.3 0.5 collective-permute-done.8.refs_3_
  92.8 1.0 update.2
  93.8 11.9 %all_to_all.15.table_ref = bf16[64,8,128]{2,1,0:T(8,128)(2,1)S(1)} all-to-all(bf16[64,8,128]{2,1,0:T(8,128)(2,1)S(1)} %get-tuple-element.38), channel_id=1, replica_groups=mesh['trip'=8,'row'=4] {'trip','row'}, dimensions={0} | all-to-all | bytes 262144 | tf_op jit(solution)/shard_map/all_to_all | solution.py:353
  105.7 0.9 coupling_terms.3
  106.6 0.5 collective-permute-start.10
  107.1 1.1 collective-permute-start.11
  108.3 2.3 %collective-permute-done.10.refs_2_ = bf16[12,8,128]{2,1,0:T(8,128)(2,1)S(1)} collective-permute-done((bf16[12,8,128]{2,1,0:T(8,128)(2,1)S(1)}, bf16[12,8,128]{2,1,0:T(8,128)(2,1)S(1)}, u32[]{:S(2)}, u32[]{:S(2)}) %collective-permute-start.10) | collective-permute-done | bytes 24608 | tf_op jit(solution)/shard_map/ppermute | solution.py:36
  110.5 1.0 collective-permute-done.9.refs_1_
  111.5 0.9 update.3
  112.4 0.3 reshape.208
  112.8 0.4 copy.37
  113.2 0.8 copy.38
  (45 shorter events, 1.5 us)
Async XLA Ops:
  2.3 13.1 %copy-start.1 = (s32[24]{0:T(128)}, s32[24]{0:T(128)S(1)}, u32[]{:S(2)}) copy-start(s32[24]{0:T(128)S(1)} %get-tuple-element.58.places.row_place) | copy-start | bytes 292
  2.4 13.3 %collective-permute-start = (s32[12]{0:T(128)S(1)}, s32[12]{0:T(128)S(1)}, u32[]{:S(2)}, u32[]{:S(2)}) collective-permute-start(s32[12]{0:T(128)S(1)} %get-tuple-element.56), channel_id=1, source_target_pairs={{0,1},{1,2},{2,3},{3,0},{4,5},{5,6},{6,7},{7,4},{8,9},{9,10},{10,1... | collective-permute-start | bytes 152 | tf_op jit(solution)/shard_map/ppermute | solution.py:36
  2.9 12.9 %collective-permute-start.1 = (s32[12]{0:T(128)S(1)}, s32[12]{0:T(128)S(1)}, u32[]{:S(2)}, u32[]{:S(2)}) collective-permute-start(s32[12]{0:T(128)S(1)} %get-tuple-element.55), channel_id=1, source_target_pairs={{0,2},{1,3},{2,0},{3,1},{4,6},{5,7},{6,4},{7,5},{8,10},{9,11},{10,... | collective-permute-start | bytes 152 | tf_op jit(solution)/shard_map/ppermute | solution.py:36
  5.4 10.3 %collective-permute-start.2 = (s32[12]{0:T(128)S(1)}, s32[12]{0:T(128)S(1)}, u32[]{:S(2)}, u32[]{:S(2)}) collective-permute-start(s32[12]{0:T(128)S(1)} %get-tuple-element.54), channel_id=1, source_target_pairs={{0,3},{1,0},{2,1},{3,2},{4,7},{5,4},{6,5},{7,6},{8,11},{9,8},{10,9... | collective-permute-start | bytes 152 | tf_op jit(solution)/shard_map/ppermute | solution.py:36
  8.7 12.0 %all-to-all-start = ((s32[32,1,128]{2,1,0:T(1,128)}), s32[32,1,128]{2,1,0:T(1,128)S(1)}, u32[]{:S(2)}, u32[]{:S(2)}) async-start(s32[32,1,128]{2,1,0:T(1,128)} %bitcast.6), calls=%async_computation | async-start | bytes 32768 | tf_op jit(solution)/shard_map/all_to_all | solution.py:353
  14.8 1.2 %copy-start = (bf16[64,64,128]{2,1,0:T(8,128)(2,1)S(1)}, bf16[64,64,128]{2,1,0:T(8,128)(2,1)}, u32[]{:S(2)}) copy-start(bf16[64,64,128]{2,1,0:T(8,128)(2,1)} %table_ref.1) | copy-start | bytes 3145732
  16.6 6.9 %collective-permute-start.3 = (bf16[12,64,128]{2,1,0:T(8,128)(2,1)S(1)}, bf16[12,64,128]{2,1,0:T(8,128)(2,1)}, u32[]{:S(2)}, u32[]{:S(2)}) collective-permute-start(bf16[12,64,128]{2,1,0:T(8,128)(2,1)S(1)} %get-tuple-element.26), channel_id=1, source_target_pairs={{0,3},{1,0},{2,1},{3,2},{4,7},{5,4},{6,5},{7,6},{8,11},{9,8},{10,9... | collective-permute-start | bytes 589832 | tf_op jit(solution)/shard_map/ppermute | solution.py:362
  18.2 10.1 %collective-permute-start.4 = (bf16[12,64,128]{2,1,0:T(8,128)(2,1)S(1)}, bf16[12,64,128]{2,1,0:T(8,128)(2,1)}, u32[]{:S(2)}, u32[]{:S(2)}) collective-permute-start(bf16[12,64,128]{2,1,0:T(8,128)(2,1)S(1)} %get-tuple-element.27), channel_id=1, source_target_pairs={{0,2},{1,3},{2,0},{3,1},{4,6},{5,7},{6,4},{7,5},{8,10},{9,11},{10,... | collective-permute-start | bytes 589832 | tf_op jit(solution)/shard_map/ppermute | solution.py:362
  18.6 9.8 %collective-permute-start.5 = (bf16[12,64,128]{2,1,0:T(8,128)(2,1)S(1)}, bf16[12,64,128]{2,1,0:T(8,128)(2,1)}, u32[]{:S(2)}, u32[]{:S(2)}) collective-permute-start(bf16[12,64,128]{2,1,0:T(8,128)(2,1)S(1)} %get-tuple-element.28), channel_id=1, source_target_pairs={{0,1},{1,2},{2,3},{3,0},{4,5},{5,6},{6,7},{7,4},{8,9},{9,10},{10,1... | collective-permute-start | bytes 589832 | tf_op jit(solution)/shard_map/ppermute | solution.py:362
  32.2 5.9 %copy-start.4 = (f32[64,768]{1,0:T(8,128)S(1)}, f32[64,768]{1,0:T(8,128)}, u32[]{:S(2)}) copy-start(f32[64,768]{1,0:T(8,128)} %param.12) | copy-start | bytes 589828
  32.2 34.9 %all-to-all-start.1 = ((bf16[64,72,128]{2,1,0:T(8,128)(2,1)}), bf16[64,72,128]{2,1,0:T(8,128)(2,1)S(1)}, u32[]{:S(2)}, u32[]{:S(2)}) async-start(bf16[64,72,128]{2,1,0:T(8,128)(2,1)} %look_up.3), calls=%async_computation.1 | async-start | bytes 2359296 | tf_op jit(solution)/shard_map/all_to_all | solution.py:353
  38.3 1.1 copy-start.5
  39.5 27.6 %copy-start.3 = (s32[24]{0:T(128)S(1)}, s32[24]{0:T(128)}, u32[]{:S(2)}) copy-start(s32[24]{0:T(128)} %weights.1) | copy-start | bytes 292
  67.1 20.3 %copy-start.2 = (s32[24]{0:T(128)S(1)}, s32[24]{0:T(128)}, u32[]{:S(2)}) copy-start(s32[24]{0:T(128)} %copy-done.1) | copy-start | bytes 292
  88.3 3.3 %collective-permute-start.6 = (bf16[12,8,128]{2,1,0:T(8,128)(2,1)S(1)}, bf16[12,8,128]{2,1,0:T(8,128)(2,1)S(1)}, u32[]{:S(2)}, u32[]{:S(2)}) collective-permute-start(bf16[12,8,128]{2,1,0:T(8,128)(2,1)S(1)} %get-tuple-element.33), channel_id=1, source_target_pairs={{0,1},{1,2},{2,3},{3,0},{4,5},{5,6},{6,7},{7,4},{8,9},{9,10},{10,1... | collective-permute-start | bytes 73736 | tf_op jit(solution)/shard_map/ppermute | solution.py:36
  88.4 3.9 %collective-permute-start.7 = (bf16[12,8,128]{2,1,0:T(8,128)(2,1)S(1)}, bf16[12,8,128]{2,1,0:T(8,128)(2,1)S(1)}, u32[]{:S(2)}, u32[]{:S(2)}) collective-permute-start(bf16[12,8,128]{2,1,0:T(8,128)(2,1)S(1)} %get-tuple-element.34), channel_id=1, source_target_pairs={{0,2},{1,3},{2,0},{3,1},{4,6},{5,7},{6,4},{7,5},{8,10},{9,11},{10,... | collective-permute-start | bytes 73736 | tf_op jit(solution)/shard_map/ppermute | solution.py:36
  89.9 2.9 %collective-permute-start.8 = (bf16[12,8,128]{2,1,0:T(8,128)(2,1)S(1)}, bf16[12,8,128]{2,1,0:T(8,128)(2,1)S(1)}, u32[]{:S(2)}, u32[]{:S(2)}) collective-permute-start(bf16[12,8,128]{2,1,0:T(8,128)(2,1)S(1)} %get-tuple-element.35), channel_id=1, source_target_pairs={{0,3},{1,0},{2,1},{3,2},{4,7},{5,4},{6,5},{7,6},{8,11},{9,8},{10,9... | collective-permute-start | bytes 73736 | tf_op jit(solution)/shard_map/ppermute | solution.py:36
  106.6 3.9 %collective-permute-start.10 = (bf16[12,8,128]{2,1,0:T(8,128)(2,1)S(1)}, bf16[12,8,128]{2,1,0:T(8,128)(2,1)S(1)}, u32[]{:S(2)}, u32[]{:S(2)}) collective-permute-start(bf16[12,8,128]{2,1,0:T(8,128)(2,1)S(1)} %get-tuple-element.41), channel_id=1, source_target_pairs={{0,2},{1,3},{2,0},{3,1},{4,6},{5,7},{6,4},{7,5},{8,10},{9,11},{10,... | collective-permute-start | bytes 73736 | tf_op jit(solution)/shard_map/ppermute | solution.py:36
  107.1 3.4 %collective-permute-start.11 = (bf16[12,8,128]{2,1,0:T(8,128)(2,1)S(1)}, bf16[12,8,128]{2,1,0:T(8,128)(2,1)S(1)}, u32[]{:S(2)}, u32[]{:S(2)}) collective-permute-start(bf16[12,8,128]{2,1,0:T(8,128)(2,1)S(1)} %get-tuple-element.42), channel_id=1, source_target_pairs={{0,3},{1,0},{2,1},{3,2},{4,7},{5,4},{6,5},{7,6},{8,11},{9,8},{10,9... | collective-permute-start | bytes 73736 | tf_op jit(solution)/shard_map/ppermute | solution.py:36
  108.3 3.3 %collective-permute-start.9 = (bf16[12,8,128]{2,1,0:T(8,128)(2,1)S(1)}, bf16[12,8,128]{2,1,0:T(8,128)(2,1)S(1)}, u32[]{:S(2)}, u32[]{:S(2)}) collective-permute-start(bf16[12,8,128]{2,1,0:T(8,128)(2,1)S(1)} %get-tuple-element.40), channel_id=1, source_target_pairs={{0,1},{1,2},{2,3},{3,0},{4,5},{5,6},{6,7},{7,4},{8,9},{9,10},{10,1... | collective-permute-start | bytes 73736 | tf_op jit(solution)/shard_map/ppermute | solution.py:36

commit v5 on v4

--- a/solution.py
+++ b/solution.py
@@ -60,54 +60,77 @@
     )(queries, table)
 
 
-def first_kernel(places, one_ref, two_ref, cubic_ref, out_ref):
+def pick_kernel(which, places, *refs):
+    table_refs, out_ref = refs[:-1], refs[-1]
+    for t in range(out_ref.shape[0]):
+        place, wanted = places[t], which[t]
+        found = table_refs[0][place]
+        for block in range(1, len(table_refs)):
+            found = jnp.where(wanted == block, table_refs[block][place], found)
+        out_ref[t] = found
+
+
+def pick(which, places, tables):
+    count = which.shape[0]
+    return pl.pallas_call(
+        pick_kernel,
+        in_specs=[pl.BlockSpec(memory_space=pltpu.SMEM)] * 2
+        + [pl.BlockSpec(memory_space=pltpu.VMEM)] * len(tables),
+        out_specs=pl.BlockSpec(memory_space=pltpu.VMEM),
+        out_shape=jax.ShapeDtypeStruct((count,) + tables[0].shape[1:], tables[0].dtype),
+        compiler_params=pltpu.CompilerParams(vmem_limit_bytes=16 * MIB),
+        name="pick",
+    )(which, places, *tables)
+
+
+def first_kernel(vec_ref, cubic_ref, out_ref):
     branches = cubic_ref.shape[1]
     both = 2 * branches
-    one, two = one_ref[0], two_ref[0]
-    none = jnp.zeros((branches, branches), one.dtype)
-    mixer = jnp.concatenate(
-        [
-            jnp.concatenate([one[:, :branches], none, one[:, branches:], none], 1),
-            jnp.concatenate([none, two[:, :branches], none, two[:, branches:]], 1),
-        ],
-        0,
-    )
     step = 4
-    for start in range(0, branches, step):
-        lanes = slice(start * branches, (start + step) * branches)
-        turned = jnp.concatenate([cubic_ref[0, :, lanes], cubic_ref[1, :, lanes]], 0).T
-        mixed = jnp.dot(turned, mixer, preferred_element_type=F32).astype(BF16)
-        for j in range(step):
-            for part in range(2):
-                out_ref[0, start + j, part * branches : (part + 1) * branches] = mixed[
-                    j * branches : (j + 1) * branches, part * both : (part + 1) * both
-                ]
-
-
-def contract_first(places, table, cubic):
+    for pair in range(out_ref.shape[0]):
+        one, two = vec_ref[2 * pair], vec_ref[2 * pair + 1]
+        none = jnp.zeros((branches, branches), one.dtype)
+        mixer = jnp.concatenate(
+            [
+                jnp.concatenate([one[:, :branches], none, one[:, branches:], none], 1),
+                jnp.concatenate([none, two[:, :branches], none, two[:, branches:]], 1),
+            ],
+            0,
+        )
+        for start in range(0, branches, step):
+            lanes = slice(start * branches, (start + step) * branches)
+            turned = jnp.concatenate(
+                [cubic_ref[2 * pair, :, lanes], cubic_ref[2 * pair + 1, :, lanes]], 0
+            ).T
+            mixed = jnp.dot(turned, mixer, preferred_element_type=F32).astype(BF16)
+            for j in range(step):
+                for part in range(2):
+                    out_ref[pair, start + j, part * branches : (part + 1) * branches] = mixed[
+                        j * branches : (j + 1) * branches, part * both : (part + 1) * both
+                    ]
+
+
+def contract_first(vectors, cubic):
     count, branches, pairs = cubic.shape
     both = 2 * branches
+    group = 2 if count % 4 == 0 else 1
     return pl.pallas_call(
         first_kernel,
-        grid_spec=pltpu.PrefetchScalarGridSpec(
-            num_scalar_prefetch=1,
-            grid=(count // 2,),
-            in_specs=[
-                pl.BlockSpec((1, branches, both), lambda t, places: (places[2 * t], 0, 0)),
-                pl.BlockSpec((1, branches, both), lambda t, places: (places[2 * t + 1], 0, 0)),
-                pl.BlockSpec((2, branches, pairs), lambda t, places: (t, 0, 0)),
-            ],
-            out_specs=pl.BlockSpec((1, branches, both, both), lambda t, places: (t, 0, 0, 0)),
-        ),
+        grid=(count // (2 * group),),
+        in_specs=[
+            pl.BlockSpec((2 * group, branches, both), lambda s: (s, 0, 0)),
+            pl.BlockSpec((2 * group, branches, pairs), lambda s: (s, 0, 0)),
+        ],
+        out_specs=pl.BlockSpec((group, branches, both, both), lambda s: (s, 0, 0, 0)),
         out_shape=jax.ShapeDtypeStruct((count // 2, branches, both, both), BF16),
-        compiler_params=pltpu.CompilerParams(vmem_limit_bytes=60 * MIB),
+        compiler_params=pltpu.CompilerParams(vmem_limit_bytes=40 * MIB),
         cost_estimate=pl.CostEstimate(
             flops=2 * count * both * branches * pairs,
             bytes_accessed=2 * count * (both + branches) * pairs,
             transcendentals=0,
         ),
         name="contract_first",
-    )(places, table, table, cubic)
+    )(vectors, cubic)
 
 
 def second_kernel(stride, group, second_place, third_place, weights, *refs):
@@ -212,7 +235,7 @@
             scratch_shapes=[pltpu.VMEM((branches * stride, both), F32)] * 2,
         ),
         out_shape=jax.ShapeDtypeStruct((2 * pairs, 2 * both, both), BF16),
-        compiler_params=pltpu.CompilerParams(vmem_limit_bytes=32 * MIB),
+        compiler_params=pltpu.CompilerParams(vmem_limit_bytes=44 * MIB),
         cost_estimate=pl.CostEstimate(
             flops=16 * pairs * both * both * branches * branches,
             bytes_accessed=2 * pairs * both * both * branches,
@@ -321,7 +344,6 @@
     columns = deviation.shape[1] // branches
     far_cap = (2 * trip_local + devices - 1) // devices
     row_cap = trip_local // 2
-    row_slots = row_count * row_cap
     rows = 8 * ((columns + 2 + 15) // 16)
 
     def packed(values):
@@ -335,34 +357,38 @@
         values = values.reshape(home_rows, 2 * rows, branches)[:, :columns]
         return jnp.swapaxes(values, 1, 2).reshape(home_rows, branches * columns)
 
-    first_dev = triplets[:, 0] // home_rows
-    first_local = triplets[:, 0] - first_dev * home_rows
-    ahead = (first_dev - lax.axis_index("row")) % row_count
-    row_place = ahead * row_cap + ranks_of(ahead)
-    row_codes = pack_ints(row_place, first_local + 1, row_slots).reshape(row_count, row_cap)
-
-    far_index = triplets[:, 1:].reshape(-1)
-    far_owner = far_index // home_rows
+    gathered = {0: eigvecs}
+    bit = row_count // 2
+    while bit:
+        pairing = [(i, i ^ bit) for i in range(row_count)]
+        gathered.update({k ^ bit: lax.ppermute(v, "row", pairing) for k, v in gathered.items()})
+        bit //= 2
+
+    me = lax.axis_index("trip") * row_count + lax.axis_index("row")
+    owner = triplets // home_rows
+    local = triplets - owner * home_rows
+    first_dev, far_owner = owner[:, 0], owner[:, 1:].reshape(-1)
+    row_rank = ranks_of(first_dev)
     far_rank = ranks_of(far_owner)
-    far_place = far_owner * far_cap + far_rank
     message = pack_ints(
-        far_owner * LANES + far_rank, far_index - far_owner * home_rows, devices * LANES
+        jnp.concatenate([far_owner * LANES + far_rank, first_dev * LANES + far_cap + row_rank]),
+        jnp.concatenate([local[:, 1:].reshape(-1), local[:, 0] + 1]),
+        devices * LANES,
     ).reshape(devices, 1, LANES)
 
     def far(values):
         return lax.all_to_all(values, AXES, split_axis=0, concat_axis=0, tiled=True)
 
-    queries = far(message)[:, 0, :far_cap].reshape(-1)
+    heard = far(message)[:, 0]
+    queries = heard[:, :far_cap].reshape(-1)
+    row_place = (first_dev - me) % row_count * row_cap + row_rank
+    far_place = far_owner * far_cap + far_rank
     second_place, third_place = far_place.reshape(trip_local, 2).T
-    codes = jnp.stack(from_peers([row_codes[d] for d in range(row_count)]))
-    row_vecs = look_up(jnp.maximum(codes - 1, 0).reshape(-1), eigvecs, row_count)
-    first_table = jnp.concatenate(
-        [row_vecs[0]]
-        + [
-            lax.ppermute(row_vecs[d], "row", [(i, (i - d) % row_count) for i in range(row_count)])
-            for d in range(1, row_count)
-        ],
-        0,
+    asked = lax.dynamic_slice(
+        heard, (lax.axis_index("trip") * row_count, far_cap), (row_count, row_cap)
+    )
+    codes = jnp.take(
+        asked, (lax.axis_index("row") - jnp.arange(row_count)) % row_count, axis=0, mode="clip"
     )
 
     state = packed(deviation)
@@ -371,12 +397,16 @@
     )
     sent_state = jnp.where(one == columns, 1.0, state).astype(BF16)
     records = jnp.concatenate([eigvecs, sent_state], 1)
-    queries, first_table = lax.optimization_barrier((queries, first_table))
     far_table = far(look_up(queries, records, 1)[0])
+    first_vecs = pick(
+        first_dev % row_count ^ lax.axis_index("row"),
+        local[:, 0],
+        [gathered[k] for k in range(row_count)],
+    )
     driven = packed(source)
     rate = jnp.concatenate([base_rate, base_rate], 1)[:, None, :]
-    first_table, driven, rate = lax.optimization_barrier((first_table, driven, rate))
-    first_part = contract_first(row_place, first_table, cubic)
+    first_vecs, driven, rate = lax.optimization_barrier((first_vecs, driven, rate))
+    first_part = contract_first(first_vecs, cubic)
     arrived_state = far_table[:, branches:]
     pairs = contract_rest(second_place, third_place, weights, far_table, first_part)
 

time: 115 us -> 133 us (1.16)
  waiting for transfers between devices: 21.8 us -> 44.7 us
  local copies, waits for them, and re-layouts: 6.27 us -> 17.8 us
  Pallas kernels: 46.3 us -> 39 us
  starting transfers between devices: 21.8 us -> 15.7 us
  other arithmetic: 5.69 us -> 1.62 us
    ppermute x3, waiting for transfers between devices: 7.49 us -> 36.2 us  [body(): lax.ppermute(v, 'row', pairing)]
    unnamed x15 -> x17, local copies, waits for them, and re-layouts: 1.52 us -> 10.1 us
    pallas_call x1 -> x2, Pallas kernels: 20 us -> 13.3 us  [the longest x1 11.2 us: contract_first(): pl.pallas_call(first_kernel, grid=(count // (2 * group),), in_specs=[pl.B...]
    ppermute x9 -> x6, starting transfers between devices: 8.98 us -> 3.95 us  [from_peers(): lax.ppermute(blocks[d], 'row', [(i, (i + d) % count) for i in range(count)])]
    all_to_all x2, waiting for transfers between devices: 9.5 us -> 4.53 us  [far(): return lax.all_to_all(values, AXES, split_axis=0, concat_axis=0, tiled=True)]
    concatenate x1, other arithmetic: 2.08 us -> 0.08 us  [body(): jnp.concatenate([far_owner * LANES + far_rank, first_dev * LANES + far_ca...]
    transpose x4, local copies, waits for them, and re-layouts: 1.12 us -> 2.91 us  [packed(): return jnp.swapaxes(values, 1, 2).reshape(home_rows, rows, 2 * branches)]
    ppermute x9 -> x6, waiting for transfers between devices: 4.78 us -> 3.9 us  [from_peers(): lax.ppermute(blocks[d], 'row', [(i, (i + d) % count) for i in range(count)])]
  transfers between devices with their start and end apart: 14 -> 11, of which waited for: 9 -> 6; matrix products, arithmetic and copies ran while one was open for 5% -> 6% of each run, Pallas kernels for 18% -> 10%
where the time goes in v5:
time: 133 us; the launch traced here: 132 us
  waiting for transfers between devices  44.7 us (34%)
  Pallas kernels  39 us (29%)
  local copies, waits for them, and re-layouts  17.8 us (13%)
  starting transfers between devices  15.7 us (12%)
  blocking collectives  13.1 us (10%)
  other arithmetic  1.62 us (1%)
    ppermute x3, waiting for transfers between devices, body(): lax.ppermute(v, 'row', pairing)  36.2 us
    pallas_call x1, Pallas kernels, contract_rest(): pl.pallas_call(functools.partial(second_kernel, stride, group), grid_spec...  20.3 us
    all_to_all x1, blocking collectives, far(): return lax.all_to_all(values, AXES, split_axis=0, concat_axis=0, tiled=True)  13.1 us
    pallas_call x1, Pallas kernels, contract_first(): pl.pallas_call(first_kernel, grid=(count // (2 * group),), in_specs=[pl.B...  11.2 us
    all_to_all x2, starting transfers between devices, far(): return lax.all_to_all(values, AXES, split_axis=0, concat_axis=0, tiled=True)  10.1 us
    unnamed x17, local copies, waits for them, and re-layouts  10.1 us
    all_to_all x2, waiting for transfers between devices, far(): return lax.all_to_all(values, AXES, split_axis=0, concat_axis=0, tiled=True)  4.53 us
    ppermute x6, starting transfers between devices, from_peers(): lax.ppermute(blocks[d], 'row', [(i, (i + d) % count) for i in range(count)])  3.95 us
  transfers between devices with their start and end apart: 11, of which 6 were waited for; matrix products, arithmetic and copies ran while one was open for 6% of the time, Pallas kernels for 10%

profile of v5, /device:TPU:0, one launch (start us, length us, event | category | flops | bytes accessed | tf_op | source)
XLA Modules:
  0.0 132.2 jit_solution(11892205897044850338)
XLA Ops:
  0.0 0.8 copy.41
  0.8 0.1 slice_reduce_fusion.3
  1.0 0.1 slice_reduce_fusion.2.places
  1.2 0.2 convert_reduce_fusion.1
  1.3 0.1 reshape.87
  1.4 0.2 convert_reduce_fusion
  1.8 0.8 select_reduce_fusion
  2.7 7.3 %all-to-all-start = ((s32[32,1,128]{2,1,0:T(1,128)}), s32[32,1,128]{2,1,0:T(1,128)S(1)}, u32[]{:S(2)}, u32[]{:S(2)}) async-start(s32[32,1,128]{2,1,0:T(1,128)} %bitcast), calls=%async_computation | async-start | bytes 32768 | tf_op jit(solution)/shard_map/all_to_all | solution.py:380
  10.0 1.1 copy.46
  11.2 0.5 copy.48
  11.7 0.3 reshape.93.refs_4_
  12.1 0.3 copy-done.1
  12.5 4.5 %all-to-all-done = s32[32,1,128]{2,1,0:T(1,128)S(1)} async-done(((s32[32,1,128]{2,1,0:T(1,128)}), s32[32,1,128]{2,1,0:T(1,128)S(1)}, u32[]{:S(2)}, u32[]{:S(2)}) %all-to-all-start) | async-done | bytes 16416 | tf_op jit(solution)/shard_map/all_to_all | solution.py:380
  17.1 1.7 %look_up.1 = bf16[64,72,128]{2,1,0:T(8,128)(2,1)} custom-call(s32[64]{0:T(128)S(1)} %reshape.90.queries, bf16[64,72,128]{2,1,0:T(8,128)(2,1)S(1)} %pad_maximum_fusion.table_ref), custom_call_target="tpu_custom_call" | custom-call | tf_op jit(solution)/shard_map/look_up/pallas_call | solution.py:50
  18.9 2.8 %all-to-all-start.1 = ((bf16[64,72,128]{2,1,0:T(8,128)(2,1)}), bf16[64,72,128]{2,1,0:T(8,128)(2,1)S(1)}, u32[]{:S(2)}, u32[]{:S(2)}) async-start(bf16[64,72,128]{2,1,0:T(8,128)(2,1)} %look_up.1), calls=%async_computation.1 | async-start | bytes 2359296 | tf_op jit(solution)/shard_map/all_to_all | solution.py:380
  21.7 1.7 %collective-permute-start.1 = (bf16[64,64,128]{2,1,0:T(8,128)(2,1)S(1)}, bf16[64,64,128]{2,1,0:T(8,128)(2,1)}, u32[]{:S(2)}, u32[]{:S(2)}) collective-permute-start(bf16[64,64,128]{2,1,0:T(8,128)(2,1)S(1)} %copy-done.1), channel_id=1, source_target_pairs={{0,2},{1,3},{2,0},{3,1},{4,6},{5,7},{6,4},{7,5},{8,10},{9,11},{10,... | collective-permute-start | bytes 3145736 | tf_op jit(solution)/shard_map/ppermute | solution.py:364
  23.4 36.2 %collective-permute-done.1.refs_2_ = bf16[64,64,128]{2,1,0:T(8,128)(2,1)} collective-permute-done((bf16[64,64,128]{2,1,0:T(8,128)(2,1)S(1)}, bf16[64,64,128]{2,1,0:T(8,128)(2,1)}, u32[]{:S(2)}, u32[]{:S(2)}) %collective-permute-start.1) | collective-permute-done | bytes 1048608 | tf_op jit(solution)/shard_map/ppermute | solution.py:364
  59.7 0.9 copy.49
  60.7 1.0 reshape.94
  61.7 0.8 pad_bitcast_fusion
  62.5 1.5 %copy.51 = f32[64,8,2,64]{3,2,1,0:T(2,128)S(1)} copy(f32[64,8,2,64]{0,1,2,3:T(8,128)} %pad_bitcast_fusion) | data formatting | bytes 524288 | tf_op jit(solution)/shard_map/transpose | solution.py:353
  64.1 0.3 reshape.96.refs_5_
  64.5 0.2 slice_reduce_fusion
  64.8 2.1 %pick.1.vec_ref = bf16[24,64,128]{2,1,0:T(8,128)(2,1)S(1)} custom-call(s32[24]{0:T(128)S(1)} %get-tuple-element.39.which, s32[24]{0:T(128)S(1)} %slice_reduce_fusion.2.places, bf16[64,64,128]{2,1,0:T(8,128)(2,1)S(1)} %copy-done.1, bf16[64,64,128]{2,1,0:T(8,128)(2,1)} %collective-permute-done.refs_1_, bf16[64,64,128]{2,1,0:T(8,128)(2,1)} %collective-permute-done.1.refs_2_, ...), custom_call_target="tpu_custom_call" | custom-call | tf_op jit(solution)/shard_map/pick/pallas_call | solution.py:75
  66.9 4.6 %copy-done = bf16[24,64,4096]{2,1,0:T(8,128)(2,1)S(1)} copy-done((bf16[24,64,4096]{2,1,0:T(8,128)(2,1)S(1)}, bf16[24,64,4096]{2,1,0:T(8,128)(2,1)}, u32[]{:S(2)}) %copy-start) | copy-done | bytes 12582936
  71.4 11.2 %contract_first.1.refs_8_ = bf16[12,64,128,128]{3,2,1,0:T(8,128)(2,1)} custom-call(bf16[24,64,128]{2,1,0:T(8,128)(2,1)S(1)} %pick.1.vec_ref, bf16[24,64,4096]{2,1,0:T(8,128)(2,1)S(1)} %copy-done), custom_call_target="tpu_custom_call" | custom-call | flops 1610612736 | bytes 37748736 | tf_op jit(solution)/shard_map/contract_first/pallas_call | solution.py:117
  82.6 1.1 copy-done.2
  83.7 1.3 copy-done.3
  85.0 20.3 %contract_rest.1.pair_ref = bf16[24,256,128]{2,1,0:T(8,128)(2,1)S(1)} custom-call(s32[24]{0:T(128)S(1)} %get-tuple-element.34.second_place, s32[24]{0:T(128)S(1)} %get-tuple-element.33.third_place, s32[24]{0:T(128)S(1)} %copy-done.4, bf16[64,72,128]{2,1,0:T(8,128)(2,1)S(1)} %copy-done.3, bf16[64,72,128]{2,1,0:T(8,128)(2,1)S(1)} %copy-done.3, ...), custom_call_target="tpu_custom_call" | custom-call | flops 12884901888 | bytes 25165824 | tf_op jit(solution)/shard_map/contract_rest/pallas_call | solution.py:227
  105.3 0.9 coupling_terms.2
  106.2 0.6 collective-permute-start.3
  106.8 0.3 collective-permute-start.4
  107.1 1.1 collective-permute-start.5
  108.3 0.6 gather_fusion
  108.8 0.7 collective-permute-done.3.refs_1_
  109.5 1.1 collective-permute-done.4.refs_2_
  110.6 1.0 update.2
  111.6 13.1 %all_to_all.15.table_ref = bf16[64,8,128]{2,1,0:T(8,128)(2,1)S(1)} all-to-all(bf16[64,8,128]{2,1,0:T(8,128)(2,1)S(1)} %get-tuple-element.26), channel_id=1, replica_groups=mesh['trip'=8,'row'=4] {'trip','row'}, dimensions={0} | all-to-all | bytes 262144 | tf_op jit(solution)/shard_map/all_to_all | solution.py:380
  124.7 0.9 coupling_terms.3
  125.6 0.3 collective-permute-start.6
  125.9 0.3 collective-permute-start.7
  126.2 1.3 %collective-permute-start.8 = (bf16[12,8,128]{2,1,0:T(8,128)(2,1)S(1)}, bf16[12,8,128]{2,1,0:T(8,128)(2,1)S(1)}, u32[]{:S(2)}, u32[]{:S(2)}) collective-permute-start(bf16[12,8,128]{2,1,0:T(8,128)(2,1)S(1)} %get-tuple-element.30), channel_id=1, source_target_pairs={{0,3},{1,0},{2,1},{3,2},{4,7},{5,4},{6,5},{7,6},{8,11},{9,8},{10,9... | collective-permute-start | bytes 73736 | tf_op jit(solution)/shard_map/ppermute | solution.py:36
  127.6 1.3 %collective-permute-done.6.refs_1_ = bf16[12,8,128]{2,1,0:T(8,128)(2,1)S(1)} collective-permute-done((bf16[12,8,128]{2,1,0:T(8,128)(2,1)S(1)}, bf16[12,8,128]{2,1,0:T(8,128)(2,1)S(1)}, u32[]{:S(2)}, u32[]{:S(2)}) %collective-permute-start.6) | collective-permute-done | bytes 24608 | tf_op jit(solution)/shard_map/ppermute | solution.py:36
  128.9 0.8 collective-permute-done.7.refs_2_
  129.7 0.9 update.3
  130.6 0.3 reshape.97
  131.0 0.4 copy.53
  131.4 0.8 copy.54
  (43 shorter events, 1.2 us)
Async XLA Ops:
  2.7 14.4 %all-to-all-start = ((s32[32,1,128]{2,1,0:T(1,128)}), s32[32,1,128]{2,1,0:T(1,128)S(1)}, u32[]{:S(2)}, u32[]{:S(2)}) async-start(s32[32,1,128]{2,1,0:T(1,128)} %bitcast), calls=%async_computation | async-start | bytes 32768 | tf_op jit(solution)/shard_map/all_to_all | solution.py:380
  11.2 1.2 copy-start.1
  18.9 40.8 %copy-start.5 = (f32[64,768]{1,0:T(8,128)S(1)}, f32[64,768]{1,0:T(8,128)}, u32[]{:S(2)}) copy-start(f32[64,768]{1,0:T(8,128)} %param.12) | copy-start | bytes 589828
  18.9 63.7 %all-to-all-start.1 = ((bf16[64,72,128]{2,1,0:T(8,128)(2,1)}), bf16[64,72,128]{2,1,0:T(8,128)(2,1)S(1)}, u32[]{:S(2)}, u32[]{:S(2)}) async-start(bf16[64,72,128]{2,1,0:T(8,128)(2,1)} %look_up.1), calls=%async_computation.1 | async-start | bytes 2359296 | tf_op jit(solution)/shard_map/all_to_all | solution.py:380
  21.7 37.9 %collective-permute-start.1 = (bf16[64,64,128]{2,1,0:T(8,128)(2,1)S(1)}, bf16[64,64,128]{2,1,0:T(8,128)(2,1)}, u32[]{:S(2)}, u32[]{:S(2)}) collective-permute-start(bf16[64,64,128]{2,1,0:T(8,128)(2,1)S(1)} %copy-done.1), channel_id=1, source_target_pairs={{0,2},{1,3},{2,0},{3,1},{4,6},{5,7},{6,4},{7,5},{8,10},{9,11},{10,... | collective-permute-start | bytes 3145736 | tf_op jit(solution)/shard_map/ppermute | solution.py:364
  23.4 41.4 %collective-permute-start = (bf16[64,64,128]{2,1,0:T(8,128)(2,1)S(1)}, bf16[64,64,128]{2,1,0:T(8,128)(2,1)}, u32[]{:S(2)}, u32[]{:S(2)}) collective-permute-start(bf16[64,64,128]{2,1,0:T(8,128)(2,1)S(1)} %copy-done.1), channel_id=1, source_target_pairs={{0,1},{1,0},{2,3},{3,2},{4,5},{5,4},{6,7},{7,6},{8,9},{9,8},{10,11... | collective-permute-start | bytes 3145736 | tf_op jit(solution)/shard_map/ppermute | solution.py:364
  59.6 5.1 %collective-permute-start.2 = (bf16[64,64,128]{2,1,0:T(8,128)(2,1)}, bf16[64,64,128]{2,1,0:T(8,128)(2,1)}, u32[]{:S(2)}, u32[]{:S(2)}) collective-permute-start(bf16[64,64,128]{2,1,0:T(8,128)(2,1)} %collective-permute-done.1.refs_2_), channel_id=1, source_target_pairs={{0,1},{1,0},{2,3},{3,2},{4,5},{5,4},{6,7},{7,6},{8,9},{9,8},{10,11... | collective-permute-start | bytes 3145736 | tf_op jit(solution)/shard_map/ppermute | solution.py:364
  62.5 2.1 %copy-start.6 = (f32[64,64]{1,0:T(8,128)S(1)}, f32[64,64]{1,0:T(8,128)}, u32[]{:S(2)}) copy-start(f32[64,64]{1,0:T(8,128)} %param.13) | copy-start | bytes 49156
  66.8 4.6 %copy-start = (bf16[24,64,4096]{2,1,0:T(8,128)(2,1)S(1)}, bf16[24,64,4096]{2,1,0:T(8,128)(2,1)}, u32[]{:S(2)}) copy-start(bf16[24,64,4096]{2,1,0:T(8,128)(2,1)} %cubic_ref.1) | copy-start | bytes 37748740
  71.4 12.3 %copy-start.4 = (s32[24]{0:T(128)S(1)}, s32[24]{0:T(128)}, u32[]{:S(2)}) copy-start(s32[24]{0:T(128)} %weights.1) | copy-start | bytes 292
  82.6 1.1 copy-start.2
  83.7 1.3 copy-start.3
  106.2 3.3 %collective-permute-start.3 = (bf16[12,8,128]{2,1,0:T(8,128)(2,1)S(1)}, bf16[12,8,128]{2,1,0:T(8,128)(2,1)S(1)}, u32[]{:S(2)}, u32[]{:S(2)}) collective-permute-start(bf16[12,8,128]{2,1,0:T(8,128)(2,1)S(1)} %get-tuple-element.21), channel_id=1, source_target_pairs={{0,1},{1,2},{2,3},{3,0},{4,5},{5,6},{6,7},{7,4},{8,9},{9,10},{10,1... | collective-permute-start | bytes 73736 | tf_op jit(solution)/shard_map/ppermute | solution.py:36
  106.8 3.8 %collective-permute-start.4 = (bf16[12,8,128]{2,1,0:T(8,128)(2,1)S(1)}, bf16[12,8,128]{2,1,0:T(8,128)(2,1)S(1)}, u32[]{:S(2)}, u32[]{:S(2)}) collective-permute-start(bf16[12,8,128]{2,1,0:T(8,128)(2,1)S(1)} %get-tuple-element.22), channel_id=1, source_target_pairs={{0,2},{1,3},{2,0},{3,1},{4,6},{5,7},{6,4},{7,5},{8,10},{9,11},{10,... | collective-permute-start | bytes 73736 | tf_op jit(solution)/shard_map/ppermute | solution.py:36
  107.1 3.5 %collective-permute-start.5 = (bf16[12,8,128]{2,1,0:T(8,128)(2,1)S(1)}, bf16[12,8,128]{2,1,0:T(8,128)(2,1)S(1)}, u32[]{:S(2)}, u32[]{:S(2)}) collective-permute-start(bf16[12,8,128]{2,1,0:T(8,128)(2,1)S(1)} %get-tuple-element.23), channel_id=1, source_target_pairs={{0,3},{1,0},{2,1},{3,2},{4,7},{5,4},{6,5},{7,6},{8,11},{9,8},{10,9... | collective-permute-start | bytes 73736 | tf_op jit(solution)/shard_map/ppermute | solution.py:36
  125.6 3.3 %collective-permute-start.6 = (bf16[12,8,128]{2,1,0:T(8,128)(2,1)S(1)}, bf16[12,8,128]{2,1,0:T(8,128)(2,1)S(1)}, u32[]{:S(2)}, u32[]{:S(2)}) collective-permute-start(bf16[12,8,128]{2,1,0:T(8,128)(2,1)S(1)} %get-tuple-element.28), channel_id=1, source_target_pairs={{0,1},{1,2},{2,3},{3,0},{4,5},{5,6},{6,7},{7,4},{8,9},{9,10},{10,1... | collective-permute-start | bytes 73736 | tf_op jit(solution)/shard_map/ppermute | solution.py:36
  125.9 3.8 %collective-permute-start.7 = (bf16[12,8,128]{2,1,0:T(8,128)(2,1)S(1)}, bf16[12,8,128]{2,1,0:T(8,128)(2,1)S(1)}, u32[]{:S(2)}, u32[]{:S(2)}) collective-permute-start(bf16[12,8,128]{2,1,0:T(8,128)(2,1)S(1)} %get-tuple-element.29), channel_id=1, source_target_pairs={{0,2},{1,3},{2,0},{3,1},{4,6},{5,7},{6,4},{7,5},{8,10},{9,11},{10,... | collective-permute-start | bytes 73736 | tf_op jit(solution)/shard_map/ppermute | solution.py:36
  126.2 3.5 %collective-permute-start.8 = (bf16[12,8,128]{2,1,0:T(8,128)(2,1)S(1)}, bf16[12,8,128]{2,1,0:T(8,128)(2,1)S(1)}, u32[]{:S(2)}, u32[]{:S(2)}) collective-permute-start(bf16[12,8,128]{2,1,0:T(8,128)(2,1)S(1)} %get-tuple-element.30), channel_id=1, source_target_pairs={{0,3},{1,0},{2,1},{3,2},{4,7},{5,4},{6,5},{7,6},{8,11},{9,8},{10,9... | collective-permute-start | bytes 73736 | tf_op jit(solution)/shard_map/ppermute | solution.py:36

commit v6 on v5

--- a/solution.py
+++ b/solution.py
@@ -38,57 +38,38 @@
     ]
 
 
-def lookup_kernel(queries, table_ref, *found_refs):
-    cap = found_refs[0].shape[0]
-    for d, found_ref in enumerate(found_refs):
-        for slot in range(cap):
-            found_ref[slot] = table_ref[queries[d * cap + slot]]
-
-
-def look_up(queries, table, parts):
-    cap = queries.shape[0] // parts
-    return pl.pallas_call(
+def lookup_kernel(far_queries, row_queries, record_ref, vec_ref, far_ref, *row_refs):
+    for d, row_ref in enumerate(row_refs):
+        for slot in range(row_ref.shape[0]):
+            row_ref[slot] = vec_ref[row_queries[d, slot]]
+    for slot in range(far_ref.shape[0]):
+        far_ref[slot] = record_ref[far_queries[slot]]
+
+
+def look_up(far_queries, row_queries, records, eigvecs):
+    row_count, row_cap = row_queries.shape
+    found = pl.pallas_call(
         lookup_kernel,
-        in_specs=[
-            pl.BlockSpec(memory_space=pltpu.SMEM),
-            pl.BlockSpec(memory_space=pltpu.VMEM),
-        ],
-        out_specs=[pl.BlockSpec(memory_space=pltpu.VMEM)] * parts,
-        out_shape=[jax.ShapeDtypeStruct((cap,) + table.shape[1:], table.dtype)] * parts,
+        in_specs=[pl.BlockSpec(memory_space=pltpu.SMEM)] * 2
+        + [pl.BlockSpec(memory_space=pltpu.VMEM)] * 2,
+        out_specs=[pl.BlockSpec(memory_space=pltpu.VMEM)] * (1 + row_count),
+        out_shape=[
+            jax.ShapeDtypeStruct(far_queries.shape + records.shape[1:], records.dtype)
+        ]
+        + [jax.ShapeDtypeStruct((row_cap,) + eigvecs.shape[1:], eigvecs.dtype)] * row_count,
         compiler_params=pltpu.CompilerParams(vmem_limit_bytes=16 * MIB),
         name="look_up",
-    )(queries, table)
-
-
-def pick_kernel(which, places, *refs):
-    table_refs, out_ref = refs[:-1], refs[-1]
-    for t in range(out_ref.shape[0]):
-        place, wanted = places[t], which[t]
-        found = table_refs[0][place]
-        for block in range(1, len(table_refs)):
-            found = jnp.where(wanted == block, table_refs[block][place], found)
-        out_ref[t] = found
-
-
-def pick(which, places, tables):
-    count = which.shape[0]
-    return pl.pallas_call(
-        pick_kernel,
-        in_specs=[pl.BlockSpec(memory_space=pltpu.SMEM)] * 2
-        + [pl.BlockSpec(memory_space=pltpu.VMEM)] * len(tables),
-        out_specs=pl.BlockSpec(memory_space=pltpu.VMEM),
-        out_shape=jax.ShapeDtypeStruct((count,) + tables[0].shape[1:], tables[0].dtype),
-        compiler_params=pltpu.CompilerParams(vmem_limit_bytes=16 * MIB),
-        name="pick",
-    )(which, places, *tables)
-
-
-def first_kernel(vec_ref, cubic_ref, out_ref):
+    )(far_queries, row_queries, records, eigvecs)
+    return found[0], found[1:]
+
+
+def first_kernel(places, *refs):
+    vec_refs, (cubic_ref, out_ref) = refs[:-2], refs[-2:]
     branches = cubic_ref.shape[1]
     both = 2 * branches
     step = 4
     for pair in range(out_ref.shape[0]):
-        one, two = vec_ref[2 * pair], vec_ref[2 * pair + 1]
+        one, two = vec_refs[2 * pair][0], vec_refs[2 * pair + 1][0]
         none = jnp.zeros((branches, branches), one.dtype)
         mixer = jnp.concatenate(
             [
@@ -110,18 +91,23 @@
                     ]
 
 
-def contract_first(vectors, cubic):
+def contract_first(places, table, cubic):
     count, branches, pairs = cubic.shape
     both = 2 * branches
     group = 2 if count % 4 == 0 else 1
+
+    def vectors(t):
+        return pl.BlockSpec((1, branches, both), lambda s, places: (places[2 * group * s + t], 0, 0))
+
     return pl.pallas_call(
         first_kernel,
-        grid=(count // (2 * group),),
-        in_specs=[
-            pl.BlockSpec((2 * group, branches, both), lambda s: (s, 0, 0)),
-            pl.BlockSpec((2 * group, branches, pairs), lambda s: (s, 0, 0)),
-        ],
-        out_specs=pl.BlockSpec((group, branches, both, both), lambda s: (s, 0, 0, 0)),
+        grid_spec=pltpu.PrefetchScalarGridSpec(
+            num_scalar_prefetch=1,
+            grid=(count // (2 * group),),
+            in_specs=[vectors(t) for t in range(2 * group)]
+            + [pl.BlockSpec((2 * group, branches, pairs), lambda s, places: (s, 0, 0))],
+            out_specs=pl.BlockSpec((group, branches, both, both), lambda s, places: (s, 0, 0, 0)),
+        ),
         out_shape=jax.ShapeDtypeStruct((count // 2, branches, both, both), BF16),
         compiler_params=pltpu.CompilerParams(vmem_limit_bytes=40 * MIB),
         cost_estimate=pl.CostEstimate(
@@ -130,7 +116,7 @@
             transcendentals=0,
         ),
         name="contract_first",
-    )(vectors, cubic)
+    )(places, *[table] * (2 * group), cubic)
 
 
 def second_kernel(stride, group, second_place, third_place, weights, *refs):
@@ -357,13 +343,6 @@
         values = values.reshape(home_rows, 2 * rows, branches)[:, :columns]
         return jnp.swapaxes(values, 1, 2).reshape(home_rows, branches * columns)
 
-    gathered = {0: eigvecs}
-    bit = row_count // 2
-    while bit:
-        pairing = [(i, i ^ bit) for i in range(row_count)]
-        gathered.update({k ^ bit: lax.ppermute(v, "row", pairing) for k, v in gathered.items()})
-        bit //= 2
-
     me = lax.axis_index("trip") * row_count + lax.axis_index("row")
     owner = triplets // home_rows
     local = triplets - owner * home_rows
@@ -397,16 +376,20 @@
     )
     sent_state = jnp.where(one == columns, 1.0, state).astype(BF16)
     records = jnp.concatenate([eigvecs, sent_state], 1)
-    far_table = far(look_up(queries, records, 1)[0])
-    first_vecs = pick(
-        first_dev % row_count ^ lax.axis_index("row"),
-        local[:, 0],
-        [gathered[k] for k in range(row_count)],
+    far_vecs, row_vecs = look_up(queries, jnp.maximum(codes - 1, 0), records, eigvecs)
+    far_table = far(far_vecs)
+    first_table = jnp.concatenate(
+        [row_vecs[0]]
+        + [
+            lax.ppermute(row_vecs[d], "row", [(i, (i - d) % row_count) for i in range(row_count)])
+            for d in range(1, row_count)
+        ],
+        0,
     )
     driven = packed(source)
     rate = jnp.concatenate([base_rate, base_rate], 1)[:, None, :]
-    first_vecs, driven, rate = lax.optimization_barrier((first_vecs, driven, rate))
-    first_part = contract_first(first_vecs, cubic)
+    first_table, driven, rate = lax.optimization_barrier((first_table, driven, rate))
+    first_part = contract_first(row_place, first_table, cubic)
     arrived_state = far_table[:, branches:]
     pairs = contract_rest(second_place, third_place, weights, far_table, first_part)
 

time: 133 us -> 109 us (0.82)
  waiting for transfers between devices: 44.7 us -> 24 us
  Pallas kernels: 39 us -> 36.4 us
  local copies, waits for them, and re-layouts: 17.8 us -> 16.3 us
    ppermute x3, waiting for transfers between devices: 36.2 us -> 15.4 us  [body(): lax.ppermute(row_vecs[d], 'row', [(i, (i - d) % row_count) for i in range...]
    pallas_call x2 -> x1, Pallas kernels: 13.3 us -> 11.7 us  [contract_first(): pl.pallas_call(first_kernel, grid_spec=pltpu.PrefetchScalarGridSpec(num_s...]
    unnamed x17 -> x15, local copies, waits for them, and re-layouts: 10.1 us -> 8.79 us
  transfers between devices with their start and end apart: 11 -> 11, of which waited for: 6 -> 7; matrix products, arithmetic and copies ran while one was open for 6% -> 7% of each run, Pallas kernels for 10% -> 11%
where the time goes in v6:
time: 109 us; the launch traced here: 108 us
  Pallas kernels  36.4 us (33%)
  waiting for transfers between devices  24 us (22%)
  local copies, waits for them, and re-layouts  16.3 us (15%)
  starting transfers between devices  16 us (15%)
  blocking collectives  13.3 us (12%)
  other arithmetic  1.9 us (2%)
    pallas_call x1, Pallas kernels, contract_rest(): pl.pallas_call(functools.partial(second_kernel, stride, group), grid_spec...  20.3 us
    ppermute x3, waiting for transfers between devices, body(): lax.ppermute(row_vecs[d], 'row', [(i, (i - d) % row_count) for i in range...  15.4 us
    all_to_all x1, blocking collectives, far(): return lax.all_to_all(values, AXES, split_axis=0, concat_axis=0, tiled=True)  13.3 us
    pallas_call x1, Pallas kernels, contract_first(): pl.pallas_call(first_kernel, grid_spec=pltpu.PrefetchScalarGridSpec(num_s...  11.7 us
    all_to_all x2, starting transfers between devices, far(): return lax.all_to_all(values, AXES, split_axis=0, concat_axis=0, tiled=True)  10.1 us
    unnamed x15, local copies, waits for them, and re-layouts  8.79 us
    all_to_all x2, waiting for transfers between devices, far(): return lax.all_to_all(values, AXES, split_axis=0, concat_axis=0, tiled=True)  4.5 us
    ppermute x6, waiting for transfers between devices, from_peers(): lax.ppermute(blocks[d], 'row', [(i, (i + d) % count) for i in range(count)])  4.03 us
  transfers between devices with their start and end apart: 11, of which 7 were waited for; matrix products, arithmetic and copies ran while one was open for 7% of the time, Pallas kernels for 11%

profile of v6, /device:TPU:0, one launch (start us, length us, event | category | flops | bytes accessed | tf_op | source)
XLA Modules:
  0.0 108.3 jit_solution(6181702188844919935)
XLA Ops:
  0.0 0.8 copy.41
  0.9 0.1 fusion.2
  1.0 0.2 convert_reduce_fusion.1
  1.3 0.2 convert_reduce_fusion
  1.8 0.8 select_reduce_fusion
  2.6 7.3 %all-to-all-start = ((s32[32,1,128]{2,1,0:T(1,128)}), s32[32,1,128]{2,1,0:T(1,128)S(1)}, u32[]{:S(2)}, u32[]{:S(2)}) async-start(s32[32,1,128]{2,1,0:T(1,128)} %bitcast), calls=%async_computation | async-start | bytes 32768 | tf_op jit(solution)/shard_map/all_to_all | solution.py:359
  10.0 1.1 %copy.46 = f32[64,768]{0,1:T(8,128)S(1)} copy(f32[64,768]{1,0:T(8,128)} %param.11) | data formatting | bytes 393216 | tf_op args[4]
  11.2 0.5 copy.48
  11.7 0.3 reshape.95.refs_4_
  12.0 0.3 copy-done.1
  12.5 4.5 %all-to-all-done = s32[32,1,128]{2,1,0:T(1,128)S(1)} async-done(((s32[32,1,128]{2,1,0:T(1,128)}), s32[32,1,128]{2,1,0:T(1,128)S(1)}, u32[]{:S(2)}, u32[]{:S(2)}) %all-to-all-start) | async-done | bytes 16416 | tf_op jit(solution)/shard_map/all_to_all | solution.py:359
  17.1 0.6 gather_fusion
  17.6 0.1 reshape.92.far_queries.queries
  17.7 0.7 look_up.1
  18.5 1.1 %copy-done.2 = bf16[64,72,128]{2,1,0:T(8,128)(2,1)} copy-done((bf16[64,72,128]{2,1,0:T(8,128)(2,1)}, bf16[64,72,128]{2,1,0:T(8,128)(2,1)S(1)}, u32[]{:S(2)}) %copy-start.2) | copy-done | bytes 1179672
  19.6 2.8 %all-to-all-start.1 = ((bf16[64,72,128]{2,1,0:T(8,128)(2,1)}), bf16[64,72,128]{2,1,0:T(8,128)(2,1)S(1)}, u32[]{:S(2)}, u32[]{:S(2)}) async-start(bf16[64,72,128]{2,1,0:T(8,128)(2,1)} %copy-done.2), calls=%async_computation.1 | async-start | bytes 2359296 | tf_op jit(solution)/shard_map/all_to_all | solution.py:359
  22.5 0.9 copy.49
  23.4 1.0 reshape.96
  24.4 0.8 pad_bitcast_fusion
  25.2 1.5 %copy.51 = f32[64,8,2,64]{3,2,1,0:T(2,128)S(1)} copy(f32[64,8,2,64]{0,1,2,3:T(8,128)} %pad_bitcast_fusion) | data formatting | bytes 524288 | tf_op jit(solution)/shard_map/transpose | solution.py:339
  26.8 0.3 reshape.98.refs_5_
  27.2 1.4 %collective-permute-start = (bf16[12,64,128]{2,1,0:T(8,128)(2,1)S(1)}, bf16[12,64,128]{2,1,0:T(8,128)(2,1)S(1)}, u32[]{:S(2)}, u32[]{:S(2)}) collective-permute-start(bf16[12,64,128]{2,1,0:T(8,128)(2,1)S(1)} %get-tuple-element.26), channel_id=1, source_target_pairs={{0,3},{1,0},{2,1},{3,2},{4,7},{5,4},{6,5},{7,6},{8,11},{9,8},{10,9... | collective-permute-start | bytes 589832 | tf_op jit(solution)/shard_map/ppermute | solution.py:384
  28.6 0.4 collective-permute-start.1
  28.9 0.1 collective-permute-start.2
  29.1 0.2 slice_reduce_fusion
  29.3 7.8 %collective-permute-done = bf16[12,64,128]{2,1,0:T(8,128)(2,1)S(1)} collective-permute-done((bf16[12,64,128]{2,1,0:T(8,128)(2,1)S(1)}, bf16[12,64,128]{2,1,0:T(8,128)(2,1)S(1)}, u32[]{:S(2)}, u32[]{:S(2)}) %collective-permute-start) | collective-permute-done | bytes 196640 | tf_op jit(solution)/shard_map/ppermute | solution.py:384
  37.2 7.6 %collective-permute-done.1 = bf16[12,64,128]{2,1,0:T(8,128)(2,1)S(1)} collective-permute-done((bf16[12,64,128]{2,1,0:T(8,128)(2,1)S(1)}, bf16[12,64,128]{2,1,0:T(8,128)(2,1)S(1)}, u32[]{:S(2)}, u32[]{:S(2)}) %collective-permute-start.1) | collective-permute-done | bytes 196640 | tf_op jit(solution)/shard_map/ppermute | solution.py:384
  44.8 0.1 pad_maximum_fusion.1.refs_0_.refs_1_.refs_2_.refs_3_
  44.9 4.6 %copy-done = bf16[24,64,4096]{2,1,0:T(8,128)(2,1)S(1)} copy-done((bf16[24,64,4096]{2,1,0:T(8,128)(2,1)S(1)}, bf16[24,64,4096]{2,1,0:T(8,128)(2,1)}, u32[]{:S(2)}) %copy-start) | copy-done | bytes 12582936
  49.4 11.7 %contract_first.1.refs_8_ = bf16[12,64,128,128]{3,2,1,0:T(8,128)(2,1)} custom-call(s32[24]{0:T(128)S(1)} %get-tuple-element.47.places.row_place, bf16[48,64,128]{2,1,0:T(8,128)(2,1)S(1)} %pad_maximum_fusion.1.refs_0_.refs_1_.refs_2_.refs_3_, bf16[48,64,128]{2,1,0:T(8,128)(2,1)S(1)} %pad_maximum_fusion.1.refs_0_.refs_1_.refs_2_.refs_3_, ...), custom_call_target="tpu_custom_call" | custom-call | flops 1610612736 | bytes 37748736 | tf_op jit(solution)/shard_map/contract_first/pallas_call | solution.py:102
  61.2 20.3 %contract_rest.1.pair_ref = bf16[24,256,128]{2,1,0:T(8,128)(2,1)S(1)} custom-call(s32[24]{0:T(128)S(1)} %get-tuple-element.44.second_place, s32[24]{0:T(128)S(1)} %get-tuple-element.43.third_place, s32[24]{0:T(128)S(1)} %copy-done.3, bf16[64,72,128]{2,1,0:T(8,128)(2,1)S(1)} %all-to-all-done.1.refs_0_.refs_1_.refs_2_.refs_3_.refs_4_.refs_5_.refs_6_.refs_7_, ...), custom_call_target="tpu_custom_call" | custom-call | flops 12884901888 | bytes 25165824 | tf_op jit(solution)/shard_map/contract_rest/pallas_call | solution.py:213
  81.5 0.9 coupling_terms.2
  82.4 0.6 collective-permute-start.4
  83.1 1.4 %collective-permute-start.5 = (bf16[12,8,128]{2,1,0:T(8,128)(2,1)S(1)}, bf16[12,8,128]{2,1,0:T(8,128)(2,1)S(1)}, u32[]{:S(2)}, u32[]{:S(2)}) collective-permute-start(bf16[12,8,128]{2,1,0:T(8,128)(2,1)S(1)} %get-tuple-element.33), channel_id=1, source_target_pairs={{0,3},{1,0},{2,1},{3,2},{4,7},{5,4},{6,5},{7,6},{8,11},{9,8},{10,9... | collective-permute-start | bytes 73736 | tf_op jit(solution)/shard_map/ppermute | solution.py:36
  84.4 1.2 %collective-permute-done.3.refs_1_ = bf16[12,8,128]{2,1,0:T(8,128)(2,1)S(1)} collective-permute-done((bf16[12,8,128]{2,1,0:T(8,128)(2,1)S(1)}, bf16[12,8,128]{2,1,0:T(8,128)(2,1)S(1)}, u32[]{:S(2)}, u32[]{:S(2)}) %collective-permute-start.3) | collective-permute-done | bytes 24608 | tf_op jit(solution)/shard_map/ppermute | solution.py:36
  85.7 0.7 collective-permute-done.4.refs_2_
  86.3 1.0 update.2
  87.4 13.3 %all_to_all.15.table_ref = bf16[64,8,128]{2,1,0:T(8,128)(2,1)S(1)} all-to-all(bf16[64,8,128]{2,1,0:T(8,128)(2,1)S(1)} %get-tuple-element.36), channel_id=1, replica_groups=mesh['trip'=8,'row'=4] {'trip','row'}, dimensions={0} | all-to-all | bytes 262144 | tf_op jit(solution)/shard_map/all_to_all | solution.py:359
  100.7 0.9 coupling_terms.3
  101.6 0.3 collective-permute-start.6
  101.9 0.3 collective-permute-start.7
  102.2 1.3 %collective-permute-start.8 = (bf16[12,8,128]{2,1,0:T(8,128)(2,1)S(1)}, bf16[12,8,128]{2,1,0:T(8,128)(2,1)S(1)}, u32[]{:S(2)}, u32[]{:S(2)}) collective-permute-start(bf16[12,8,128]{2,1,0:T(8,128)(2,1)S(1)} %get-tuple-element.40), channel_id=1, source_target_pairs={{0,3},{1,0},{2,1},{3,2},{4,7},{5,4},{6,5},{7,6},{8,11},{9,8},{10,9... | collective-permute-start | bytes 73736 | tf_op jit(solution)/shard_map/ppermute | solution.py:36
  103.6 1.3 %collective-permute-done.6.refs_1_ = bf16[12,8,128]{2,1,0:T(8,128)(2,1)S(1)} collective-permute-done((bf16[12,8,128]{2,1,0:T(8,128)(2,1)S(1)}, bf16[12,8,128]{2,1,0:T(8,128)(2,1)S(1)}, u32[]{:S(2)}, u32[]{:S(2)}) %collective-permute-start.6) | collective-permute-done | bytes 24608 | tf_op jit(solution)/shard_map/ppermute | solution.py:36
  104.9 0.8 collective-permute-done.7.refs_2_
  105.7 0.9 update.3
  106.6 0.3 reshape.99
  107.1 0.4 copy.53
  107.5 0.8 copy.54
  (41 shorter events, 1.3 us)
Async XLA Ops:
  2.6 14.4 %all-to-all-start = ((s32[32,1,128]{2,1,0:T(1,128)}), s32[32,1,128]{2,1,0:T(1,128)S(1)}, u32[]{:S(2)}, u32[]{:S(2)}) async-start(s32[32,1,128]{2,1,0:T(1,128)} %bitcast), calls=%async_computation | async-start | bytes 32768 | tf_op jit(solution)/shard_map/all_to_all | solution.py:359
  11.2 1.2 %copy-start.1 = (bf16[64,64,128]{2,1,0:T(8,128)(2,1)S(1)}, bf16[64,64,128]{2,1,0:T(8,128)(2,1)}, u32[]{:S(2)}) copy-start(bf16[64,64,128]{2,1,0:T(8,128)(2,1)} %vec_ref.1) | copy-start | bytes 3145732
  18.5 1.1 %copy-start.2 = (bf16[64,72,128]{2,1,0:T(8,128)(2,1)}, bf16[64,72,128]{2,1,0:T(8,128)(2,1)S(1)}, u32[]{:S(2)}) copy-start(bf16[64,72,128]{2,1,0:T(8,128)(2,1)S(1)} %get-tuple-element.24) | copy-start | bytes 3538948
  19.6 2.9 %copy-start.4 = (f32[64,768]{1,0:T(8,128)S(1)}, f32[64,768]{1,0:T(8,128)}, u32[]{:S(2)}) copy-start(f32[64,768]{1,0:T(8,128)} %param.12) | copy-start | bytes 589828
  19.6 41.6 %all-to-all-start.1 = ((bf16[64,72,128]{2,1,0:T(8,128)(2,1)}), bf16[64,72,128]{2,1,0:T(8,128)(2,1)S(1)}, u32[]{:S(2)}, u32[]{:S(2)}) async-start(bf16[64,72,128]{2,1,0:T(8,128)(2,1)} %copy-done.2), calls=%async_computation.1 | async-start | bytes 2359296 | tf_op jit(solution)/shard_map/all_to_all | solution.py:359
  25.2 4.0 %copy-start.5 = (f32[64,64]{1,0:T(8,128)S(1)}, f32[64,64]{1,0:T(8,128)}, u32[]{:S(2)}) copy-start(f32[64,64]{1,0:T(8,128)} %param.13) | copy-start | bytes 49156
  27.2 10.0 %collective-permute-start = (bf16[12,64,128]{2,1,0:T(8,128)(2,1)S(1)}, bf16[12,64,128]{2,1,0:T(8,128)(2,1)S(1)}, u32[]{:S(2)}, u32[]{:S(2)}) collective-permute-start(bf16[12,64,128]{2,1,0:T(8,128)(2,1)S(1)} %get-tuple-element.26), channel_id=1, source_target_pairs={{0,3},{1,0},{2,1},{3,2},{4,7},{5,4},{6,5},{7,6},{8,11},{9,8},{10,9... | collective-permute-start | bytes 589832 | tf_op jit(solution)/shard_map/ppermute | solution.py:384
  28.6 16.2 %collective-permute-start.1 = (bf16[12,64,128]{2,1,0:T(8,128)(2,1)S(1)}, bf16[12,64,128]{2,1,0:T(8,128)(2,1)S(1)}, u32[]{:S(2)}, u32[]{:S(2)}) collective-permute-start(bf16[12,64,128]{2,1,0:T(8,128)(2,1)S(1)} %get-tuple-element.27), channel_id=1, source_target_pairs={{0,2},{1,3},{2,0},{3,1},{4,6},{5,7},{6,4},{7,5},{8,10},{9,11},{10,... | collective-permute-start | bytes 589832 | tf_op jit(solution)/shard_map/ppermute | solution.py:384
  28.9 15.8 %collective-permute-start.2 = (bf16[12,64,128]{2,1,0:T(8,128)(2,1)S(1)}, bf16[12,64,128]{2,1,0:T(8,128)(2,1)S(1)}, u32[]{:S(2)}, u32[]{:S(2)}) collective-permute-start(bf16[12,64,128]{2,1,0:T(8,128)(2,1)S(1)} %get-tuple-element.28), channel_id=1, source_target_pairs={{0,1},{1,2},{2,3},{3,0},{4,5},{5,6},{6,7},{7,4},{8,9},{9,10},{10,1... | collective-permute-start | bytes 589832 | tf_op jit(solution)/shard_map/ppermute | solution.py:384
  44.9 4.6 %copy-start = (bf16[24,64,4096]{2,1,0:T(8,128)(2,1)S(1)}, bf16[24,64,4096]{2,1,0:T(8,128)(2,1)}, u32[]{:S(2)}) copy-start(bf16[24,64,4096]{2,1,0:T(8,128)(2,1)} %refs_4_.1) | copy-start | bytes 37748740
  49.4 11.8 %copy-start.3 = (s32[24]{0:T(128)S(1)}, s32[24]{0:T(128)}, u32[]{:S(2)}) copy-start(s32[24]{0:T(128)} %weights.1) | copy-start | bytes 292
  82.4 3.3 %collective-permute-start.3 = (bf16[12,8,128]{2,1,0:T(8,128)(2,1)S(1)}, bf16[12,8,128]{2,1,0:T(8,128)(2,1)S(1)}, u32[]{:S(2)}, u32[]{:S(2)}) collective-permute-start(bf16[12,8,128]{2,1,0:T(8,128)(2,1)S(1)} %get-tuple-element.31), channel_id=1, source_target_pairs={{0,1},{1,2},{2,3},{3,0},{4,5},{5,6},{6,7},{7,4},{8,9},{9,10},{10,1... | collective-permute-start | bytes 73736 | tf_op jit(solution)/shard_map/ppermute | solution.py:36
  82.4 3.9 %collective-permute-start.4 = (bf16[12,8,128]{2,1,0:T(8,128)(2,1)S(1)}, bf16[12,8,128]{2,1,0:T(8,128)(2,1)S(1)}, u32[]{:S(2)}, u32[]{:S(2)}) collective-permute-start(bf16[12,8,128]{2,1,0:T(8,128)(2,1)S(1)} %get-tuple-element.32), channel_id=1, source_target_pairs={{0,2},{1,3},{2,0},{3,1},{4,6},{5,7},{6,4},{7,5},{8,10},{9,11},{10,... | collective-permute-start | bytes 73736 | tf_op jit(solution)/shard_map/ppermute | solution.py:36
  83.1 3.3 %collective-permute-start.5 = (bf16[12,8,128]{2,1,0:T(8,128)(2,1)S(1)}, bf16[12,8,128]{2,1,0:T(8,128)(2,1)S(1)}, u32[]{:S(2)}, u32[]{:S(2)}) collective-permute-start(bf16[12,8,128]{2,1,0:T(8,128)(2,1)S(1)} %get-tuple-element.33), channel_id=1, source_target_pairs={{0,3},{1,0},{2,1},{3,2},{4,7},{5,4},{6,5},{7,6},{8,11},{9,8},{10,9... | collective-permute-start | bytes 73736 | tf_op jit(solution)/shard_map/ppermute | solution.py:36
  101.6 3.3 %collective-permute-start.6 = (bf16[12,8,128]{2,1,0:T(8,128)(2,1)S(1)}, bf16[12,8,128]{2,1,0:T(8,128)(2,1)S(1)}, u32[]{:S(2)}, u32[]{:S(2)}) collective-permute-start(bf16[12,8,128]{2,1,0:T(8,128)(2,1)S(1)} %get-tuple-element.38), channel_id=1, source_target_pairs={{0,1},{1,2},{2,3},{3,0},{4,5},{5,6},{6,7},{7,4},{8,9},{9,10},{10,1... | collective-permute-start | bytes 73736 | tf_op jit(solution)/shard_map/ppermute | solution.py:36
  101.9 3.8 %collective-permute-start.7 = (bf16[12,8,128]{2,1,0:T(8,128)(2,1)S(1)}, bf16[12,8,128]{2,1,0:T(8,128)(2,1)S(1)}, u32[]{:S(2)}, u32[]{:S(2)}) collective-permute-start(bf16[12,8,128]{2,1,0:T(8,128)(2,1)S(1)} %get-tuple-element.39), channel_id=1, source_target_pairs={{0,2},{1,3},{2,0},{3,1},{4,6},{5,7},{6,4},{7,5},{8,10},{9,11},{10,... | collective-permute-start | bytes 73736 | tf_op jit(solution)/shard_map/ppermute | solution.py:36
  102.2 3.5 %collective-permute-start.8 = (bf16[12,8,128]{2,1,0:T(8,128)(2,1)S(1)}, bf16[12,8,128]{2,1,0:T(8,128)(2,1)S(1)}, u32[]{:S(2)}, u32[]{:S(2)}) collective-permute-start(bf16[12,8,128]{2,1,0:T(8,128)(2,1)S(1)} %get-tuple-element.40), channel_id=1, source_target_pairs={{0,3},{1,0},{2,1},{3,2},{4,7},{5,4},{6,5},{7,6},{8,11},{9,8},{10,9... | collective-permute-start | bytes 73736 | tf_op jit(solution)/shard_map/ppermute | solution.py:36

commit v7 on v6

--- a/solution.py
+++ b/solution.py
@@ -63,12 +63,18 @@
     return found[0], found[1:]
 
 
+def pairs_per_step(pairs):
+    return next(group for group in (3, 2, 1) if pairs % group == 0)
+
+
 def first_kernel(places, *refs):
     vec_refs, (cubic_ref, out_ref) = refs[:-2], refs[-2:]
+    group = len(vec_refs) // 2
     branches = cubic_ref.shape[1]
     both = 2 * branches
     step = 4
-    for pair in range(out_ref.shape[0]):
+    for pair in range(group):
+        out = group * pl.program_id(0) + pair
         one, two = vec_refs[2 * pair][0], vec_refs[2 * pair + 1][0]
         none = jnp.zeros((branches, branches), one.dtype)
         mixer = jnp.concatenate(
@@ -86,7 +92,7 @@
             mixed = jnp.dot(turned, mixer, preferred_element_type=F32).astype(BF16)
             for j in range(step):
                 for part in range(2):
-                    out_ref[pair, start + j, part * branches : (part + 1) * branches] = mixed[
+                    out_ref[out, start + j, part * branches : (part + 1) * branches] = mixed[
                         j * branches : (j + 1) * branches, part * both : (part + 1) * both
                     ]
 
@@ -94,7 +100,7 @@
 def contract_first(places, table, cubic):
     count, branches, pairs = cubic.shape
     both = 2 * branches
-    group = 2 if count % 4 == 0 else 1
+    group = pairs_per_step(count // 2)
 
     def vectors(t):
         return pl.BlockSpec((1, branches, both), lambda s, places: (places[2 * group * s + t], 0, 0))
@@ -106,10 +112,10 @@
             grid=(count // (2 * group),),
             in_specs=[vectors(t) for t in range(2 * group)]
             + [pl.BlockSpec((2 * group, branches, pairs), lambda s, places: (s, 0, 0))],
-            out_specs=pl.BlockSpec((group, branches, both, both), lambda s, places: (s, 0, 0, 0)),
+            out_specs=pl.BlockSpec(memory_space=pltpu.VMEM),
         ),
-        out_shape=jax.ShapeDtypeStruct((count // 2, branches, both, both), BF16),
-        compiler_params=pltpu.CompilerParams(vmem_limit_bytes=40 * MIB),
+        out_shape=pltpu.VMEM((count // 2, branches, both, both), BF16),
+        compiler_params=pltpu.CompilerParams(vmem_limit_bytes=30 * MIB),
         cost_estimate=pl.CostEstimate(
             flops=2 * count * both * branches * pairs,
             bytes_accessed=2 * count * (both + branches) * pairs,
@@ -141,9 +147,10 @@
 
     def over_k(pair, third_mixer, j):
         turned = scratch[pair % 2]
+        at = group * pl.program_id(0) + pair
         mixed = jnp.dot(
             third_mixer,
-            jnp.concatenate([apart(first_ref[pair, j]), apart(first_ref[pair, j + 1])], 1),
+            jnp.concatenate([apart(first_ref[at, j]), apart(first_ref[at, j + 1])], 1),
             preferred_element_type=F32,
         )
         for half in range(2):
@@ -202,7 +209,7 @@
 
 def contract_rest(second_place, third_place, weights, table, first):
     pairs, branches, both = first.shape[:3]
-    group = 2 if pairs % 2 == 0 else 1
+    group = pairs_per_step(pairs)
     stride = both + 9
 
     def vectors(which, t):
@@ -216,19 +223,19 @@
             num_scalar_prefetch=3,
             grid=(pairs // group,),
             in_specs=[vectors(which, t) for which in range(2) for t in range(2 * group)]
-            + [pl.BlockSpec((group, branches, both, both), lambda s, *places: (s, 0, 0, 0))],
+            + [pl.BlockSpec(memory_space=pltpu.VMEM)],
             out_specs=pl.BlockSpec((2 * group, 2 * both, both), lambda s, *places: (s, 0, 0)),
             scratch_shapes=[pltpu.VMEM((branches * stride, both), F32)] * 2,
         ),
         out_shape=jax.ShapeDtypeStruct((2 * pairs, 2 * both, both), BF16),
-        compiler_params=pltpu.CompilerParams(vmem_limit_bytes=44 * MIB),
+        compiler_params=pltpu.CompilerParams(vmem_limit_bytes=30 * MIB),
         cost_estimate=pl.CostEstimate(
             flops=16 * pairs * both * both * branches * branches,
             bytes_accessed=2 * pairs * both * both * branches,
             transcendentals=0,
         ),
         name="contract_rest",
-    )(second_place, third_place, weights, *[table] * (4 * group), first)
+    )(second_place, third_place, weights, *[table] * (4 * group), pltpu.with_memory_space_constraint(first, pltpu.VMEM))
 
 
 def terms_kernel(
@@ -378,16 +385,14 @@
     records = jnp.concatenate([eigvecs, sent_state], 1)
     far_vecs, row_vecs = look_up(queries, jnp.maximum(codes - 1, 0), records, eigvecs)
     far_table = far(far_vecs)
-    first_table = jnp.concatenate(
-        [row_vecs[0]]
-        + [
-            lax.ppermute(row_vecs[d], "row", [(i, (i - d) % row_count) for i in range(row_count)])
-            for d in range(1, row_count)
-        ],
-        0,
-    )
+    first_vecs = [row_vecs[0]] + [
+        lax.ppermute(row_vecs[d], "row", [(i, (i - d) % row_count) for i in range(row_count)])
+        for d in range(1, row_count)
+    ]
+    source, base_rate, first_vecs[1] = lax.optimization_barrier((source, base_rate, first_vecs[1]))
     driven = packed(source)
     rate = jnp.concatenate([base_rate, base_rate], 1)[:, None, :]
+    first_table = jnp.concatenate(first_vecs, 0)
     first_table, driven, rate = lax.optimization_barrier((first_table, driven, rate))
     first_part = contract_first(row_place, first_table, cubic)
     arrived_state = far_table[:, branches:]

time: 109 us -> 124 us (1.14)
  local copies, waits for them, and re-layouts: 16.3 us -> 27.4 us
  waiting for transfers between devices: 24 us -> 26.8 us
  Pallas kernels: 36.4 us -> 34.3 us
  other arithmetic: 1.9 us -> 3.32 us
    unnamed x15 -> x24, local copies, waits for them, and re-layouts: 8.79 us -> 21.1 us
    ppermute x3, waiting for transfers between devices: 15.4 us -> 18.2 us  [body(): lax.ppermute(row_vecs[d], 'row', [(i, (i - d) % row_count) for i in range...]
    transpose x4, local copies, waits for them, and re-layouts: 2.92 us -> 1.11 us  [packed(): return jnp.swapaxes(values, 1, 2).reshape(home_rows, rows, 2 * branches)]
  transfers between devices with their start and end apart: 11 -> 11, of which waited for: 7 -> 7; matrix products, arithmetic and copies ran while one was open for 7% -> 4% of each run, Pallas kernels for 11% -> 9%
where the time goes in v7:
time: 124 us; the launch traced here: 122 us
  Pallas kernels  34.3 us (28%)
  local copies, waits for them, and re-layouts  27.4 us (22%)
  waiting for transfers between devices  26.8 us (22%)
  starting transfers between devices  16.5 us (13%)
  blocking collectives  13.6 us (11%)
  other arithmetic  3.32 us (3%)
    unnamed x24, local copies, waits for them, and re-layouts  21.1 us
    pallas_call x1, Pallas kernels, contract_rest(): pl.pallas_call(functools.partial(second_kernel, stride, group), grid_spec...  19.5 us
    ppermute x3, waiting for transfers between devices, body(): lax.ppermute(row_vecs[d], 'row', [(i, (i - d) % row_count) for i in range...  18.2 us
    all_to_all x1, blocking collectives, far(): return lax.all_to_all(values, AXES, split_axis=0, concat_axis=0, tiled=True)  13.6 us
    all_to_all x2, starting transfers between devices, far(): return lax.all_to_all(values, AXES, split_axis=0, concat_axis=0, tiled=True)  10.8 us
    pallas_call x1, Pallas kernels, contract_first(): pl.pallas_call(first_kernel, grid_spec=pltpu.PrefetchScalarGridSpec(num_s...  10.5 us
    all_to_all x2, waiting for transfers between devices, far(): return lax.all_to_all(values, AXES, split_axis=0, concat_axis=0, tiled=True)  4.49 us
    ppermute x6, waiting for transfers between devices, from_peers(): lax.ppermute(blocks[d], 'row', [(i, (i + d) % count) for i in range(count)])  4.18 us
  transfers between devices with their start and end apart: 11, of which 7 were waited for; matrix products, arithmetic and copies ran while one was open for 4% of the time, Pallas kernels for 9%

profile of v7, /device:TPU:0, one launch (start us, length us, event | category | flops | bytes accessed | tf_op | source)
XLA Modules:
  0.0 122.4 jit_solution(17987583408743111649)
XLA Ops:
  0.0 0.8 copy.41
  1.0 0.2 convert_reduce_fusion.1
  1.3 0.2 convert_reduce_fusion
  1.6 0.5 fusion.7
  2.3 0.8 select_reduce_fusion
  3.1 7.3 %all-to-all-start = ((s32[32,1,128]{2,1,0:T(1,128)}), s32[32,1,128]{2,1,0:T(1,128)S(1)}, u32[]{:S(2)}, u32[]{:S(2)}) async-start(s32[32,1,128]{2,1,0:T(1,128)} %bitcast), calls=%async_computation | async-start | bytes 32768 | tf_op jit(solution)/shard_map/all_to_all | solution.py:366
  10.5 1.1 copy.46
  11.7 0.5 copy.48
  12.2 0.3 reshape.95.refs_4_
  12.6 0.3 copy-done.4
  13.0 4.5 %all-to-all-done = s32[32,1,128]{2,1,0:T(1,128)S(1)} async-done(((s32[32,1,128]{2,1,0:T(1,128)}), s32[32,1,128]{2,1,0:T(1,128)S(1)}, u32[]{:S(2)}, u32[]{:S(2)}) %all-to-all-start) | async-done | bytes 16416 | tf_op jit(solution)/shard_map/all_to_all | solution.py:366
  17.6 0.6 gather_fusion
  18.3 0.7 look_up.1
  19.0 1.0 copy-done.5
  20.0 3.5 %all-to-all-start.1 = ((bf16[64,72,128]{2,1,0:T(8,128)(2,1)}), bf16[64,72,128]{2,1,0:T(8,128)(2,1)}, u32[]{:S(2)}, u32[]{:S(2)}) async-start(bf16[64,72,128]{2,1,0:T(8,128)(2,1)} %copy-done.5), calls=%async_computation.1 | async-start | bytes 2359296 | tf_op jit(solution)/shard_map/all_to_all | solution.py:366
  23.6 1.4 %collective-permute-start = (bf16[12,64,128]{2,1,0:T(8,128)(2,1)S(1)}, bf16[12,64,128]{2,1,0:T(8,128)(2,1)S(1)}, u32[]{:S(2)}, u32[]{:S(2)}) collective-permute-start(bf16[12,64,128]{2,1,0:T(8,128)(2,1)S(1)} %get-tuple-element.29), channel_id=1, source_target_pairs={{0,3},{1,0},{2,1},{3,2},{4,7},{5,4},{6,5},{7,6},{8,11},{9,8},{10,9... | collective-permute-start | bytes 589832 | tf_op jit(solution)/shard_map/ppermute | solution.py:389
  25.1 0.7 slice_reduce_fusion
  25.8 0.4 collective-permute-start.1
  26.1 0.1 collective-permute-start.2
  26.3 11.8 %collective-permute-done = bf16[12,64,128]{2,1,0:T(8,128)(2,1)S(1)} collective-permute-done((bf16[12,64,128]{2,1,0:T(8,128)(2,1)S(1)}, bf16[12,64,128]{2,1,0:T(8,128)(2,1)S(1)}, u32[]{:S(2)}, u32[]{:S(2)}) %collective-permute-start) | collective-permute-done | bytes 196640 | tf_op jit(solution)/shard_map/ppermute | solution.py:389
  38.1 0.2 copy.49
  38.4 0.5 copy.51
  38.9 0.3 reshape.98.refs_5_
  39.3 6.4 %collective-permute-done.1 = bf16[12,64,128]{2,1,0:T(8,128)(2,1)S(1)} collective-permute-done((bf16[12,64,128]{2,1,0:T(8,128)(2,1)S(1)}, bf16[12,64,128]{2,1,0:T(8,128)(2,1)S(1)}, u32[]{:S(2)}, u32[]{:S(2)}) %collective-permute-start.1) | collective-permute-done | bytes 196640 | tf_op jit(solution)/shard_map/ppermute | solution.py:389
  45.7 1.0 pad_maximum_fusion.1.refs_0_.refs_1_.refs_2_.refs_3_.refs_4_.refs_5_
  46.6 10.5 %contract_first.1.refs_12_ = bf16[12,64,128,128]{3,2,1,0:T(8,128)(2,1)S(1)} custom-call(s32[24]{0:T(128)} %get-tuple-element.53.places.row_place, bf16[48,64,128]{2,1,0:T(8,128)(2,1)} %pad_maximum_fusion.1.refs_0_.refs_1_.refs_2_.refs_3_.refs_4_.refs_5_, bf16[48,64,128]{2,1,0:T(8,128)(2,1)} %pad_maximum_fusion.1.refs_0_.refs_1_.refs_2_.refs_3_.refs_4_.refs_5_, ...), custom_call_target="tpu_custom_call" | custom-call | flops 1610612736 | bytes 37748736 | tf_op jit(solution)/shard_map/contract_first/pallas_call | solution.py:108
  57.2 8.3 %copy-done = bf16[12,64,128,128]{3,2,1,0:T(8,128)(2,1)} copy-done((bf16[12,64,128,128]{3,2,1,0:T(8,128)(2,1)}, bf16[12,64,128,128]{3,2,1,0:T(8,128)(2,1)S(1)}, u32[]{:S(2)}) %copy-start) | copy-done | bytes 25165848
  65.5 0.9 slice.35.table_ref
  66.4 8.1 %copy-done.1 = bf16[12,64,128,128]{3,2,1,0:T(8,128)(2,1)S(1)} copy-done((bf16[12,64,128,128]{3,2,1,0:T(8,128)(2,1)S(1)}, bf16[12,64,128,128]{3,2,1,0:T(8,128)(2,1)}, u32[]{:S(2)}) %copy-start.1) | copy-done | bytes 25165848
  74.6 19.5 %contract_rest.1.pair_ref = bf16[24,256,128]{2,1,0:T(8,128)(2,1)} custom-call(s32[24]{0:T(128)} %get-tuple-element.50.second_place, s32[24]{0:T(128)} %get-tuple-element.49.third_place, s32[24]{0:T(128)} %weights.1, bf16[64,72,128]{2,1,0:T(8,128)(2,1)} %all-to-all-done.1.refs_0_.refs_1_.refs_2_.refs_3_.refs_4_.refs_5_.refs_6_.refs_7_.refs_8_.refs_9_.refs_10_.refs_11_, ...), custom_call_target="tpu_custom_call" | custom-call | flops 12884901888 | bytes 25165824 | tf_op jit(solution)/shard_map/contract_rest/pallas_call | solution.py:220
  94.1 1.4 %copy-done.2 = bf16[24,256,128]{2,1,0:T(8,128)(2,1)S(1)} copy-done((bf16[24,256,128]{2,1,0:T(8,128)(2,1)S(1)}, bf16[24,256,128]{2,1,0:T(8,128)(2,1)}, u32[]{:S(2)}) %copy-start.2) | copy-done | bytes 1572888
  95.5 0.9 coupling_terms.2
  96.5 0.4 collective-permute-start.4
  96.9 1.4 %collective-permute-start.5 = (bf16[12,8,128]{2,1,0:T(8,128)(2,1)S(1)}, bf16[12,8,128]{2,1,0:T(8,128)(2,1)S(1)}, u32[]{:S(2)}, u32[]{:S(2)}) collective-permute-start(bf16[12,8,128]{2,1,0:T(8,128)(2,1)S(1)} %get-tuple-element.39), channel_id=1, source_target_pairs={{0,3},{1,0},{2,1},{3,2},{4,7},{5,4},{6,5},{7,6},{8,11},{9,8},{10,9... | collective-permute-start | bytes 73736 | tf_op jit(solution)/shard_map/ppermute | solution.py:36
  98.3 1.4 %collective-permute-done.3.refs_1_ = bf16[12,8,128]{2,1,0:T(8,128)(2,1)S(1)} collective-permute-done((bf16[12,8,128]{2,1,0:T(8,128)(2,1)S(1)}, bf16[12,8,128]{2,1,0:T(8,128)(2,1)S(1)}, u32[]{:S(2)}, u32[]{:S(2)}) %collective-permute-start.3) | collective-permute-done | bytes 24608 | tf_op jit(solution)/shard_map/ppermute | solution.py:36
  99.7 0.7 collective-permute-done.4.refs_2_
  100.4 0.9 update.2
  101.3 13.6 %all_to_all.15.table_ref = bf16[64,8,128]{2,1,0:T(8,128)(2,1)S(1)} all-to-all(bf16[64,8,128]{2,1,0:T(8,128)(2,1)S(1)} %get-tuple-element.42), channel_id=1, replica_groups=mesh['trip'=8,'row'=4] {'trip','row'}, dimensions={0} | all-to-all | bytes 262144 | tf_op jit(solution)/shard_map/all_to_all | solution.py:366
  115.0 0.9 coupling_terms.3
  115.9 0.3 collective-permute-start.6
  116.1 0.3 collective-permute-start.7
  116.5 1.3 %collective-permute-start.8 = (bf16[12,8,128]{2,1,0:T(8,128)(2,1)S(1)}, bf16[12,8,128]{2,1,0:T(8,128)(2,1)S(1)}, u32[]{:S(2)}, u32[]{:S(2)}) collective-permute-start(bf16[12,8,128]{2,1,0:T(8,128)(2,1)S(1)} %get-tuple-element.46), channel_id=1, source_target_pairs={{0,3},{1,0},{2,1},{3,2},{4,7},{5,4},{6,5},{7,6},{8,11},{9,8},{10,9... | collective-permute-start | bytes 73736 | tf_op jit(solution)/shard_map/ppermute | solution.py:36
  117.8 1.3 %collective-permute-done.6.refs_1_ = bf16[12,8,128]{2,1,0:T(8,128)(2,1)S(1)} collective-permute-done((bf16[12,8,128]{2,1,0:T(8,128)(2,1)S(1)}, bf16[12,8,128]{2,1,0:T(8,128)(2,1)S(1)}, u32[]{:S(2)}, u32[]{:S(2)}) %collective-permute-start.6) | collective-permute-done | bytes 24608 | tf_op jit(solution)/shard_map/ppermute | solution.py:36
  119.2 0.8 collective-permute-done.7.refs_2_
  120.0 0.8 update.3
  120.8 0.3 reshape.99
  121.2 0.4 copy.53
  121.6 0.8 copy.54
  (51 shorter events, 1.6 us)
Async XLA Ops:
  3.1 14.4 %all-to-all-start = ((s32[32,1,128]{2,1,0:T(1,128)}), s32[32,1,128]{2,1,0:T(1,128)S(1)}, u32[]{:S(2)}, u32[]{:S(2)}) async-start(s32[32,1,128]{2,1,0:T(1,128)} %bitcast), calls=%async_computation | async-start | bytes 32768 | tf_op jit(solution)/shard_map/all_to_all | solution.py:366
  11.7 1.2 %copy-start.4 = (bf16[64,64,128]{2,1,0:T(8,128)(2,1)S(1)}, bf16[64,64,128]{2,1,0:T(8,128)(2,1)}, u32[]{:S(2)}) copy-start(bf16[64,64,128]{2,1,0:T(8,128)(2,1)} %vec_ref.1) | copy-start | bytes 3145732
  19.0 1.0 copy-start.5
  20.0 18.1 %copy-start.9 = (f32[64,768]{1,0:T(8,128)S(1)}, f32[64,768]{1,0:T(8,128)}, u32[]{:S(2)}) copy-start(f32[64,768]{1,0:T(8,128)} %param.12) | copy-start | bytes 589828
  20.0 45.5 %all-to-all-start.1 = ((bf16[64,72,128]{2,1,0:T(8,128)(2,1)}), bf16[64,72,128]{2,1,0:T(8,128)(2,1)}, u32[]{:S(2)}, u32[]{:S(2)}) async-start(bf16[64,72,128]{2,1,0:T(8,128)(2,1)} %copy-done.5), calls=%async_computation.1 | async-start | bytes 2359296 | tf_op jit(solution)/shard_map/all_to_all | solution.py:366
  23.6 14.4 %collective-permute-start = (bf16[12,64,128]{2,1,0:T(8,128)(2,1)S(1)}, bf16[12,64,128]{2,1,0:T(8,128)(2,1)S(1)}, u32[]{:S(2)}, u32[]{:S(2)}) collective-permute-start(bf16[12,64,128]{2,1,0:T(8,128)(2,1)S(1)} %get-tuple-element.29), channel_id=1, source_target_pairs={{0,3},{1,0},{2,1},{3,2},{4,7},{5,4},{6,5},{7,6},{8,11},{9,8},{10,9... | collective-permute-start | bytes 589832 | tf_op jit(solution)/shard_map/ppermute | solution.py:389
  25.8 19.9 %collective-permute-start.1 = (bf16[12,64,128]{2,1,0:T(8,128)(2,1)S(1)}, bf16[12,64,128]{2,1,0:T(8,128)(2,1)S(1)}, u32[]{:S(2)}, u32[]{:S(2)}) collective-permute-start(bf16[12,64,128]{2,1,0:T(8,128)(2,1)S(1)} %get-tuple-element.31), channel_id=1, source_target_pairs={{0,2},{1,3},{2,0},{3,1},{4,6},{5,7},{6,4},{7,5},{8,10},{9,11},{10,... | collective-permute-start | bytes 589832 | tf_op jit(solution)/shard_map/ppermute | solution.py:389
  26.1 19.5 %collective-permute-start.2 = (bf16[12,64,128]{2,1,0:T(8,128)(2,1)S(1)}, bf16[12,64,128]{2,1,0:T(8,128)(2,1)S(1)}, u32[]{:S(2)}, u32[]{:S(2)}) collective-permute-start(bf16[12,64,128]{2,1,0:T(8,128)(2,1)S(1)} %get-tuple-element.32), channel_id=1, source_target_pairs={{0,1},{1,2},{2,3},{3,0},{4,5},{5,6},{6,7},{7,4},{8,9},{9,10},{10,1... | collective-permute-start | bytes 589832 | tf_op jit(solution)/shard_map/ppermute | solution.py:389
  38.4 0.8 copy-start.10
  57.2 8.3 %copy-start = (bf16[12,64,128,128]{3,2,1,0:T(8,128)(2,1)}, bf16[12,64,128,128]{3,2,1,0:T(8,128)(2,1)S(1)}, u32[]{:S(2)}) copy-start(bf16[12,64,128,128]{3,2,1,0:T(8,128)(2,1)S(1)} %contract_first.1.refs_12_) | copy-start | bytes 75497472
  66.4 8.2 %copy-start.1 = (bf16[12,64,128,128]{3,2,1,0:T(8,128)(2,1)S(1)}, bf16[12,64,128,128]{3,2,1,0:T(8,128)(2,1)}, u32[]{:S(2)}) copy-start(bf16[12,64,128,128]{3,2,1,0:T(8,128)(2,1)} %copy-done) | copy-start | bytes 75497472
  74.6 19.5 %copy-start.6 = (s32[24]{0:T(128)S(1)}, s32[24]{0:T(128)}, u32[]{:S(2)}) copy-start(s32[24]{0:T(128)} %get-tuple-element.53.places.row_place) | copy-start | bytes 292
  74.6 19.5 %copy-start.7 = (s32[24]{0:T(128)S(1)}, s32[24]{0:T(128)}, u32[]{:S(2)}) copy-start(s32[24]{0:T(128)} %get-tuple-element.49.third_place) | copy-start | bytes 292
  74.6 19.5 %copy-start.8 = (s32[24]{0:T(128)S(1)}, s32[24]{0:T(128)}, u32[]{:S(2)}) copy-start(s32[24]{0:T(128)} %get-tuple-element.50.second_place) | copy-start | bytes 292
  94.1 1.4 %copy-start.2 = (bf16[24,256,128]{2,1,0:T(8,128)(2,1)S(1)}, bf16[24,256,128]{2,1,0:T(8,128)(2,1)}, u32[]{:S(2)}) copy-start(bf16[24,256,128]{2,1,0:T(8,128)(2,1)} %contract_rest.1.pair_ref) | copy-start | bytes 4718596
  95.5 19.4 %copy-start.3 = (bf16[24,256,128]{2,1,0:T(8,128)(2,1)S(1)}, bf16[24,256,128]{2,1,0:T(8,128)(2,1)}, u32[]{:S(2)}) copy-start(bf16[24,256,128]{2,1,0:T(8,128)(2,1)} %contract_rest.1.pair_ref) | copy-start | bytes 4718596
  96.4 3.3 %collective-permute-start.3 = (bf16[12,8,128]{2,1,0:T(8,128)(2,1)S(1)}, bf16[12,8,128]{2,1,0:T(8,128)(2,1)S(1)}, u32[]{:S(2)}, u32[]{:S(2)}) collective-permute-start(bf16[12,8,128]{2,1,0:T(8,128)(2,1)S(1)} %get-tuple-element.37), channel_id=1, source_target_pairs={{0,1},{1,2},{2,3},{3,0},{4,5},{5,6},{6,7},{7,4},{8,9},{9,10},{10,1... | collective-permute-start | bytes 73736 | tf_op jit(solution)/shard_map/ppermute | solution.py:36
  96.5 3.9 %collective-permute-start.4 = (bf16[12,8,128]{2,1,0:T(8,128)(2,1)S(1)}, bf16[12,8,128]{2,1,0:T(8,128)(2,1)S(1)}, u32[]{:S(2)}, u32[]{:S(2)}) collective-permute-start(bf16[12,8,128]{2,1,0:T(8,128)(2,1)S(1)} %get-tuple-element.38), channel_id=1, source_target_pairs={{0,2},{1,3},{2,0},{3,1},{4,6},{5,7},{6,4},{7,5},{8,10},{9,11},{10,... | collective-permute-start | bytes 73736 | tf_op jit(solution)/shard_map/ppermute | solution.py:36
  96.9 3.5 %collective-permute-start.5 = (bf16[12,8,128]{2,1,0:T(8,128)(2,1)S(1)}, bf16[12,8,128]{2,1,0:T(8,128)(2,1)S(1)}, u32[]{:S(2)}, u32[]{:S(2)}) collective-permute-start(bf16[12,8,128]{2,1,0:T(8,128)(2,1)S(1)} %get-tuple-element.39), channel_id=1, source_target_pairs={{0,3},{1,0},{2,1},{3,2},{4,7},{5,4},{6,5},{7,6},{8,11},{9,8},{10,9... | collective-permute-start | bytes 73736 | tf_op jit(solution)/shard_map/ppermute | solution.py:36
  115.9 3.3 %collective-permute-start.6 = (bf16[12,8,128]{2,1,0:T(8,128)(2,1)S(1)}, bf16[12,8,128]{2,1,0:T(8,128)(2,1)S(1)}, u32[]{:S(2)}, u32[]{:S(2)}) collective-permute-start(bf16[12,8,128]{2,1,0:T(8,128)(2,1)S(1)} %get-tuple-element.44), channel_id=1, source_target_pairs={{0,1},{1,2},{2,3},{3,0},{4,5},{5,6},{6,7},{7,4},{8,9},{9,10},{10,1... | collective-permute-start | bytes 73736 | tf_op jit(solution)/shard_map/ppermute | solution.py:36
  116.1 3.8 %collective-permute-start.7 = (bf16[12,8,128]{2,1,0:T(8,128)(2,1)S(1)}, bf16[12,8,128]{2,1,0:T(8,128)(2,1)S(1)}, u32[]{:S(2)}, u32[]{:S(2)}) collective-permute-start(bf16[12,8,128]{2,1,0:T(8,128)(2,1)S(1)} %get-tuple-element.45), channel_id=1, source_target_pairs={{0,2},{1,3},{2,0},{3,1},{4,6},{5,7},{6,4},{7,5},{8,10},{9,11},{10,... | collective-permute-start | bytes 73736 | tf_op jit(solution)/shard_map/ppermute | solution.py:36
  116.5 3.5 %collective-permute-start.8 = (bf16[12,8,128]{2,1,0:T(8,128)(2,1)S(1)}, bf16[12,8,128]{2,1,0:T(8,128)(2,1)S(1)}, u32[]{:S(2)}, u32[]{:S(2)}) collective-permute-start(bf16[12,8,128]{2,1,0:T(8,128)(2,1)S(1)} %get-tuple-element.46), channel_id=1, source_target_pairs={{0,3},{1,0},{2,1},{3,2},{4,7},{5,4},{6,5},{7,6},{8,11},{9,8},{10,9... | collective-permute-start | bytes 73736 | tf_op jit(solution)/shard_map/ppermute | solution.py:36

commit v8 on v7

--- a/solution.py
+++ b/solution.py
@@ -74,7 +74,6 @@
     both = 2 * branches
     step = 4
     for pair in range(group):
-        out = group * pl.program_id(0) + pair
         one, two = vec_refs[2 * pair][0], vec_refs[2 * pair + 1][0]
         none = jnp.zeros((branches, branches), one.dtype)
         mixer = jnp.concatenate(
@@ -92,7 +91,7 @@
             mixed = jnp.dot(turned, mixer, preferred_element_type=F32).astype(BF16)
             for j in range(step):
                 for part in range(2):
-                    out_ref[out, start + j, part * branches : (part + 1) * branches] = mixed[
+                    out_ref[pair, start + j, part * branches : (part + 1) * branches] = mixed[
                         j * branches : (j + 1) * branches, part * both : (part + 1) * both
                     ]
 
@@ -112,12 +111,12 @@
             grid=(count // (2 * group),),
             in_specs=[vectors(t) for t in range(2 * group)]
             + [pl.BlockSpec((2 * group, branches, pairs), lambda s, places: (s, 0, 0))],
-            out_specs=pl.BlockSpec(memory_space=pltpu.VMEM),
+            out_specs=pl.BlockSpec((group, branches, both, both), lambda s, places: (s, 0, 0, 0)),
         ),
-        out_shape=pltpu.VMEM((count // 2, branches, both, both), BF16),
-        compiler_params=pltpu.CompilerParams(vmem_limit_bytes=30 * MIB),
+        out_shape=jax.ShapeDtypeStruct((count // 2, branches, both, both), BF16),
+        compiler_params=pltpu.CompilerParams(vmem_limit_bytes=60 * MIB),
         cost_estimate=pl.CostEstimate(
-            flops=2 * count * both * branches * pairs,
+            flops=20 * 2 * count * both * branches * pairs,
             bytes_accessed=2 * count * (both + branches) * pairs,
             transcendentals=0,
         ),
@@ -147,10 +146,9 @@
 
     def over_k(pair, third_mixer, j):
         turned = scratch[pair % 2]
-        at = group * pl.program_id(0) + pair
         mixed = jnp.dot(
             third_mixer,
-            jnp.concatenate([apart(first_ref[at, j]), apart(first_ref[at, j + 1])], 1),
+            jnp.concatenate([apart(first_ref[pair, j]), apart(first_ref[pair, j + 1])], 1),
             preferred_element_type=F32,
         )
         for half in range(2):
@@ -223,19 +221,19 @@
             num_scalar_prefetch=3,
             grid=(pairs // group,),
             in_specs=[vectors(which, t) for which in range(2) for t in range(2 * group)]
-            + [pl.BlockSpec(memory_space=pltpu.VMEM)],
+            + [pl.BlockSpec((group, branches, both, both), lambda s, *places: (s, 0, 0, 0))],
             out_specs=pl.BlockSpec((2 * group, 2 * both, both), lambda s, *places: (s, 0, 0)),
             scratch_shapes=[pltpu.VMEM((branches * stride, both), F32)] * 2,
         ),
         out_shape=jax.ShapeDtypeStruct((2 * pairs, 2 * both, both), BF16),
-        compiler_params=pltpu.CompilerParams(vmem_limit_bytes=30 * MIB),
+        compiler_params=pltpu.CompilerParams(vmem_limit_bytes=44 * MIB),
         cost_estimate=pl.CostEstimate(
             flops=16 * pairs * both * both * branches * branches,
             bytes_accessed=2 * pairs * both * both * branches,
             transcendentals=0,
         ),
         name="contract_rest",
-    )(second_place, third_place, weights, *[table] * (4 * group), pltpu.with_memory_space_constraint(first, pltpu.VMEM))
+    )(second_place, third_place, weights, *[table] * (4 * group), first)
 
 
 def terms_kernel(

time: 124 us -> 100 us (0.81)
  local copies, waits for them, and re-layouts: 27.4 us -> 8.87 us
  waiting for transfers between devices: 26.8 us -> 17.7 us
  Pallas kernels: 34.3 us -> 40.7 us
  blocking collectives: 13.6 us -> 11.3 us
    unnamed x24 -> x16, local copies, waits for them, and re-layouts: 21.1 us -> 3.98 us
    ppermute x3, waiting for transfers between devices: 18.2 us -> 9.35 us  [body(): lax.ppermute(row_vecs[d], 'row', [(i, (i - d) % row_count) for i in range...]
    pallas_call x1, Pallas kernels: 10.5 us -> 16.7 us  [contract_first(): pl.pallas_call(first_kernel, grid_spec=pltpu.PrefetchScalarGridSpec(num_s...]
    all_to_all x1, blocking collectives: 13.6 us -> 11.3 us  [far(): return lax.all_to_all(values, AXES, split_axis=0, concat_axis=0, tiled=True)]
  transfers between devices with their start and end apart: 11 -> 11, of which waited for: 7 -> 8; matrix products, arithmetic and copies ran while one was open for 4% -> 6% of each run, Pallas kernels for 9% -> 17%
where the time goes in v8:
time: 100 us; the launch traced here: 99.4 us
  Pallas kernels  40.7 us (41%)
  waiting for transfers between devices  17.7 us (18%)
  starting transfers between devices  16 us (16%)
  blocking collectives  11.3 us (11%)
  local copies, waits for them, and re-layouts  8.87 us (9%)
  other arithmetic  4.49 us (4%)
    pallas_call x1, Pallas kernels, contract_rest(): pl.pallas_call(functools.partial(second_kernel, stride, group), grid_spec...  19.7 us
    pallas_call x1, Pallas kernels, contract_first(): pl.pallas_call(first_kernel, grid_spec=pltpu.PrefetchScalarGridSpec(num_s...  16.7 us
    all_to_all x1, blocking collectives, far(): return lax.all_to_all(values, AXES, split_axis=0, concat_axis=0, tiled=True)  11.3 us
    all_to_all x2, starting transfers between devices, far(): return lax.all_to_all(values, AXES, split_axis=0, concat_axis=0, tiled=True)  10.1 us
    ppermute x3, waiting for transfers between devices, body(): lax.ppermute(row_vecs[d], 'row', [(i, (i - d) % row_count) for i in range...  9.35 us
    all_to_all x2, waiting for transfers between devices, far(): return lax.all_to_all(values, AXES, split_axis=0, concat_axis=0, tiled=True)  4.4 us
    ppermute x6, starting transfers between devices, from_peers(): lax.ppermute(blocks[d], 'row', [(i, (i + d) % count) for i in range(count)])  4.34 us
    unnamed x16, local copies, waits for them, and re-layouts  3.98 us
  transfers between devices with their start and end apart: 11, of which 8 were waited for; matrix products, arithmetic and copies ran while one was open for 6% of the time, Pallas kernels for 17%

profile of v8, /device:TPU:0, one launch (start us, length us, event | category | flops | bytes accessed | tf_op | source)
XLA Modules:
  0.0 99.4 jit_solution(16897192502390528815)
XLA Ops:
  0.0 0.8 copy.41
  0.9 0.1 fusion.2
  1.0 0.2 convert_reduce_fusion.1
  1.2 0.1 reshape.89
  1.3 0.2 convert_reduce_fusion
  1.6 0.6 fusion.7
  2.4 0.8 select_reduce_fusion
  3.2 7.3 %all-to-all-start = ((s32[32,1,128]{2,1,0:T(1,128)}), s32[32,1,128]{2,1,0:T(1,128)S(1)}, u32[]{:S(2)}, u32[]{:S(2)}) async-start(s32[32,1,128]{2,1,0:T(1,128)} %bitcast), calls=%async_computation | async-start | bytes 32768 | tf_op jit(solution)/shard_map/all_to_all | solution.py:364
  10.5 1.1 %copy.46 = f32[64,768]{0,1:T(8,128)S(1)} copy(f32[64,768]{1,0:T(8,128)} %param.11) | data formatting | bytes 393216 | tf_op args[4]
  11.7 0.5 copy.48
  12.2 0.3 reshape.95.refs_4_
  12.6 0.3 copy-done
  12.9 0.1 pad_maximum_fusion.record_ref
  13.2 4.4 %all-to-all-done = s32[32,1,128]{2,1,0:T(1,128)S(1)} async-done(((s32[32,1,128]{2,1,0:T(1,128)}), s32[32,1,128]{2,1,0:T(1,128)S(1)}, u32[]{:S(2)}, u32[]{:S(2)}) %all-to-all-start) | async-done | bytes 16416 | tf_op jit(solution)/shard_map/all_to_all | solution.py:364
  17.6 0.6 gather_fusion
  18.2 0.1 reshape.92.far_queries.queries
  18.3 0.7 look_up.1
  19.0 1.1 %copy-done.1 = bf16[64,72,128]{2,1,0:T(8,128)(2,1)} copy-done((bf16[64,72,128]{2,1,0:T(8,128)(2,1)}, bf16[64,72,128]{2,1,0:T(8,128)(2,1)S(1)}, u32[]{:S(2)}) %copy-start.1) | copy-done | bytes 1179672
  20.2 0.2 slice_reduce_fusion
  20.4 1.6 %collective-permute-start.1 = (bf16[12,64,128]{2,1,0:T(8,128)(2,1)S(1)}, bf16[12,64,128]{2,1,0:T(8,128)(2,1)}, u32[]{:S(2)}, u32[]{:S(2)}) collective-permute-start(bf16[12,64,128]{2,1,0:T(8,128)(2,1)S(1)} %get-tuple-element.31), channel_id=1, source_target_pairs={{0,2},{1,3},{2,0},{3,1},{4,6},{5,7},{6,4},{7,5},{8,10},{9,11},{10,... | collective-permute-start | bytes 589832 | tf_op jit(solution)/shard_map/ppermute | solution.py:387
  21.9 2.8 %all-to-all-start.1 = ((bf16[64,72,128]{2,1,0:T(8,128)(2,1)}), bf16[64,72,128]{2,1,0:T(8,128)(2,1)S(1)}, u32[]{:S(2)}, u32[]{:S(2)}) async-start(bf16[64,72,128]{2,1,0:T(8,128)(2,1)} %copy-done.1), calls=%async_computation.1 | async-start | bytes 2359296 | tf_op jit(solution)/shard_map/all_to_all | solution.py:364
  24.7 0.4 collective-permute-done
  25.1 0.7 copy-done.4
  25.8 0.2 copy.49
  26.1 0.5 copy.51
  26.6 0.3 reshape.98.refs_5_
  27.0 7.8 %collective-permute-done.1 = bf16[12,64,128]{2,1,0:T(8,128)(2,1)} collective-permute-done((bf16[12,64,128]{2,1,0:T(8,128)(2,1)S(1)}, bf16[12,64,128]{2,1,0:T(8,128)(2,1)}, u32[]{:S(2)}, u32[]{:S(2)}) %collective-permute-start.1) | collective-permute-done | bytes 196640 | tf_op jit(solution)/shard_map/ppermute | solution.py:387
  34.8 1.1 %collective-permute-done.2 = bf16[12,64,128]{2,1,0:T(8,128)(2,1)} collective-permute-done((bf16[12,64,128]{2,1,0:T(8,128)(2,1)S(1)}, bf16[12,64,128]{2,1,0:T(8,128)(2,1)}, u32[]{:S(2)}, u32[]{:S(2)}) %collective-permute-start.2) | collective-permute-done | bytes 196640 | tf_op jit(solution)/shard_map/ppermute | solution.py:387
  36.0 2.1 %pad_maximum_fusion.1.refs_0_.refs_1_.refs_2_.refs_3_.refs_4_.refs_5_ = bf16[48,64,128]{2,1,0:T(8,128)(2,1)} fusion(bf16[12,64,128]{2,1,0:T(8,128)(2,1)} %collective-permute-done.2, bf16[12,64,128]{2,1,0:T(8,128)(2,1)} %collective-permute-done.1, bf16[12,64,128]{2,1,0:T(8,128)(2,1)} %copy-done.4, bf16[12,64,128]{2,1,0:T(8,128)(2,1)S(1)} %get-tuple-element.28), kind=kLoop, calls=%fused_computation.4 | loop fusion | flops 1179648 | bytes 1572864 | tf_op jit(solution)/shard_map/concatenate | solution.py:393
  38.1 16.7 %contract_first.1.refs_12_ = bf16[12,64,128,128]{3,2,1,0:T(8,128)(2,1)} custom-call(s32[24]{0:T(128)} %get-tuple-element.53.places.row_place, bf16[48,64,128]{2,1,0:T(8,128)(2,1)} %pad_maximum_fusion.1.refs_0_.refs_1_.refs_2_.refs_3_.refs_4_.refs_5_, bf16[48,64,128]{2,1,0:T(8,128)(2,1)} %pad_maximum_fusion.1.refs_0_.refs_1_.refs_2_.refs_3_.refs_4_.refs_5_, ...), custom_call_target="tpu_custom_call" | custom-call | flops 32212254720 | bytes 37748736 | tf_op jit(solution)/shard_map/contract_first/pallas_call | solution.py:107
  54.8 19.7 %contract_rest.1.pair_ref = bf16[24,256,128]{2,1,0:T(8,128)(2,1)S(1)} custom-call(s32[24]{0:T(128)S(1)} %get-tuple-element.50.second_place, s32[24]{0:T(128)S(1)} %get-tuple-element.49.third_place, s32[24]{0:T(128)S(1)} %copy-done.3, ...), custom_call_target="tpu_custom_call" | custom-call | flops 12884901888 | bytes 25165824 | tf_op jit(solution)/shard_map/contract_rest/pallas_call | solution.py:218
  74.5 0.9 coupling_terms.2
  75.5 0.9 collective-permute-start.4
  76.4 1.4 %collective-permute-start.5 = (bf16[12,8,128]{2,1,0:T(8,128)(2,1)S(1)}, bf16[12,8,128]{2,1,0:T(8,128)(2,1)S(1)}, u32[]{:S(2)}, u32[]{:S(2)}) collective-permute-start(bf16[12,8,128]{2,1,0:T(8,128)(2,1)S(1)} %get-tuple-element.39), channel_id=1, source_target_pairs={{0,3},{1,0},{2,1},{3,2},{4,7},{5,4},{6,5},{7,6},{8,11},{9,8},{10,9... | collective-permute-start | bytes 73736 | tf_op jit(solution)/shard_map/ppermute | solution.py:36
  77.8 0.9 collective-permute-done.3.refs_1_
  78.7 0.9 collective-permute-done.4.refs_2_
  79.6 1.0 update.2
  80.6 11.3 %all_to_all.15.table_ref = bf16[64,8,128]{2,1,0:T(8,128)(2,1)S(1)} all-to-all(bf16[64,8,128]{2,1,0:T(8,128)(2,1)S(1)} %get-tuple-element.42), channel_id=1, replica_groups=mesh['trip'=8,'row'=4] {'trip','row'}, dimensions={0} | all-to-all | bytes 262144 | tf_op jit(solution)/shard_map/all_to_all | solution.py:364
  91.9 0.9 coupling_terms.3
  92.8 0.3 collective-permute-start.6
  93.0 0.3 collective-permute-start.7
  93.4 1.3 %collective-permute-start.8 = (bf16[12,8,128]{2,1,0:T(8,128)(2,1)S(1)}, bf16[12,8,128]{2,1,0:T(8,128)(2,1)S(1)}, u32[]{:S(2)}, u32[]{:S(2)}) collective-permute-start(bf16[12,8,128]{2,1,0:T(8,128)(2,1)S(1)} %get-tuple-element.46), channel_id=1, source_target_pairs={{0,3},{1,0},{2,1},{3,2},{4,7},{5,4},{6,5},{7,6},{8,11},{9,8},{10,9... | collective-permute-start | bytes 73736 | tf_op jit(solution)/shard_map/ppermute | solution.py:36
  94.7 1.3 %collective-permute-done.6.refs_1_ = bf16[12,8,128]{2,1,0:T(8,128)(2,1)S(1)} collective-permute-done((bf16[12,8,128]{2,1,0:T(8,128)(2,1)S(1)}, bf16[12,8,128]{2,1,0:T(8,128)(2,1)S(1)}, u32[]{:S(2)}, u32[]{:S(2)}) %collective-permute-start.6) | collective-permute-done | bytes 24608 | tf_op jit(solution)/shard_map/ppermute | solution.py:36
  96.1 0.8 collective-permute-done.7.refs_2_
  96.9 0.8 update.3
  97.7 0.3 reshape.99
  98.1 0.4 copy.53
  98.5 0.8 copy.54
  (43 shorter events, 1.2 us)
Async XLA Ops:
  3.2 14.4 %all-to-all-start = ((s32[32,1,128]{2,1,0:T(1,128)}), s32[32,1,128]{2,1,0:T(1,128)S(1)}, u32[]{:S(2)}, u32[]{:S(2)}) async-start(s32[32,1,128]{2,1,0:T(1,128)} %bitcast), calls=%async_computation | async-start | bytes 32768 | tf_op jit(solution)/shard_map/all_to_all | solution.py:364
  11.7 1.2 %copy-start = (bf16[64,64,128]{2,1,0:T(8,128)(2,1)S(1)}, bf16[64,64,128]{2,1,0:T(8,128)(2,1)}, u32[]{:S(2)}) copy-start(bf16[64,64,128]{2,1,0:T(8,128)(2,1)} %vec_ref.1) | copy-start | bytes 3145732
  19.0 1.1 %copy-start.1 = (bf16[64,72,128]{2,1,0:T(8,128)(2,1)}, bf16[64,72,128]{2,1,0:T(8,128)(2,1)S(1)}, u32[]{:S(2)}) copy-start(bf16[64,72,128]{2,1,0:T(8,128)(2,1)S(1)} %get-tuple-element.27) | copy-start | bytes 3538948
  20.1 5.0 %collective-permute-start = (bf16[12,64,128]{2,1,0:T(8,128)(2,1)S(1)}, bf16[12,64,128]{2,1,0:T(8,128)(2,1)S(1)}, u32[]{:S(2)}, u32[]{:S(2)}) collective-permute-start(bf16[12,64,128]{2,1,0:T(8,128)(2,1)S(1)} %get-tuple-element.29), channel_id=1, source_target_pairs={{0,3},{1,0},{2,1},{3,2},{4,7},{5,4},{6,5},{7,6},{8,11},{9,8},{10,9... | collective-permute-start | bytes 589832 | tf_op jit(solution)/shard_map/ppermute | solution.py:387
  20.4 14.4 %collective-permute-start.1 = (bf16[12,64,128]{2,1,0:T(8,128)(2,1)S(1)}, bf16[12,64,128]{2,1,0:T(8,128)(2,1)}, u32[]{:S(2)}, u32[]{:S(2)}) collective-permute-start(bf16[12,64,128]{2,1,0:T(8,128)(2,1)S(1)} %get-tuple-element.31), channel_id=1, source_target_pairs={{0,2},{1,3},{2,0},{3,1},{4,6},{5,7},{6,4},{7,5},{8,10},{9,11},{10,... | collective-permute-start | bytes 589832 | tf_op jit(solution)/shard_map/ppermute | solution.py:387
  21.9 14.0 %collective-permute-start.2 = (bf16[12,64,128]{2,1,0:T(8,128)(2,1)S(1)}, bf16[12,64,128]{2,1,0:T(8,128)(2,1)}, u32[]{:S(2)}, u32[]{:S(2)}) collective-permute-start(bf16[12,64,128]{2,1,0:T(8,128)(2,1)S(1)} %get-tuple-element.32), channel_id=1, source_target_pairs={{0,1},{1,2},{2,3},{3,0},{4,5},{5,6},{6,7},{7,4},{8,9},{9,10},{10,1... | collective-permute-start | bytes 589832 | tf_op jit(solution)/shard_map/ppermute | solution.py:387
  21.9 3.9 %copy-start.5 = (f32[64,768]{1,0:T(8,128)S(1)}, f32[64,768]{1,0:T(8,128)}, u32[]{:S(2)}) copy-start(f32[64,768]{1,0:T(8,128)} %param.12) | copy-start | bytes 589828
  21.9 32.8 %all-to-all-start.1 = ((bf16[64,72,128]{2,1,0:T(8,128)(2,1)}), bf16[64,72,128]{2,1,0:T(8,128)(2,1)S(1)}, u32[]{:S(2)}, u32[]{:S(2)}) async-start(bf16[64,72,128]{2,1,0:T(8,128)(2,1)} %copy-done.1), calls=%async_computation.1 | async-start | bytes 2359296 | tf_op jit(solution)/shard_map/all_to_all | solution.py:364
  25.1 0.7 copy-start.4
  26.1 0.8 copy-start.6
  38.1 16.7 %copy-start.3 = (s32[24]{0:T(128)S(1)}, s32[24]{0:T(128)}, u32[]{:S(2)}) copy-start(s32[24]{0:T(128)} %weights.1) | copy-start | bytes 292
  54.8 19.8 %copy-start.2 = (s32[24]{0:T(128)S(1)}, s32[24]{0:T(128)}, u32[]{:S(2)}) copy-start(s32[24]{0:T(128)} %get-tuple-element.53.places.row_place) | copy-start | bytes 292
  75.4 3.3 %collective-permute-start.3 = (bf16[12,8,128]{2,1,0:T(8,128)(2,1)S(1)}, bf16[12,8,128]{2,1,0:T(8,128)(2,1)S(1)}, u32[]{:S(2)}, u32[]{:S(2)}) collective-permute-start(bf16[12,8,128]{2,1,0:T(8,128)(2,1)S(1)} %get-tuple-element.37), channel_id=1, source_target_pairs={{0,1},{1,2},{2,3},{3,0},{4,5},{5,6},{6,7},{7,4},{8,9},{9,10},{10,1... | collective-permute-start | bytes 73736 | tf_op jit(solution)/shard_map/ppermute | solution.py:36
  75.5 4.1 %collective-permute-start.4 = (bf16[12,8,128]{2,1,0:T(8,128)(2,1)S(1)}, bf16[12,8,128]{2,1,0:T(8,128)(2,1)S(1)}, u32[]{:S(2)}, u32[]{:S(2)}) collective-permute-start(bf16[12,8,128]{2,1,0:T(8,128)(2,1)S(1)} %get-tuple-element.38), channel_id=1, source_target_pairs={{0,2},{1,3},{2,0},{3,1},{4,6},{5,7},{6,4},{7,5},{8,10},{9,11},{10,... | collective-permute-start | bytes 73736 | tf_op jit(solution)/shard_map/ppermute | solution.py:36
  76.4 3.2 %collective-permute-start.5 = (bf16[12,8,128]{2,1,0:T(8,128)(2,1)S(1)}, bf16[12,8,128]{2,1,0:T(8,128)(2,1)S(1)}, u32[]{:S(2)}, u32[]{:S(2)}) collective-permute-start(bf16[12,8,128]{2,1,0:T(8,128)(2,1)S(1)} %get-tuple-element.39), channel_id=1, source_target_pairs={{0,3},{1,0},{2,1},{3,2},{4,7},{5,4},{6,5},{7,6},{8,11},{9,8},{10,9... | collective-permute-start | bytes 73736 | tf_op jit(solution)/shard_map/ppermute | solution.py:36
  92.8 3.3 %collective-permute-start.6 = (bf16[12,8,128]{2,1,0:T(8,128)(2,1)S(1)}, bf16[12,8,128]{2,1,0:T(8,128)(2,1)S(1)}, u32[]{:S(2)}, u32[]{:S(2)}) collective-permute-start(bf16[12,8,128]{2,1,0:T(8,128)(2,1)S(1)} %get-tuple-element.44), channel_id=1, source_target_pairs={{0,1},{1,2},{2,3},{3,0},{4,5},{5,6},{6,7},{7,4},{8,9},{9,10},{10,1... | collective-permute-start | bytes 73736 | tf_op jit(solution)/shard_map/ppermute | solution.py:36
  93.0 3.8 %collective-permute-start.7 = (bf16[12,8,128]{2,1,0:T(8,128)(2,1)S(1)}, bf16[12,8,128]{2,1,0:T(8,128)(2,1)S(1)}, u32[]{:S(2)}, u32[]{:S(2)}) collective-permute-start(bf16[12,8,128]{2,1,0:T(8,128)(2,1)S(1)} %get-tuple-element.45), channel_id=1, source_target_pairs={{0,2},{1,3},{2,0},{3,1},{4,6},{5,7},{6,4},{7,5},{8,10},{9,11},{10,... | collective-permute-start | bytes 73736 | tf_op jit(solution)/shard_map/ppermute | solution.py:36
  93.4 3.5 %collective-permute-start.8 = (bf16[12,8,128]{2,1,0:T(8,128)(2,1)S(1)}, bf16[12,8,128]{2,1,0:T(8,128)(2,1)S(1)}, u32[]{:S(2)}, u32[]{:S(2)}) collective-permute-start(bf16[12,8,128]{2,1,0:T(8,128)(2,1)S(1)} %get-tuple-element.46), channel_id=1, source_target_pairs={{0,3},{1,0},{2,1},{3,2},{4,7},{5,4},{6,5},{7,6},{8,11},{9,8},{10,9... | collective-permute-start | bytes 73736 | tf_op jit(solution)/shard_map/ppermute | solution.py:36

commit v9 on v8

--- a/solution.py
+++ b/solution.py
@@ -16,51 +16,103 @@
 MIB = 2**20
 
 
-def ranks_of(target):
-    extent = target.shape[0]
-    matches = target[:, None] == target[None, :]
-    earlier = lax.broadcasted_iota(jnp.int32, (extent, extent), 1) < lax.broadcasted_iota(
-        jnp.int32, (extent, extent), 0
+def prepare_kernel(home_rows, far_cap, row_count, row_cap, triplets_ref, message_ref, places_ref):
+    count, devices = triplets_ref.shape[1], message_ref.shape[0]
+    sub = lax.broadcasted_iota(jnp.int32, (count, count), 0)
+    lane = lax.broadcasted_iota(jnp.int32, (count, count), 1)
+    same, earlier = sub == lane, sub < lane
+
+    def whole_part(values, size):
+        return jnp.floor((values.astype(F32) + 0.5) * (1.0 / size)).astype(jnp.int32)
+
+    wanted = [triplets_ref[which : which + 1, :] for which in range(3)]
+    owner = [whole_part(values, home_rows) for values in wanted]
+    local = [values - own * home_rows for values, own in zip(wanted, owner)]
+    upright = [jnp.sum(jnp.where(same, own, 0), 1, keepdims=True) for own in owner]
+
+    def matches(one, two, mask):
+        return (mask & (upright[one] == owner[two])).astype(jnp.int32)
+
+    rank = [
+        jnp.sum(found, 0, keepdims=True)
+        for found in (
+            matches(0, 0, earlier),
+            matches(1, 1, earlier) + matches(2, 1, earlier),
+            matches(1, 2, earlier | same) + matches(2, 2, earlier),
+        )
+    ]
+    device = lax.broadcasted_iota(jnp.int32, (devices, count), 0)
+    slot = lax.broadcasted_iota(jnp.int32, (LANES, count), 0)
+    kind, precision = (
+        (BF16, None) if home_rows <= 256 else (F32, lax.Precision.HIGHEST)
     )
-    return jnp.sum((matches & earlier).astype(jnp.int32), axis=1)
-
-
-def pack_ints(places, values, extent):
-    onehot = lax.broadcasted_iota(jnp.int32, (extent, places.shape[0]), 0) == places[None, :]
-    return jnp.sum(jnp.where(onehot, values[None, :], 0), axis=1)
+    message = jnp.zeros((devices, LANES), F32)
+    for which in range(3):
+        value, at = (local[0] + 1, rank[0] + far_cap) if which == 0 else (local[which], rank[which])
+        message = message + lax.dot_general(
+            jnp.where(device == owner[which], 1.0, 0.0).astype(kind),
+            jnp.where(slot == at, value.astype(F32), 0.0).astype(kind),
+            (((1,), (1,)), ((), ())),
+            precision=precision,
+            preferred_element_type=F32,
+        )
+    message_ref[...] = (message + 0.5).astype(jnp.int32)
+    apart = (owner[0] - row_count * whole_part(owner[0], row_count)) ^ lax.axis_index("row")
+    places_ref[...] = jnp.zeros_like(places_ref)
+    places_ref[0:1, :count] = apart * row_cap + rank[0]
+    for which in range(1, 3):
+        places_ref[which : which + 1, :count] = owner[which] * far_cap + rank[which]
+
+
+def prepare(triplets, home_rows, devices, far_cap, row_count, row_cap):
+    return pl.pallas_call(
+        functools.partial(prepare_kernel, home_rows, far_cap, row_count, row_cap),
+        in_specs=[pl.BlockSpec(memory_space=pltpu.VMEM)],
+        out_specs=[pl.BlockSpec(memory_space=pltpu.VMEM)] * 2,
+        out_shape=[
+            jax.ShapeDtypeStruct((devices, LANES), jnp.int32),
+            jax.ShapeDtypeStruct((8, LANES), jnp.int32),
+        ],
+        name="prepare",
+    )(triplets.T)
+
+
+def to_peer(values, bits, count):
+    return lax.ppermute(values, "row", [(i, i ^ bits) for i in range(count)])
 
 
 def from_peers(blocks):
-    count = len(blocks)
-    return [blocks[0]] + [
-        lax.ppermute(blocks[d], "row", [(i, (i + d) % count) for i in range(count)])
-        for d in range(1, count)
-    ]
-
-
-def lookup_kernel(far_queries, row_queries, record_ref, vec_ref, far_ref, *row_refs):
-    for d, row_ref in enumerate(row_refs):
-        for slot in range(row_ref.shape[0]):
-            row_ref[slot] = vec_ref[row_queries[d, slot]]
+    return [blocks[0]] + [to_peer(blocks[k], k, len(blocks)) for k in range(1, len(blocks))]
+
+
+def lookup_kernel(far_cap, row_count, heard, record_ref, vec_ref, far_ref, near_ref, away_ref):
+    half = row_count // 2
+    cap = near_ref.shape[0] // half
+    base = lax.axis_index("trip") * row_count
+    for k in range(row_count):
+        peer = base + (lax.axis_index("row") ^ k)
+        row_ref = near_ref if k < half else away_ref
+        for slot in range(cap):
+            code = heard[peer, far_cap + slot]
+            row_ref[k % half * cap + slot] = vec_ref[jnp.maximum(code - 1, 0)]
     for slot in range(far_ref.shape[0]):
-        far_ref[slot] = record_ref[far_queries[slot]]
-
-
-def look_up(far_queries, row_queries, records, eigvecs):
-    row_count, row_cap = row_queries.shape
-    found = pl.pallas_call(
-        lookup_kernel,
-        in_specs=[pl.BlockSpec(memory_space=pltpu.SMEM)] * 2
+        far_ref[slot] = record_ref[heard[slot // far_cap, slot % far_cap]]
+
+
+def look_up(heard, records, eigvecs, far_cap, row_count, row_cap):
+    row_shape = (row_count // 2 * row_cap,) + eigvecs.shape[1:]
+    return pl.pallas_call(
+        functools.partial(lookup_kernel, far_cap, row_count),
+        in_specs=[pl.BlockSpec(memory_space=pltpu.SMEM)]
         + [pl.BlockSpec(memory_space=pltpu.VMEM)] * 2,
-        out_specs=[pl.BlockSpec(memory_space=pltpu.VMEM)] * (1 + row_count),
+        out_specs=[pl.BlockSpec(memory_space=pltpu.VMEM)] * 3,
         out_shape=[
-            jax.ShapeDtypeStruct(far_queries.shape + records.shape[1:], records.dtype)
+            jax.ShapeDtypeStruct((heard.shape[0] * far_cap,) + records.shape[1:], records.dtype)
         ]
-        + [jax.ShapeDtypeStruct((row_cap,) + eigvecs.shape[1:], eigvecs.dtype)] * row_count,
+        + [jax.ShapeDtypeStruct(row_shape, eigvecs.dtype)] * 2,
         compiler_params=pltpu.CompilerParams(vmem_limit_bytes=16 * MIB),
         name="look_up",
-    )(far_queries, row_queries, records, eigvecs)
-    return found[0], found[1:]
+    )(heard, records, eigvecs)
 
 
 def pairs_per_step(pairs):
@@ -102,7 +154,7 @@
     group = pairs_per_step(count // 2)
 
     def vectors(t):
-        return pl.BlockSpec((1, branches, both), lambda s, places: (places[2 * group * s + t], 0, 0))
+        return pl.BlockSpec((1, branches, both), lambda s, places: (places[0, 2 * group * s + t], 0, 0))
 
     return pl.pallas_call(
         first_kernel,
@@ -114,9 +166,9 @@
             out_specs=pl.BlockSpec((group, branches, both, both), lambda s, places: (s, 0, 0, 0)),
         ),
         out_shape=jax.ShapeDtypeStruct((count // 2, branches, both, both), BF16),
-        compiler_params=pltpu.CompilerParams(vmem_limit_bytes=60 * MIB),
+        compiler_params=pltpu.CompilerParams(vmem_limit_bytes=40 * MIB),
         cost_estimate=pl.CostEstimate(
-            flops=20 * 2 * count * both * branches * pairs,
+            flops=8 * 2 * count * both * branches * pairs,
             bytes_accessed=2 * count * (both + branches) * pairs,
             transcendentals=0,
         ),
@@ -124,16 +176,16 @@
     )(places, *[table] * (2 * group), cubic)
 
 
-def second_kernel(stride, group, second_place, third_place, weights, *refs):
-    second_refs, third_refs = refs[: 2 * group], refs[2 * group : 4 * group]
-    first_ref, pair_ref, *scratch = refs[4 * group :]
+def second_kernel(stride, group, places, weights, *refs):
+    table_ref, first_ref, pair_ref, *scratch = refs
     branches = first_ref.shape[1]
     both = 2 * branches
 
-    def mixer(vec_refs):
+    def mixer(which, pair):
         columns = []
-        for vec_ref in vec_refs:
-            vectors = vec_ref[0].astype(F32).T
+        for t in range(2):
+            place = places[which, 2 * (group * pl.program_id(0) + pair) + t]
+            vectors = table_ref[place, :branches].astype(F32).T
             real, imag = vectors[:branches], vectors[branches:]
             columns += [jnp.concatenate([real, imag], 0), jnp.concatenate([-imag, real], 0)]
         return jnp.concatenate(columns, 1).astype(BF16)
@@ -192,9 +244,9 @@
     for phase in range(group + 1):
         before = phase - 1
         if phase < group:
-            third_mixer = mixer(third_refs[2 * phase : 2 * phase + 2])
+            third_mixer = mixer(2, phase)
         if phase > 0:
-            second_mixer = mixer(second_refs[2 * before : 2 * before + 2])
+            second_mixer = mixer(1, before)
             total = jnp.zeros((branches, both), F32)
         for at in range(0, branches, 2):
             if phase > 0:
@@ -205,22 +257,17 @@
             finish(before, total)
 
 
-def contract_rest(second_place, third_place, weights, table, first):
+def contract_rest(places, weights, table, first):
     pairs, branches, both = first.shape[:3]
     group = pairs_per_step(pairs)
     stride = both + 9
 
-    def vectors(which, t):
-        return pl.BlockSpec(
-            (1, branches, both), lambda s, *places: (places[which][2 * group * s + t], 0, 0)
-        )
-
     return pl.pallas_call(
         functools.partial(second_kernel, stride, group),
         grid_spec=pltpu.PrefetchScalarGridSpec(
-            num_scalar_prefetch=3,
+            num_scalar_prefetch=2,
             grid=(pairs // group,),
-            in_specs=[vectors(which, t) for which in range(2) for t in range(2 * group)]
+            in_specs=[pl.BlockSpec(memory_space=pltpu.VMEM)]
             + [pl.BlockSpec((group, branches, both, both), lambda s, *places: (s, 0, 0, 0))],
             out_specs=pl.BlockSpec((2 * group, 2 * both, both), lambda s, *places: (s, 0, 0)),
             scratch_shapes=[pltpu.VMEM((branches * stride, both), F32)] * 2,
@@ -233,41 +280,42 @@
             transcendentals=0,
         ),
         name="contract_rest",
-    )(second_place, third_place, weights, *[table] * (4 * group), first)
-
-
-def terms_kernel(
-    columns, second_place, third_place, row_place, table_ref, pair_ref, *rest
-):
+    )(places, weights, table, first)
+
+
+def terms_kernel(columns, start, places, table_ref, pair_ref, *rest):
     out_refs, packed = rest[:-1], rest[-1]
-    rows, lanes = table_ref.shape[1:]
+    rows, lanes = packed.shape[1:]
+    state = slice(start, start + rows)
     packed[...] = jnp.zeros_like(packed)
     row = lax.broadcasted_iota(jnp.int32, (rows, lanes), 0)
     lane = lax.broadcasted_iota(jnp.int32, (rows, lanes), 1)
     is_rest = (row == columns - rows + 1) & (lane >= lanes // 2)
     for t in range(pair_ref.shape[0]):
-        states = jnp.concatenate([table_ref[second_place[t]], table_ref[third_place[t]]], 1)
+        states = jnp.concatenate(
+            [table_ref[places[1, t], state], table_ref[places[2, t], state]], 1
+        )
         terms = jnp.dot(states, pair_ref[t], preferred_element_type=F32)
         short = terms.astype(BF16).astype(F32)
         terms = jnp.where(is_rest, pltpu.roll(terms - short, 1, 0), terms)
-        packed[row_place[t]] = terms.astype(BF16)
+        packed[places[0, t]] = terms.astype(BF16)
     cap = out_refs[0].shape[0]
     for d, out_ref in enumerate(out_refs):
         out_ref[...] = packed[d * cap : (d + 1) * cap]
 
 
-def coupling_terms(second_place, third_place, row_place, table, pairs, columns, row_count, row_cap):
-    rows, lanes = table.shape[1:]
-    return pl.pallas_call(
-        functools.partial(terms_kernel, columns),
-        in_specs=[pl.BlockSpec(memory_space=pltpu.SMEM)] * 3
+def coupling_terms(places, table, start, pairs, columns, row_count, row_cap):
+    rows, lanes = table.shape[1] - start, table.shape[2]
+    return pl.pallas_call(
+        functools.partial(terms_kernel, columns, start),
+        in_specs=[pl.BlockSpec(memory_space=pltpu.SMEM)]
         + [pl.BlockSpec(memory_space=pltpu.VMEM)] * 2,
         out_specs=[pl.BlockSpec(memory_space=pltpu.VMEM)] * row_count,
         out_shape=[jax.ShapeDtypeStruct((row_cap, rows, lanes), BF16)] * row_count,
         scratch_shapes=[pltpu.VMEM((row_count * row_cap, rows, lanes), BF16)],
         compiler_params=pltpu.CompilerParams(vmem_limit_bytes=16 * MIB),
         name="coupling_terms",
-    )(second_place, third_place, row_place, table, pairs)
+    )(places, table, pairs)
 
 
 def update_kernel(columns, first, last, codes, queries, *rest):
@@ -348,32 +396,16 @@
         values = values.reshape(home_rows, 2 * rows, branches)[:, :columns]
         return jnp.swapaxes(values, 1, 2).reshape(home_rows, branches * columns)
 
-    me = lax.axis_index("trip") * row_count + lax.axis_index("row")
-    owner = triplets // home_rows
-    local = triplets - owner * home_rows
-    first_dev, far_owner = owner[:, 0], owner[:, 1:].reshape(-1)
-    row_rank = ranks_of(first_dev)
-    far_rank = ranks_of(far_owner)
-    message = pack_ints(
-        jnp.concatenate([far_owner * LANES + far_rank, first_dev * LANES + far_cap + row_rank]),
-        jnp.concatenate([local[:, 1:].reshape(-1), local[:, 0] + 1]),
-        devices * LANES,
-    ).reshape(devices, 1, LANES)
-
     def far(values):
         return lax.all_to_all(values, AXES, split_axis=0, concat_axis=0, tiled=True)
 
-    heard = far(message)[:, 0]
+    message, places = prepare(triplets, home_rows, devices, far_cap, row_count, row_cap)
+    heard = far(message.reshape(devices, 1, LANES)).reshape(devices, LANES)
     queries = heard[:, :far_cap].reshape(-1)
-    row_place = (first_dev - me) % row_count * row_cap + row_rank
-    far_place = far_owner * far_cap + far_rank
-    second_place, third_place = far_place.reshape(trip_local, 2).T
     asked = lax.dynamic_slice(
         heard, (lax.axis_index("trip") * row_count, far_cap), (row_count, row_cap)
     )
-    codes = jnp.take(
-        asked, (lax.axis_index("row") - jnp.arange(row_count)) % row_count, axis=0, mode="clip"
-    )
+    codes = jnp.take(asked, lax.axis_index("row") ^ jnp.arange(row_count), axis=0, mode="clip")
 
     state = packed(deviation)
     one = lax.broadcasted_iota(jnp.int32, state.shape[1:], 0) + rows * (
@@ -381,25 +413,32 @@
     )
     sent_state = jnp.where(one == columns, 1.0, state).astype(BF16)
     records = jnp.concatenate([eigvecs, sent_state], 1)
-    far_vecs, row_vecs = look_up(queries, jnp.maximum(codes - 1, 0), records, eigvecs)
+    far_vecs, near, away = look_up(heard, records, eigvecs, far_cap, row_count, row_cap)
     far_table = far(far_vecs)
-    first_vecs = [row_vecs[0]] + [
-        lax.ppermute(row_vecs[d], "row", [(i, (i - d) % row_count) for i in range(row_count)])
-        for d in range(1, row_count)
-    ]
-    source, base_rate, first_vecs[1] = lax.optimization_barrier((source, base_rate, first_vecs[1]))
+    half = row_count // 2
+    held = {(r, 0): near[r * row_cap : (r + 1) * row_cap] for r in range(half)}
+    sent = [(r, 0) for r in range(half, row_count)]
+    moving, bit = away, half
+    while bit:
+        moved = to_peer(moving, bit, row_count)
+        if bit == half:
+            source, base_rate, moved = lax.optimization_barrier((source, base_rate, moved))
+        for n, (r, o) in enumerate(sent):
+            held[r ^ bit, o ^ bit] = moved[n * row_cap : (n + 1) * row_cap]
+        bit //= 2
+        sent = [key for key in held if key[0] & bit]
+        if bit:
+            moving = jnp.concatenate([held.pop(key) for key in sent], 0)
     driven = packed(source)
     rate = jnp.concatenate([base_rate, base_rate], 1)[:, None, :]
-    first_table = jnp.concatenate(first_vecs, 0)
+    first_table = jnp.concatenate([held[0, o] for o in range(row_count)], 0)
     first_table, driven, rate = lax.optimization_barrier((first_table, driven, rate))
-    first_part = contract_first(row_place, first_table, cubic)
-    arrived_state = far_table[:, branches:]
-    pairs = contract_rest(second_place, third_place, weights, far_table, first_part)
-
+    first_part = contract_first(places, first_table, cubic)
+    pairs = contract_rest(places, weights, far_table, first_part)
+
+    table, start = far_table, branches
     for step in range(ITERS):
-        terms = coupling_terms(
-            second_place, third_place, row_place, arrived_state, pairs, columns, row_count, row_cap
-        )
+        terms = coupling_terms(places, table, start, pairs, columns, row_count, row_cap)
         arrived = from_peers(terms)
         first, last = step == 0, step == ITERS - 1
         results = update(codes, queries, arrived, state, driven, rate, columns, first, last)
@@ -407,7 +446,7 @@
         if first:
             rate = results[1]
         if not last:
-            arrived_state = far(results[-1])
+            table, start = far(results[-1]), 0
     return unpacked(state)
 
 

time: 100 us -> 99.9 us (level)
  waiting for transfers between devices: 17.7 us -> 23.6 us
  local copies, waits for them, and re-layouts: 8.87 us -> 12.5 us
  other arithmetic: 4.49 us -> 1.12 us
  Pallas kernels: 40.7 us -> 37.7 us
  starting transfers between devices: 16 us -> 14.3 us
  blocking collectives: 11.3 us -> 9.93 us
    ppermute x9 -> x8, waiting for transfers between devices: 13.3 us -> 19 us  [to_peer(): return lax.ppermute(values, 'row', [(i, i ^ bits) for i in range(count)])]
    pallas_call x1, Pallas kernels: 16.7 us -> 11.5 us  [contract_first(): pl.pallas_call(first_kernel, grid_spec=pltpu.PrefetchScalarGridSpec(num_s...]
    unnamed x16 -> x15, local copies, waits for them, and re-layouts: 3.98 us -> 7.08 us
    pallas_call x3 -> x4, Pallas kernels: 2.49 us -> 4.45 us  [the longest x2 1.87 us: coupling_terms(): pl.pallas_call(functools.partial(terms_kernel, columns, start), in_specs=...]
    ppermute x9 -> x8, starting transfers between devices: 5.91 us -> 4.38 us  [to_peer(): return lax.ppermute(values, 'row', [(i, i ^ bits) for i in range(count)])]
    all_to_all x1, blocking collectives: 11.3 us -> 9.93 us  [far(): return lax.all_to_all(values, AXES, split_axis=0, concat_axis=0, tiled=True)]
    concatenate x3 -> x2, other arithmetic: 2.25 us -> 0.89 us  [the longest x1 0.78 us: body(): moving = jnp.concatenate([held.pop(key) for key in sent], 0)]
    reduce_sum x3 -> x0, other arithmetic: 1.18 us -> none  [the longest x1 0.82 us: pack_ints(): return jnp.sum(jnp.where(onehot, values[None, :], 0), axis=1)]
  transfers between devices with their start and end apart: 11 -> 10, of which waited for: 8 -> 6; matrix products, arithmetic and copies ran while one was open for 6% -> 6% of each run, Pallas kernels for 17% -> 12%
where the time goes in v9:
time: 99.9 us; the launch traced here: 99.5 us
  Pallas kernels  37.7 us (38%)
  waiting for transfers between devices  23.6 us (24%)
  starting transfers between devices  14.3 us (14%)
  local copies, waits for them, and re-layouts  12.5 us (13%)
  blocking collectives  9.93 us (10%)
  other arithmetic  1.12 us (1%)
    pallas_call x1, Pallas kernels, contract_rest(): pl.pallas_call(functools.partial(second_kernel, stride, group), grid_spec...  19.8 us
    ppermute x8, waiting for transfers between devices, to_peer(): return lax.ppermute(values, 'row', [(i, i ^ bits) for i in range(count)])  19 us
    pallas_call x1, Pallas kernels, contract_first(): pl.pallas_call(first_kernel, grid_spec=pltpu.PrefetchScalarGridSpec(num_s...  11.5 us
    all_to_all x2, starting transfers between devices, far(): return lax.all_to_all(values, AXES, split_axis=0, concat_axis=0, tiled=True)  9.95 us
    all_to_all x1, blocking collectives, far(): return lax.all_to_all(values, AXES, split_axis=0, concat_axis=0, tiled=True)  9.93 us
    unnamed x15, local copies, waits for them, and re-layouts  7.08 us
    all_to_all x2, waiting for transfers between devices, far(): return lax.all_to_all(values, AXES, split_axis=0, concat_axis=0, tiled=True)  4.58 us
    ppermute x8, starting transfers between devices, to_peer(): return lax.ppermute(values, 'row', [(i, i ^ bits) for i in range(count)])  4.38 us
  transfers between devices with their start and end apart: 10, of which 6 were waited for; matrix products, arithmetic and copies ran while one was open for 6% of the time, Pallas kernels for 12%

profile of v9, /device:TPU:0, one launch (start us, length us, event | category | flops | bytes accessed | tf_op | source)
XLA Modules:
  0.0 99.5 jit_solution(3731715489187362218)
XLA Ops:
  0.0 1.6 %prepare.1 = (s32[32,128]{1,0:T(8,128)}, s32[8,128]{1,0:T(8,128)}) custom-call(s32[3,24]{1,0:T(4,128)} %bitcast.41), custom_call_target="tpu_custom_call" | custom-call | tf_op jit(solution)/shard_map/prepare/pallas_call | solution.py:68
  1.6 7.3 %all-to-all-start = ((s32[32,1,128]{2,1,0:T(1,128)}), s32[32,1,128]{2,1,0:T(1,128)S(1)}, u32[]{:S(2)}, u32[]{:S(2)}) async-start(s32[32,1,128]{2,1,0:T(1,128)} %bitcast.40), calls=%async_computation | async-start | bytes 32768 | tf_op jit(solution)/shard_map/all_to_all | solution.py:400
  8.9 1.1 %copy.18 = f32[64,768]{0,1:T(8,128)S(1)} copy(f32[64,768]{1,0:T(8,128)} %param.11) | data formatting | bytes 393216 | tf_op args[4]
  10.1 0.0 copy-start
  10.1 0.5 copy.20
  10.6 0.3 reshape.49.refs_4_
  11.0 0.3 copy-done
  11.3 0.1 pad_maximum_fusion.record_ref
  11.4 4.6 %all-to-all-done = s32[32,1,128]{2,1,0:T(1,128)S(1)} async-done(((s32[32,1,128]{2,1,0:T(1,128)}), s32[32,1,128]{2,1,0:T(1,128)S(1)}, u32[]{:S(2)}, u32[]{:S(2)}) %all-to-all-start) | async-done | bytes 16416 | tf_op jit(solution)/shard_map/all_to_all | solution.py:400
  16.0 1.0 %look_up.1 = (bf16[64,72,128]{2,1,0:T(8,128)(2,1)S(1)}, bf16[24,64,128]{2,1,0:T(8,128)(2,1)S(1)}, bf16[24,64,128]{2,1,0:T(8,128)(2,1)S(1)}) custom-call(s32[32,128]{1,0:T(8,128)S(1)} %bitcast.33, bf16[64,72,128]{2,1,0:T(8,128)(2,1)S(1)} %pad_maximum_fusion.record_ref, bf16[64,64,128]{2,1,0:T(8,128)(2,1)S(1)} %copy-done), custom_call_target="tpu_custom_call" | custom-call | tf_op jit(solution)/shard_map/look_up/pallas_call | solution.py:104
  17.0 1.1 %copy-done.1 = bf16[64,72,128]{2,1,0:T(8,128)(2,1)} copy-done((bf16[64,72,128]{2,1,0:T(8,128)(2,1)}, bf16[64,72,128]{2,1,0:T(8,128)(2,1)S(1)}, u32[]{:S(2)}) %copy-start.1) | copy-done | bytes 1179672
  18.1 0.5 collective-permute-start
  18.6 2.7 %all-to-all-start.1 = ((bf16[64,72,128]{2,1,0:T(8,128)(2,1)}), bf16[64,72,128]{2,1,0:T(8,128)(2,1)S(1)}, u32[]{:S(2)}, u32[]{:S(2)}) async-start(bf16[64,72,128]{2,1,0:T(8,128)(2,1)} %copy-done.1), calls=%async_computation.1 | async-start | bytes 2359296 | tf_op jit(solution)/shard_map/all_to_all | solution.py:400
  21.3 0.0 copy-start.5
  21.3 14.3 %collective-permute-done = bf16[24,64,128]{2,1,0:T(8,128)(2,1)S(1)} collective-permute-done((bf16[24,64,128]{2,1,0:T(8,128)(2,1)S(1)}, bf16[24,64,128]{2,1,0:T(8,128)(2,1)S(1)}, u32[]{:S(2)}, u32[]{:S(2)}) %collective-permute-start) | collective-permute-done | bytes 393248 | tf_op jit(solution)/shard_map/ppermute | solution.py:81
  35.6 0.8 pad_maximum_fusion.2
  36.4 0.2 copy.21
  36.6 0.0 copy-start.6
  36.7 0.5 copy.23
  37.2 0.3 reshape.52.refs_5_
  37.5 0.1 pad_maximum_fusion.3
  37.6 0.8 collective-permute-done.1
  38.4 1.0 %fusion.1 = (bf16[12,64,128]{2,1,0:T(8,128)(2,1)S(1)}, bf16[12,64,128]{2,1,0:T(8,128)(2,1)S(1)}) fusion(bf16[24,64,128]{2,1,0:T(8,128)(2,1)} %collective-permute-done.1), kind=kLoop, calls=%fused_computation.20 | loop fusion | bytes 786432 | tf_op jit(solution)/shard_map/slice | solution.py:427
  39.5 0.1 pad_maximum_fusion.1.refs_0_.refs_1_.refs_2_.refs_3_.refs_4_.refs_5_
  39.6 0.0 copy-start.3
  39.6 4.6 %copy-done.3 = bf16[24,64,4096]{2,1,0:T(8,128)(2,1)S(1)} copy-done((bf16[24,64,4096]{2,1,0:T(8,128)(2,1)S(1)}, bf16[24,64,4096]{2,1,0:T(8,128)(2,1)}, u32[]{:S(2)}) %copy-start.3) | copy-done | bytes 12582936
  44.2 11.5 %contract_first.1.refs_1_ = bf16[12,64,128,128]{3,2,1,0:T(8,128)(2,1)} custom-call(s32[8,128]{1,0:T(8,128)S(1)} %copy-done.2, bf16[48,64,128]{2,1,0:T(8,128)(2,1)S(1)} %pad_maximum_fusion.1.refs_0_.refs_1_.refs_2_.refs_3_.refs_4_.refs_5_, bf16[48,64,128]{2,1,0:T(8,128)(2,1)S(1)} %pad_maximum_fusion.1.refs_0_.refs_1_.refs_2_.refs_3_.refs_4_.refs_5_, ...), custom_call_target="tpu_custom_call" | custom-call | flops 12884901888 | bytes 37748736 | tf_op jit(solution)/shard_map/contract_first/pallas_call | solution.py:159
  55.7 19.8 %contract_rest.1.pair_ref = bf16[24,256,128]{2,1,0:T(8,128)(2,1)S(1)} custom-call(s32[8,128]{1,0:T(8,128)S(1)} %copy-done.2, s32[24]{0:T(128)S(1)} %copy-done.4, bf16[64,72,128]{2,1,0:T(8,128)(2,1)S(1)} %all-to-all-done.1.refs_0_.table_ref, bf16[12,64,128,128]{3,2,1,0:T(8,128)(2,1)} %contract_first.1.refs_1_), custom_call_target="tpu_custom_call" | custom-call | flops 12884901888 | bytes 25165824 | tf_op jit(solution)/shard_map/contract_rest/pallas_call | solution.py:265
  75.6 0.9 coupling_terms.2
  76.5 0.2 collective-permute-start.2
  76.7 0.9 collective-permute-start.3
  77.6 0.8 collective-permute-start.4
  78.4 0.1 constant_dynamic-slice_fusion
  78.5 0.1 reshape.46.queries
  78.6 0.6 gather_fusion
  79.2 1.4 %collective-permute-done.3.refs_2_ = bf16[12,8,128]{2,1,0:T(8,128)(2,1)S(1)} collective-permute-done((bf16[12,8,128]{2,1,0:T(8,128)(2,1)S(1)}, bf16[12,8,128]{2,1,0:T(8,128)(2,1)S(1)}, u32[]{:S(2)}, u32[]{:S(2)}) %collective-permute-start.3) | collective-permute-done | bytes 24608 | tf_op jit(solution)/shard_map/ppermute | solution.py:81
  80.5 0.3 collective-permute-done.4.refs_3_
  80.9 1.0 %update.2 = (f32[64,8,128]{2,1,0:T(8,128)S(1)}, f32[64,8,128]{2,1,0:T(8,128)S(1)}, bf16[64,8,128]{2,1,0:T(8,128)(2,1)S(1)}) custom-call(s32[4,12]{1,0:T(4,128)S(1)} %gather_fusion, s32[64]{0:T(128)S(1)} %reshape.46.queries, bf16[12,8,128]{2,1,0:T(8,128)(2,1)S(1)} %get-tuple-element.36.refs_0_, bf16[12,8,128]{2,1,0:T(8,128)(2,1)S(1)} %collective-permute-done.2.refs_1_, ...), custom_call_target="tpu_custom_call" | custom-call | tf_op jit(solution)/shard_map/update/pallas_call | solution.py:366
  81.9 9.9 %all_to_all.15.table_ref = bf16[64,8,128]{2,1,0:T(8,128)(2,1)S(1)} all-to-all(bf16[64,8,128]{2,1,0:T(8,128)(2,1)S(1)} %get-tuple-element.42), channel_id=1, replica_groups=mesh['trip'=8,'row'=4] {'trip','row'}, dimensions={0} | all-to-all | bytes 262144 | tf_op jit(solution)/shard_map/all_to_all | solution.py:400
  91.8 0.9 coupling_terms.3
  92.8 0.3 collective-permute-start.5
  93.0 0.4 collective-permute-start.6
  93.4 1.3 %collective-permute-start.7 = (bf16[12,8,128]{2,1,0:T(8,128)(2,1)S(1)}, bf16[12,8,128]{2,1,0:T(8,128)(2,1)S(1)}, u32[]{:S(2)}, u32[]{:S(2)}) collective-permute-start(bf16[12,8,128]{2,1,0:T(8,128)(2,1)S(1)} %get-tuple-element.46), channel_id=1, source_target_pairs={{0,3},{1,2},{2,1},{3,0},{4,7},{5,6},{6,5},{7,4},{8,11},{9,10},{10,... | collective-permute-start | bytes 73736 | tf_op jit(solution)/shard_map/ppermute | solution.py:81
  94.7 2.2 %collective-permute-done.6.refs_2_ = bf16[12,8,128]{2,1,0:T(8,128)(2,1)S(1)} collective-permute-done((bf16[12,8,128]{2,1,0:T(8,128)(2,1)S(1)}, bf16[12,8,128]{2,1,0:T(8,128)(2,1)S(1)}, u32[]{:S(2)}, u32[]{:S(2)}) %collective-permute-start.6) | collective-permute-done | bytes 24608 | tf_op jit(solution)/shard_map/ppermute | solution.py:81
  96.9 0.9 update.3
  97.8 0.3 reshape.53
  98.2 0.4 copy.25
  98.7 0.8 copy.26
  (27 shorter events, 0.4 us)
Async XLA Ops:
  1.6 14.4 %all-to-all-start = ((s32[32,1,128]{2,1,0:T(1,128)}), s32[32,1,128]{2,1,0:T(1,128)S(1)}, u32[]{:S(2)}, u32[]{:S(2)}) async-start(s32[32,1,128]{2,1,0:T(1,128)} %bitcast.40), calls=%async_computation | async-start | bytes 32768 | tf_op jit(solution)/shard_map/all_to_all | solution.py:400
  10.1 1.2 %copy-start = (bf16[64,64,128]{2,1,0:T(8,128)(2,1)S(1)}, bf16[64,64,128]{2,1,0:T(8,128)(2,1)}, u32[]{:S(2)}) copy-start(bf16[64,64,128]{2,1,0:T(8,128)(2,1)} %vec_ref.1) | copy-start | bytes 3145732
  17.0 1.1 %copy-start.1 = (bf16[64,72,128]{2,1,0:T(8,128)(2,1)}, bf16[64,72,128]{2,1,0:T(8,128)(2,1)S(1)}, u32[]{:S(2)}) copy-start(bf16[64,72,128]{2,1,0:T(8,128)(2,1)S(1)} %get-tuple-element.29) | copy-start | bytes 3538948
  18.1 17.5 %collective-permute-start = (bf16[24,64,128]{2,1,0:T(8,128)(2,1)S(1)}, bf16[24,64,128]{2,1,0:T(8,128)(2,1)S(1)}, u32[]{:S(2)}, u32[]{:S(2)}) collective-permute-start(bf16[24,64,128]{2,1,0:T(8,128)(2,1)S(1)} %get-tuple-element.31), channel_id=1, source_target_pairs={{0,2},{1,3},{2,0},{3,1},{4,6},{5,7},{6,4},{7,5},{8,10},{9,11},{10,... | collective-permute-start | bytes 1179656 | tf_op jit(solution)/shard_map/ppermute | solution.py:81
  18.6 37.1 %all-to-all-start.1 = ((bf16[64,72,128]{2,1,0:T(8,128)(2,1)}), bf16[64,72,128]{2,1,0:T(8,128)(2,1)S(1)}, u32[]{:S(2)}, u32[]{:S(2)}) async-start(bf16[64,72,128]{2,1,0:T(8,128)(2,1)} %copy-done.1), calls=%async_computation.1 | async-start | bytes 2359296 | tf_op jit(solution)/shard_map/all_to_all | solution.py:400
  21.3 15.1 %copy-start.5 = (f32[64,768]{1,0:T(8,128)S(1)}, f32[64,768]{1,0:T(8,128)}, u32[]{:S(2)}) copy-start(f32[64,768]{1,0:T(8,128)} %param.12) | copy-start | bytes 589828
  36.4 2.1 %collective-permute-start.1 = (bf16[24,64,128]{2,1,0:T(8,128)(2,1)}, bf16[24,64,128]{2,1,0:T(8,128)(2,1)}, u32[]{:S(2)}, u32[]{:S(2)}) collective-permute-start(bf16[24,64,128]{2,1,0:T(8,128)(2,1)} %pad_maximum_fusion.2), channel_id=1, source_target_pairs={{0,1},{1,0},{2,3},{3,2},{4,5},{5,4},{6,7},{7,6},{8,9},{9,8},{10,11... | collective-permute-start | bytes 1179656 | tf_op jit(solution)/shard_map/ppermute | solution.py:81
  36.6 0.9 copy-start.6
  37.2 2.4 %copy-start.2 = (s32[8,128]{1,0:T(8,128)S(1)}, s32[8,128]{1,0:T(8,128)}, u32[]{:S(2)}) copy-start(s32[8,128]{1,0:T(8,128)} %get-tuple-element.28.places) | copy-start | bytes 12292
  39.6 4.6 %copy-start.3 = (bf16[24,64,4096]{2,1,0:T(8,128)(2,1)S(1)}, bf16[24,64,4096]{2,1,0:T(8,128)(2,1)}, u32[]{:S(2)}) copy-start(bf16[24,64,4096]{2,1,0:T(8,128)(2,1)} %refs_6_.1) | copy-start | bytes 37748740
  44.2 11.5 %copy-start.4 = (s32[24]{0:T(128)S(1)}, s32[24]{0:T(128)}, u32[]{:S(2)}) copy-start(s32[24]{0:T(128)} %weights.1) | copy-start | bytes 292
  76.5 2.7 %collective-permute-start.2 = (bf16[12,8,128]{2,1,0:T(8,128)(2,1)S(1)}, bf16[12,8,128]{2,1,0:T(8,128)(2,1)S(1)}, u32[]{:S(2)}, u32[]{:S(2)}) collective-permute-start(bf16[12,8,128]{2,1,0:T(8,128)(2,1)S(1)} %get-tuple-element.37), channel_id=1, source_target_pairs={{0,1},{1,0},{2,3},{3,2},{4,5},{5,4},{6,7},{7,6},{8,9},{9,8},{10,11... | collective-permute-start | bytes 73736 | tf_op jit(solution)/shard_map/ppermute | solution.py:81
  76.7 3.8 %collective-permute-start.3 = (bf16[12,8,128]{2,1,0:T(8,128)(2,1)S(1)}, bf16[12,8,128]{2,1,0:T(8,128)(2,1)S(1)}, u32[]{:S(2)}, u32[]{:S(2)}) collective-permute-start(bf16[12,8,128]{2,1,0:T(8,128)(2,1)S(1)} %get-tuple-element.38), channel_id=1, source_target_pairs={{0,2},{1,3},{2,0},{3,1},{4,6},{5,7},{6,4},{7,5},{8,10},{9,11},{10,... | collective-permute-start | bytes 73736 | tf_op jit(solution)/shard_map/ppermute | solution.py:81
  77.6 3.3 %collective-permute-start.4 = (bf16[12,8,128]{2,1,0:T(8,128)(2,1)S(1)}, bf16[12,8,128]{2,1,0:T(8,128)(2,1)S(1)}, u32[]{:S(2)}, u32[]{:S(2)}) collective-permute-start(bf16[12,8,128]{2,1,0:T(8,128)(2,1)S(1)} %get-tuple-element.39), channel_id=1, source_target_pairs={{0,3},{1,2},{2,1},{3,0},{4,7},{5,6},{6,5},{7,4},{8,11},{9,10},{10,... | collective-permute-start | bytes 73736 | tf_op jit(solution)/shard_map/ppermute | solution.py:81
  92.8 1.9 %collective-permute-start.5 = (bf16[12,8,128]{2,1,0:T(8,128)(2,1)S(1)}, bf16[12,8,128]{2,1,0:T(8,128)(2,1)S(1)}, u32[]{:S(2)}, u32[]{:S(2)}) collective-permute-start(bf16[12,8,128]{2,1,0:T(8,128)(2,1)S(1)} %get-tuple-element.44), channel_id=1, source_target_pairs={{0,1},{1,0},{2,3},{3,2},{4,5},{5,4},{6,7},{7,6},{8,9},{9,8},{10,11... | collective-permute-start | bytes 73736 | tf_op jit(solution)/shard_map/ppermute | solution.py:81
  93.0 3.9 %collective-permute-start.6 = (bf16[12,8,128]{2,1,0:T(8,128)(2,1)S(1)}, bf16[12,8,128]{2,1,0:T(8,128)(2,1)S(1)}, u32[]{:S(2)}, u32[]{:S(2)}) collective-permute-start(bf16[12,8,128]{2,1,0:T(8,128)(2,1)S(1)} %get-tuple-element.45), channel_id=1, source_target_pairs={{0,2},{1,3},{2,0},{3,1},{4,6},{5,7},{6,4},{7,5},{8,10},{9,11},{10,... | collective-permute-start | bytes 73736 | tf_op jit(solution)/shard_map/ppermute | solution.py:81
  93.4 3.5 %collective-permute-start.7 = (bf16[12,8,128]{2,1,0:T(8,128)(2,1)S(1)}, bf16[12,8,128]{2,1,0:T(8,128)(2,1)S(1)}, u32[]{:S(2)}, u32[]{:S(2)}) collective-permute-start(bf16[12,8,128]{2,1,0:T(8,128)(2,1)S(1)} %get-tuple-element.46), channel_id=1, source_target_pairs={{0,3},{1,2},{2,1},{3,0},{4,7},{5,6},{6,5},{7,4},{8,11},{9,10},{10,... | collective-permute-start | bytes 73736 | tf_op jit(solution)/shard_map/ppermute | solution.py:81

commit v10 on v9

--- a/solution.py
+++ b/solution.py
@@ -119,14 +119,24 @@
     return next(group for group in (3, 2, 1) if pairs % group == 0)
 
 
-def first_kernel(places, *refs):
+def first_kernel(cap, offsets, places, *refs):
     vec_refs, (cubic_ref, out_ref) = refs[:-2], refs[-2:]
-    group = len(vec_refs) // 2
+    group = cubic_ref.shape[0] // 2
     branches = cubic_ref.shape[1]
     both = 2 * branches
     step = 4
+
+    def vectors(t):
+        place = places[0, 2 * group * pl.program_id(0) + t]
+        block = lax.div(place, cap)
+        row = place - block * cap
+        found = vec_refs[0][offsets[0] + row]
+        for k in range(1, len(vec_refs)):
+            found = jnp.where(block == k, vec_refs[k][offsets[k] + row], found)
+        return found
+
     for pair in range(group):
-        one, two = vec_refs[2 * pair][0], vec_refs[2 * pair + 1][0]
+        one, two = vectors(2 * pair), vectors(2 * pair + 1)
         none = jnp.zeros((branches, branches), one.dtype)
         mixer = jnp.concatenate(
             [
@@ -148,32 +158,29 @@
                     ]
 
 
-def contract_first(places, table, cubic):
+def contract_first(places, tables, offsets, cap, cubic):
     count, branches, pairs = cubic.shape
     both = 2 * branches
     group = pairs_per_step(count // 2)
 
-    def vectors(t):
-        return pl.BlockSpec((1, branches, both), lambda s, places: (places[0, 2 * group * s + t], 0, 0))
-
-    return pl.pallas_call(
-        first_kernel,
+    return pl.pallas_call(
+        functools.partial(first_kernel, cap, offsets),
         grid_spec=pltpu.PrefetchScalarGridSpec(
             num_scalar_prefetch=1,
             grid=(count // (2 * group),),
-            in_specs=[vectors(t) for t in range(2 * group)]
+            in_specs=[pl.BlockSpec(memory_space=pltpu.VMEM)] * len(tables)
             + [pl.BlockSpec((2 * group, branches, pairs), lambda s, places: (s, 0, 0))],
             out_specs=pl.BlockSpec((group, branches, both, both), lambda s, places: (s, 0, 0, 0)),
         ),
         out_shape=jax.ShapeDtypeStruct((count // 2, branches, both, both), BF16),
         compiler_params=pltpu.CompilerParams(vmem_limit_bytes=40 * MIB),
         cost_estimate=pl.CostEstimate(
-            flops=8 * 2 * count * both * branches * pairs,
+            flops=11 * 2 * count * both * branches * pairs,
             bytes_accessed=2 * count * (both + branches) * pairs,
             transcendentals=0,
         ),
         name="contract_first",
-    )(places, *[table] * (2 * group), cubic)
+    )(places, *tables, cubic)
 
 
 def second_kernel(stride, group, places, weights, *refs):
@@ -416,7 +423,7 @@
     far_vecs, near, away = look_up(heard, records, eigvecs, far_cap, row_count, row_cap)
     far_table = far(far_vecs)
     half = row_count // 2
-    held = {(r, 0): near[r * row_cap : (r + 1) * row_cap] for r in range(half)}
+    held = {(r, 0): (near, r * row_cap) for r in range(half)}
     sent = [(r, 0) for r in range(half, row_count)]
     moving, bit = away, half
     while bit:
@@ -424,16 +431,17 @@
         if bit == half:
             source, base_rate, moved = lax.optimization_barrier((source, base_rate, moved))
         for n, (r, o) in enumerate(sent):
-            held[r ^ bit, o ^ bit] = moved[n * row_cap : (n + 1) * row_cap]
+            held[r ^ bit, o ^ bit] = (moved, n * row_cap)
         bit //= 2
         sent = [key for key in held if key[0] & bit]
         if bit:
-            moving = jnp.concatenate([held.pop(key) for key in sent], 0)
+            parts = [held.pop(key) for key in sent]
+            moving = jnp.concatenate([v[start : start + row_cap] for v, start in parts], 0)
     driven = packed(source)
     rate = jnp.concatenate([base_rate, base_rate], 1)[:, None, :]
-    first_table = jnp.concatenate([held[0, o] for o in range(row_count)], 0)
-    first_table, driven, rate = lax.optimization_barrier((first_table, driven, rate))
-    first_part = contract_first(places, first_table, cubic)
+    tables, offsets = zip(*[held[0, o] for o in range(row_count)])
+    tables, driven, rate = lax.optimization_barrier((tables, driven, rate))
+    first_part = contract_first(places, tables, offsets, row_cap, cubic)
     pairs = contract_rest(places, weights, far_table, first_part)
 
     table, start = far_table, branches

time: 99.9 us -> 105 us (1.051)
  local copies, waits for them, and re-layouts: 12.5 us -> 16.7 us
    transpose x4, local copies, waits for them, and re-layouts: 1.11 us -> 4.61 us  [packed(): return jnp.swapaxes(values, 1, 2).reshape(home_rows, rows, 2 * branches)]
    slice x3 -> x2, local copies, waits for them, and re-layouts: 1.1 us -> 0.03 us  [body(): v[start:start + row_cap]]
  transfers between devices with their start and end apart: 10 -> 10, of which waited for: 6 -> 5; matrix products, arithmetic and copies ran while one was open for 6% -> 10% of each run, Pallas kernels for 12% -> 11%
where the time goes in v10:
time: 105 us; the launch traced here: 104 us
  Pallas kernels  38.5 us (37%)
  waiting for transfers between devices  23.4 us (22%)
  local copies, waits for them, and re-layouts  16.7 us (16%)
  starting transfers between devices  14.6 us (14%)
  blocking collectives  9.93 us (9%)
    pallas_call x1, Pallas kernels, contract_rest(): pl.pallas_call(functools.partial(second_kernel, stride, group), grid_spec...  19.8 us
    ppermute x8, waiting for transfers between devices, to_peer(): return lax.ppermute(values, 'row', [(i, i ^ bits) for i in range(count)])  18.8 us
    pallas_call x1, Pallas kernels, contract_first(): pl.pallas_call(functools.partial(first_kernel, cap, offsets), grid_spec=p...  11.5 us
    all_to_all x2, starting transfers between devices, far(): return lax.all_to_all(values, AXES, split_axis=0, concat_axis=0, tiled=True)  10.1 us
    all_to_all x1, blocking collectives, far(): return lax.all_to_all(values, AXES, split_axis=0, concat_axis=0, tiled=True)  9.93 us
    unnamed x15, local copies, waits for them, and re-layouts  7.07 us
    transpose x4, local copies, waits for them, and re-layouts, packed(): return jnp.swapaxes(values, 1, 2).reshape(home_rows, rows, 2 * branches)  4.61 us
    all_to_all x2, waiting for transfers between devices, far(): return lax.all_to_all(values, AXES, split_axis=0, concat_axis=0, tiled=True)  4.58 us
  transfers between devices with their start and end apart: 10, of which 5 were waited for; matrix products, arithmetic and copies ran while one was open for 10% of the time, Pallas kernels for 11%

profile of v10, /device:TPU:0, one launch (start us, length us, event | category | flops | bytes accessed | tf_op | source)
XLA Modules:
  0.0 104.3 jit_solution(6438882116649481803)
XLA Ops:
  0.0 1.6 %prepare.1 = (s32[32,128]{1,0:T(8,128)}, s32[8,128]{1,0:T(8,128)}) custom-call(s32[3,24]{1,0:T(4,128)} %bitcast.41), custom_call_target="tpu_custom_call" | custom-call | tf_op jit(solution)/shard_map/prepare/pallas_call | solution.py:68
  1.6 7.3 %all-to-all-start = ((s32[32,1,128]{2,1,0:T(1,128)}), s32[32,1,128]{2,1,0:T(1,128)S(1)}, u32[]{:S(2)}, u32[]{:S(2)}) async-start(s32[32,1,128]{2,1,0:T(1,128)} %bitcast.40), calls=%async_computation | async-start | bytes 32768 | tf_op jit(solution)/shard_map/all_to_all | solution.py:407
  8.9 1.1 %copy.18 = f32[64,768]{0,1:T(8,128)S(1)} copy(f32[64,768]{1,0:T(8,128)} %param.11) | data formatting | bytes 393216 | tf_op args[4]
  10.1 0.0 copy-start
  10.1 0.5 copy.20
  10.6 0.3 reshape.49.refs_4_
  11.0 0.3 copy-done
  11.3 0.1 pad_maximum_fusion.record_ref
  11.4 4.6 %all-to-all-done = s32[32,1,128]{2,1,0:T(1,128)S(1)} async-done(((s32[32,1,128]{2,1,0:T(1,128)}), s32[32,1,128]{2,1,0:T(1,128)S(1)}, u32[]{:S(2)}, u32[]{:S(2)}) %all-to-all-start) | async-done | bytes 16416 | tf_op jit(solution)/shard_map/all_to_all | solution.py:407
  16.0 1.7 %look_up.1 = (bf16[64,72,128]{2,1,0:T(8,128)(2,1)S(1)}, bf16[24,64,128]{2,1,0:T(8,128)(2,1)S(1)}, bf16[24,64,128]{2,1,0:T(8,128)(2,1)}) custom-call(s32[32,128]{1,0:T(8,128)S(1)} %bitcast.33, bf16[64,72,128]{2,1,0:T(8,128)(2,1)S(1)} %pad_maximum_fusion.record_ref, bf16[64,64,128]{2,1,0:T(8,128)(2,1)S(1)} %copy-done), custom_call_target="tpu_custom_call" | custom-call | tf_op jit(solution)/shard_map/look_up/pallas_call | solution.py:104
  17.7 1.1 %copy-done.1 = bf16[64,72,128]{2,1,0:T(8,128)(2,1)} copy-done((bf16[64,72,128]{2,1,0:T(8,128)(2,1)}, bf16[64,72,128]{2,1,0:T(8,128)(2,1)S(1)}, u32[]{:S(2)}) %copy-start.1) | copy-done | bytes 1179672
  18.8 0.5 collective-permute-start
  19.3 2.8 %all-to-all-start.1 = ((bf16[64,72,128]{2,1,0:T(8,128)(2,1)}), bf16[64,72,128]{2,1,0:T(8,128)(2,1)S(1)}, u32[]{:S(2)}, u32[]{:S(2)}) async-start(bf16[64,72,128]{2,1,0:T(8,128)(2,1)} %copy-done.1), calls=%async_computation.1 | async-start | bytes 2359296 | tf_op jit(solution)/shard_map/all_to_all | solution.py:407
  22.2 14.3 %collective-permute-done.refs_2_ = bf16[24,64,128]{2,1,0:T(8,128)(2,1)S(1)} collective-permute-done((bf16[24,64,128]{2,1,0:T(8,128)(2,1)}, bf16[24,64,128]{2,1,0:T(8,128)(2,1)S(1)}, u32[]{:S(2)}, u32[]{:S(2)}) %collective-permute-start) | collective-permute-done | bytes 393248 | tf_op jit(solution)/shard_map/ppermute | solution.py:81
  36.5 0.8 pad_maximum_fusion.1
  37.3 0.0 collective-permute-start.1
  37.3 0.2 copy.21
  37.5 0.9 reshape.50
  38.4 1.9 %pad_bitcast_fusion = f32[64,8,2,64]{0,1,2,3:T(8,128)} fusion(f32[64,12,64]{0,1,2:T(8,128)} %bitcast.37), kind=kLoop, calls=%fused_computation.4 | loop fusion | bytes 458752 | tf_op jit(solution)/shard_map/transpose | solution.py:399
  40.3 2.2 %copy.23 = f32[64,8,2,64]{3,2,1,0:T(2,128)} copy(f32[64,8,2,64]{0,1,2,3:T(8,128)} %pad_bitcast_fusion) | data formatting | bytes 524288 | tf_op jit(solution)/shard_map/transpose | solution.py:399
  42.4 1.3 %reshape.52.refs_5_ = f32[64,8,128]{2,1,0:T(8,128)S(1)} reshape(f32[64,8,2,64]{3,2,1,0:T(2,128)} %copy.23) | data formatting | bytes 524288 | tf_op jit(solution)/shard_map/reshape | solution.py:399
  43.8 0.1 pad_maximum_fusion.2
  43.9 0.0 collective-permute-done.1.refs_1_.refs_3_
  43.9 0.0 copy-start.3
  43.9 4.6 %copy-done.3 = bf16[24,64,4096]{2,1,0:T(8,128)(2,1)S(1)} copy-done((bf16[24,64,4096]{2,1,0:T(8,128)(2,1)S(1)}, bf16[24,64,4096]{2,1,0:T(8,128)(2,1)}, u32[]{:S(2)}) %copy-start.3) | copy-done | bytes 12582936
  48.5 11.5 %contract_first.1.refs_1_ = bf16[12,64,128,128]{3,2,1,0:T(8,128)(2,1)} custom-call(s32[8,128]{1,0:T(8,128)S(1)} %copy-done.2, bf16[24,64,128]{2,1,0:T(8,128)(2,1)S(1)} %get-tuple-element.38.refs_0_, bf16[24,64,128]{2,1,0:T(8,128)(2,1)S(1)} %collective-permute-done.1.refs_1_.refs_3_, bf16[24,64,128]{2,1,0:T(8,128)(2,1)S(1)} %collective-permute-done.refs_2_, ...), custom_call_target="tpu_custom_call" | custom-call | flops 17716740096 | bytes 37748736 | tf_op jit(solution)/shard_map/contract_first/pallas_call | solution.py:166
  60.0 0.0 all-to-all-done.1.refs_0_.table_ref
  60.0 19.8 %contract_rest.1.pair_ref = bf16[24,256,128]{2,1,0:T(8,128)(2,1)S(1)} custom-call(s32[8,128]{1,0:T(8,128)S(1)} %copy-done.2, s32[24]{0:T(128)S(1)} %copy-done.4, bf16[64,72,128]{2,1,0:T(8,128)(2,1)S(1)} %all-to-all-done.1.refs_0_.table_ref, bf16[12,64,128,128]{3,2,1,0:T(8,128)(2,1)} %contract_first.1.refs_1_), custom_call_target="tpu_custom_call" | custom-call | flops 12884901888 | bytes 25165824 | tf_op jit(solution)/shard_map/contract_rest/pallas_call | solution.py:272
  79.8 0.9 coupling_terms.2
  80.8 0.6 collective-permute-start.2
  81.4 0.9 collective-permute-start.3
  82.2 0.5 collective-permute-start.4
  82.8 0.1 constant_dynamic-slice_fusion
  82.9 0.1 reshape.46.queries
  83.0 0.6 gather_fusion
  83.5 1.6 %collective-permute-done.3.refs_2_ = bf16[12,8,128]{2,1,0:T(8,128)(2,1)S(1)} collective-permute-done((bf16[12,8,128]{2,1,0:T(8,128)(2,1)S(1)}, bf16[12,8,128]{2,1,0:T(8,128)(2,1)S(1)}, u32[]{:S(2)}, u32[]{:S(2)}) %collective-permute-start.3) | collective-permute-done | bytes 24608 | tf_op jit(solution)/shard_map/ppermute | solution.py:81
  85.2 0.6 collective-permute-done.4.refs_3_
  85.7 1.0 update.2
  86.7 9.9 %all_to_all.15.table_ref = bf16[64,8,128]{2,1,0:T(8,128)(2,1)S(1)} all-to-all(bf16[64,8,128]{2,1,0:T(8,128)(2,1)S(1)} %get-tuple-element.48), channel_id=1, replica_groups=mesh['trip'=8,'row'=4] {'trip','row'}, dimensions={0} | all-to-all | bytes 262144 | tf_op jit(solution)/shard_map/all_to_all | solution.py:407
  96.7 0.9 coupling_terms.3
  97.6 0.3 collective-permute-start.5
  97.9 0.4 collective-permute-start.6
  98.3 1.3 %collective-permute-start.7 = (bf16[12,8,128]{2,1,0:T(8,128)(2,1)S(1)}, bf16[12,8,128]{2,1,0:T(8,128)(2,1)S(1)}, u32[]{:S(2)}, u32[]{:S(2)}) collective-permute-start(bf16[12,8,128]{2,1,0:T(8,128)(2,1)S(1)} %get-tuple-element.52), channel_id=1, source_target_pairs={{0,3},{1,2},{2,1},{3,0},{4,7},{5,6},{6,5},{7,4},{8,11},{9,10},{10,... | collective-permute-start | bytes 73736 | tf_op jit(solution)/shard_map/ppermute | solution.py:81
  99.6 2.2 %collective-permute-done.6.refs_2_ = bf16[12,8,128]{2,1,0:T(8,128)(2,1)S(1)} collective-permute-done((bf16[12,8,128]{2,1,0:T(8,128)(2,1)S(1)}, bf16[12,8,128]{2,1,0:T(8,128)(2,1)S(1)}, u32[]{:S(2)}, u32[]{:S(2)}) %collective-permute-start.6) | collective-permute-done | bytes 24608 | tf_op jit(solution)/shard_map/ppermute | solution.py:81
  101.8 0.9 update.3
  102.7 0.3 reshape.53
  103.1 0.4 copy.25
  103.5 0.8 copy.26
  (25 shorter events, 0.3 us)
Async XLA Ops:
  1.6 14.4 %all-to-all-start = ((s32[32,1,128]{2,1,0:T(1,128)}), s32[32,1,128]{2,1,0:T(1,128)S(1)}, u32[]{:S(2)}, u32[]{:S(2)}) async-start(s32[32,1,128]{2,1,0:T(1,128)} %bitcast.40), calls=%async_computation | async-start | bytes 32768 | tf_op jit(solution)/shard_map/all_to_all | solution.py:407
  10.1 1.2 %copy-start = (bf16[64,64,128]{2,1,0:T(8,128)(2,1)S(1)}, bf16[64,64,128]{2,1,0:T(8,128)(2,1)}, u32[]{:S(2)}) copy-start(bf16[64,64,128]{2,1,0:T(8,128)(2,1)} %vec_ref.1) | copy-start | bytes 3145732
  17.7 1.1 %copy-start.1 = (bf16[64,72,128]{2,1,0:T(8,128)(2,1)}, bf16[64,72,128]{2,1,0:T(8,128)(2,1)S(1)}, u32[]{:S(2)}) copy-start(bf16[64,72,128]{2,1,0:T(8,128)(2,1)S(1)} %get-tuple-element.32) | copy-start | bytes 3538948
  18.8 17.7 %collective-permute-start = (bf16[24,64,128]{2,1,0:T(8,128)(2,1)}, bf16[24,64,128]{2,1,0:T(8,128)(2,1)S(1)}, u32[]{:S(2)}, u32[]{:S(2)}) collective-permute-start(bf16[24,64,128]{2,1,0:T(8,128)(2,1)} %get-tuple-element.34), channel_id=1, source_target_pairs={{0,2},{1,3},{2,0},{3,1},{4,6},{5,7},{6,4},{7,5},{8,10},{9,11},{10,... | collective-permute-start | bytes 1179656 | tf_op jit(solution)/shard_map/ppermute | solution.py:81
  19.3 18.0 %copy-start.5 = (f32[64,768]{1,0:T(8,128)S(1)}, f32[64,768]{1,0:T(8,128)}, u32[]{:S(2)}) copy-start(f32[64,768]{1,0:T(8,128)} %param.12) | copy-start | bytes 589828
  19.3 40.7 %all-to-all-start.1 = ((bf16[64,72,128]{2,1,0:T(8,128)(2,1)}), bf16[64,72,128]{2,1,0:T(8,128)(2,1)S(1)}, u32[]{:S(2)}, u32[]{:S(2)}) async-start(bf16[64,72,128]{2,1,0:T(8,128)(2,1)} %copy-done.1), calls=%async_computation.1 | async-start | bytes 2359296 | tf_op jit(solution)/shard_map/all_to_all | solution.py:407
  37.3 6.5 %collective-permute-start.1 = (bf16[24,64,128]{2,1,0:T(8,128)(2,1)}, bf16[24,64,128]{2,1,0:T(8,128)(2,1)S(1)}, u32[]{:S(2)}, u32[]{:S(2)}) collective-permute-start(bf16[24,64,128]{2,1,0:T(8,128)(2,1)} %pad_maximum_fusion.1), channel_id=1, source_target_pairs={{0,1},{1,0},{2,3},{3,2},{4,5},{5,4},{6,7},{7,6},{8,9},{9,8},{10,11... | collective-permute-start | bytes 1179656 | tf_op jit(solution)/shard_map/ppermute | solution.py:81
  38.4 5.4 %copy-start.6 = (f32[64,64]{1,0:T(8,128)S(1)}, f32[64,64]{1,0:T(8,128)}, u32[]{:S(2)}) copy-start(f32[64,64]{1,0:T(8,128)} %param.13) | copy-start | bytes 49156
  38.4 5.5 %copy-start.2 = (s32[8,128]{1,0:T(8,128)S(1)}, s32[8,128]{1,0:T(8,128)}, u32[]{:S(2)}) copy-start(s32[8,128]{1,0:T(8,128)} %get-tuple-element.31.places) | copy-start | bytes 12292
  43.9 4.6 %copy-start.3 = (bf16[24,64,4096]{2,1,0:T(8,128)(2,1)S(1)}, bf16[24,64,4096]{2,1,0:T(8,128)(2,1)}, u32[]{:S(2)}) copy-start(bf16[24,64,4096]{2,1,0:T(8,128)(2,1)} %refs_4_.1) | copy-start | bytes 37748740
  48.5 11.6 %copy-start.4 = (s32[24]{0:T(128)S(1)}, s32[24]{0:T(128)}, u32[]{:S(2)}) copy-start(s32[24]{0:T(128)} %weights.1) | copy-start | bytes 292
  80.8 2.8 %collective-permute-start.2 = (bf16[12,8,128]{2,1,0:T(8,128)(2,1)S(1)}, bf16[12,8,128]{2,1,0:T(8,128)(2,1)S(1)}, u32[]{:S(2)}, u32[]{:S(2)}) collective-permute-start(bf16[12,8,128]{2,1,0:T(8,128)(2,1)S(1)} %get-tuple-element.43), channel_id=1, source_target_pairs={{0,1},{1,0},{2,3},{3,2},{4,5},{5,4},{6,7},{7,6},{8,9},{9,8},{10,11... | collective-permute-start | bytes 73736 | tf_op jit(solution)/shard_map/ppermute | solution.py:81
  81.4 3.8 %collective-permute-start.3 = (bf16[12,8,128]{2,1,0:T(8,128)(2,1)S(1)}, bf16[12,8,128]{2,1,0:T(8,128)(2,1)S(1)}, u32[]{:S(2)}, u32[]{:S(2)}) collective-permute-start(bf16[12,8,128]{2,1,0:T(8,128)(2,1)S(1)} %get-tuple-element.44), channel_id=1, source_target_pairs={{0,2},{1,3},{2,0},{3,1},{4,6},{5,7},{6,4},{7,5},{8,10},{9,11},{10,... | collective-permute-start | bytes 73736 | tf_op jit(solution)/shard_map/ppermute | solution.py:81
  82.2 3.5 %collective-permute-start.4 = (bf16[12,8,128]{2,1,0:T(8,128)(2,1)S(1)}, bf16[12,8,128]{2,1,0:T(8,128)(2,1)S(1)}, u32[]{:S(2)}, u32[]{:S(2)}) collective-permute-start(bf16[12,8,128]{2,1,0:T(8,128)(2,1)S(1)} %get-tuple-element.45), channel_id=1, source_target_pairs={{0,3},{1,2},{2,1},{3,0},{4,7},{5,6},{6,5},{7,4},{8,11},{9,10},{10,... | collective-permute-start | bytes 73736 | tf_op jit(solution)/shard_map/ppermute | solution.py:81
  97.6 1.9 %collective-permute-start.5 = (bf16[12,8,128]{2,1,0:T(8,128)(2,1)S(1)}, bf16[12,8,128]{2,1,0:T(8,128)(2,1)S(1)}, u32[]{:S(2)}, u32[]{:S(2)}) collective-permute-start(bf16[12,8,128]{2,1,0:T(8,128)(2,1)S(1)} %get-tuple-element.50), channel_id=1, source_target_pairs={{0,1},{1,0},{2,3},{3,2},{4,5},{5,4},{6,7},{7,6},{8,9},{9,8},{10,11... | collective-permute-start | bytes 73736 | tf_op jit(solution)/shard_map/ppermute | solution.py:81
  97.9 3.9 %collective-permute-start.6 = (bf16[12,8,128]{2,1,0:T(8,128)(2,1)S(1)}, bf16[12,8,128]{2,1,0:T(8,128)(2,1)S(1)}, u32[]{:S(2)}, u32[]{:S(2)}) collective-permute-start(bf16[12,8,128]{2,1,0:T(8,128)(2,1)S(1)} %get-tuple-element.51), channel_id=1, source_target_pairs={{0,2},{1,3},{2,0},{3,1},{4,6},{5,7},{6,4},{7,5},{8,10},{9,11},{10,... | collective-permute-start | bytes 73736 | tf_op jit(solution)/shard_map/ppermute | solution.py:81
  98.3 3.5 %collective-permute-start.7 = (bf16[12,8,128]{2,1,0:T(8,128)(2,1)S(1)}, bf16[12,8,128]{2,1,0:T(8,128)(2,1)S(1)}, u32[]{:S(2)}, u32[]{:S(2)}) collective-permute-start(bf16[12,8,128]{2,1,0:T(8,128)(2,1)S(1)} %get-tuple-element.52), channel_id=1, source_target_pairs={{0,3},{1,2},{2,1},{3,0},{4,7},{5,6},{6,5},{7,4},{8,11},{9,10},{10,... | collective-permute-start | bytes 73736 | tf_op jit(solution)/shard_map/ppermute | solution.py:81
